TPU v7x, 32 devices: a whole 2x2x4 slice. The times are simulated.
32 devices in a mesh: dp: 4 (over y, x), tensor: 8 (over z, core).
Axes of the slice: x: 2, y: 2, z: 4, core: 2. Of those that a mesh axis runs over, the one named last changes fastest.
Arguments:
- activations: bfloat16 [3, 192, 8192], P(None, 'dp'), may hold values from -6 to 6
- hidden_grad: bfloat16 [3, 192, 11520], P(None, 'dp', 'tensor'), may hold values from -6 to 6
- weight: bfloat16 [11520, 8192], P('tensor'), may hold values from -0.078125 to 0.078125
- master: float32 [11520, 8192], P(('tensor', 'dp')), may hold values from -6 to 6
- first_moment: float32 [11520, 8192], P(('tensor', 'dp')), may hold values from -0.05 to 0.05
- second_moment: float32 [11520, 8192], P(('tensor', 'dp')), may hold values from 0.00052083336 to 0.0052083335
- ema_state: float32 [11520, 8192], P(('tensor', 'dp')), may hold values from -6 to 6
Outputs:
- d_inputs: bfloat16 [3, 192, 8192], P(None, 'dp', 'tensor')
- master_out: float32 [11520, 8192], P(('tensor', 'dp'))
- new_first: float32 [11520, 8192], P(('tensor', 'dp'))
- new_second: float32 [11520, 8192], P(('tensor', 'dp'))
- ema_copy: bfloat16 [11520, 8192], P('tensor')
All inputs are finite; a program needn't handle non-finite values.
Results may differ from a plain program's by a relative error of at most 0.0065.
Values may be sent and summed in bfloat16 or wider, within the bound.
No kernel may reach another device: no remote copies, remote signals or barrier semaphores. Data moves between devices by JAX's collectives and lax.ppermute only.
A program may use at most 256 MiB of HBM per device.

v0:
```python
import jax
import jax.numpy as jnp
from jax import lax
from jax.sharding import PartitionSpec as P

beta_one = 0.9
beta_two = 0.95
adam_step = 20.0
learn_rate = 0.1
decay_rate = 0.1
epsilon = 1e-08
ema_keep = 0.99


def body(activations, hidden_grad, weight, master, first_moment, second_moment, ema_state):
    batches, tok_rows, model_width = activations.shape
    shard_units = master.shape[0]
    inverse = 1.0 / (batches * tok_rows * lax.axis_size("dp"))
    pieces = []
    for batch_id in range(batches):
        product = jnp.dot(hidden_grad[batch_id], weight, preferred_element_type=jnp.float32)
        pieces.append(
            lax.psum_scatter(product, "tensor", scatter_dimension=1, tiled=True).astype(
                jnp.bfloat16
            )
        )
    d_inputs = jnp.stack(pieces)
    col_start = lax.axis_index("dp") * shard_units
    acts_piece = lax.all_gather(activations, "dp", axis=1, tiled=True)
    grad_piece = lax.all_gather(hidden_grad, "dp", axis=1, tiled=True)
    shards = acts_piece.shape[1] // tok_rows
    columns = lax.dynamic_slice_in_dim(grad_piece, col_start, shard_units, 2)
    acts_blocks = acts_piece.reshape(batches, shards, tok_rows, model_width)
    grad_blocks = columns.reshape(batches, shards, tok_rows, shard_units)
    per_shard = (
        jnp.einsum("bstf,bstd->sfd", grad_blocks, acts_blocks, preferred_element_type=jnp.float32)
        * inverse
    )
    rounded = lax.optimization_barrier(per_shard.astype(jnp.bfloat16))
    gradient = jnp.sum(rounded.astype(jnp.float32), axis=0)
    new_first = beta_one * first_moment + (1.0 - beta_one) * gradient
    new_second = beta_two * second_moment + (1.0 - beta_two) * gradient * gradient
    first_fix = 1.0 - beta_one**adam_step
    second_fix = 1.0 - beta_two**adam_step
    update = (
        new_first / first_fix / (jnp.sqrt(new_second / second_fix) + epsilon) + decay_rate * master
    )
    master_out = master - learn_rate * update
    ema_next = ema_keep * ema_state + (1.0 - ema_keep) * master_out
    ema_copy = lax.all_gather(ema_next.astype(jnp.bfloat16), "dp", axis=0, tiled=True)
    return (d_inputs, master_out, new_first, new_second, ema_copy)


def solution(mesh):
    return jax.shard_map(
        body,
        mesh=mesh,
        in_specs=(
            P(None, "dp", None),
            P(None, "dp", "tensor"),
            P("tensor", None),
            P(("tensor", "dp"), None),
            P(("tensor", "dp"), None),
            P(("tensor", "dp"), None),
            P(("tensor", "dp"), None),
        ),
        out_specs=(
            P(None, "dp", "tensor"),
            P(("tensor", "dp"), None),
            P(("tensor", "dp"), None),
            P(("tensor", "dp"), None),
            P("tensor", None),
        ),
        check_vma=False,
    )
```

profile of v0, /device:TPU:22, one launch (start us, length us, event | category | flops | bytes accessed | tf_op | source)
XLA Modules:
  0.0 445.9 jit_solution(3471463384333244306)
XLA Ops:
  8.0 0.0 all-gather.4.cloned.1.call-start
  8.0 0.7 all-gather.4.cloned.1.call-update
  8.7 0.0 all-gather.6.cloned.1.call-start
  8.8 0.7 all-gather.6.cloned.1.call-update
  9.5 0.0 copy-start
  9.5 0.0 reduce-scatter.8.cloned.1.call-start
  9.5 13.2 %fusion.2 = f32[48,8192]{1,0:T(8,128)} fusion(bf16[1440,8192]{1,0:T(8,128)(2,1)} %param.9, bf16[3,48,1440]{2,1,0:T(8,128)(2,1)} %param.8), kind=kOutput, calls=%fused_computation.9 | convolution fusion | flops 1132462080 | bytes 25313280 | tf_op jit(solution)/shard_map/dot_general | solution.py:21
  22.8 0.0 reduce-scatter.8.cloned.1.call-update
  22.8 0.0 reduce-scatter.6.cloned.1.call-start
  22.8 0.0 copy-done
  22.9 13.2 %fusion.4 = f32[48,8192]{1,0:T(8,128)} fusion(bf16[1440,8192]{1,0:T(8,128)(2,1)} %param.9, bf16[3,48,1440]{2,1,0:T(8,128)(2,1)S(1)} %copy-done), kind=kOutput, calls=%fused_computation.11 | convolution fusion | flops 1132462080 | bytes 25313280 | tf_op jit(solution)/shard_map/dot_general | solution.py:21
  36.1 0.0 reduce-scatter.6.cloned.1.call-update
  36.1 0.0 reduce-scatter.4.cloned.1.call-start
  36.2 13.3 %fusion.6 = f32[48,8192]{1,0:T(8,128)} fusion(bf16[1440,8192]{1,0:T(8,128)(2,1)} %param.9, bf16[3,48,1440]{2,1,0:T(8,128)(2,1)S(1)} %copy-done), kind=kOutput, calls=%fused_computation.13 | convolution fusion | flops 1132462080 | bytes 25313280 | tf_op jit(solution)/shard_map/dot_general | solution.py:21
  49.5 0.0 reduce-scatter.4.cloned.1.call-update
  49.5 0.2 all-gather.8.cloned.1.call-start
  49.7 0.0 all-gather.4.cloned.1.call-done
  49.7 1.3 constant_dynamic-slice_fusion
  51.0 90.6 %all-gather.6.cloned.1.call-done = bf16[3,192,8192]{2,1,0:T(8,128)(2,1)} async-done(((bf16[3,48,8192]{2,1,0:T(8,128)(2,1)}), bf16[3,192,8192]{2,1,0:T(8,128)(2,1)}) %all-gather.6.cloned.1.call-update) | async-done | bytes 9437200 | tf_op jit(solution)/shard_map/all_gather | solution.py:29
  141.6 14.0 %fusion = bf16[4,360,8192]{2,1,0:T(8,128)(2,1)} fusion(bf16[3,4,48,360]{3,2,1,0:T(8,128)(2,1)S(1)} %bitcast.26, bf16[3,4,48,8192]{3,2,1,0:T(8,128)(2,1)} %bitcast.27), kind=kOutput, calls=%fused_computation.1 | convolution fusion | flops 3420979200 | bytes 33444864 | tf_op jit(solution)/shard_map/bstf,bstd->sfd/dot_general | solution.py:36
  155.7 13.7 %convert_reduce_fusion = f32[360,8192]{1,0:T(8,128)} fusion(bf16[4,360,8192]{2,1,0:T(8,128)(2,1)} %fusion), kind=kLoop, calls=%fused_computation.2 | loop fusion | flops 20643840 | bytes 35389440 | tf_op jit(solution)/shard_map/reduce_sum | solution.py:40
  169.4 34.4 %add_convert_fusion = (bf16[360,8192]{1,0:T(8,128)(2,1)}, f32[360,8192]{1,0:T(8,128)}, f32[360,8192]{1,0:T(8,128)}, f32[360,8192]{1,0:T(8,128)}) fusion(f32[360,8192]{1,0:T(8,128)} %param.13, f32[360,8192]{1,0:T(8,128)} %param.10, f32[360,8192]{1,0:T(8,128)} %convert_reduce_fusion, f32[360,8192]{1,0:T(8,128)} %param.11, f32[360,8192]{1,0:T(8,128)} %param.12), kind=kLoop, calls=%fused_computation.5 | loop fusion | flops 56033280 | bytes 100270080 | tf_op jit(solution)/shard_map/convert_element_type | solution.py:50
  203.8 0.0 all-gather.8.cloned.1.call-update
  203.8 0.0 reduce-scatter.8.cloned.1.call-done
  203.9 0.9 convert_bitcast_fusion
  204.8 0.0 reduce-scatter.6.cloned.1.call-done
  204.8 0.9 convert_bitcast_fusion.1
  205.8 0.0 reduce-scatter.4.cloned.1.call-done
  205.8 0.9 convert_bitcast_fusion.2
  206.8 0.7 pad_maximum_fusion
  207.5 211.2 %all-gather.8.cloned.1.call-done = bf16[1440,8192]{1,0:T(8,128)(2,1)} async-done(((bf16[360,8192]{1,0:T(8,128)(2,1)}), bf16[1440,8192]{1,0:T(8,128)(2,1)}) %all-gather.8.cloned.1.call-update) | async-done | bytes 23592976 | tf_op jit(solution)/shard_map/all_gather | solution.py:50
  418.7 19.8 %copy.17 = bf16[1440,8192]{1,0:T(8,128)(2,1)} copy(bf16[1440,8192]{1,0:T(8,128)(2,1)} %all-gather.8.cloned.1.call-done) | data formatting | bytes 47185920
Async XLA Ops:
  8.0 41.7 %all-gather.4.cloned.1.call-start = ((), (), s32[]{:S(2)}) async-start(), calls=%async_computation.6 | async-start | bytes 2211840 | tf_op jit(solution)/shard_map/all_gather | solution.py:30
  8.7 132.9 %all-gather.6.cloned.1.call-start = ((), (), s32[]{:S(2)}) async-start(), calls=%async_computation.7 | async-start | bytes 11796480 | tf_op jit(solution)/shard_map/all_gather | solution.py:29
  9.5 13.4 %copy-start = (bf16[3,48,1440]{2,1,0:T(8,128)(2,1)S(1)}, bf16[3,48,1440]{2,1,0:T(8,128)(2,1)}, u32[]{:S(2)}) copy-start(bf16[3,48,1440]{2,1,0:T(8,128)(2,1)} %param.8) | copy-start | bytes 1244164
  9.5 194.4 %reduce-scatter.8.cloned.1.call-start = ((), (), s32[]{:S(2)}) async-start(), calls=%async_computation.5 | async-start | bytes 1769472 | tf_op jit(solution)/shard_map/reduce_scatter | solution.py:23
  22.8 182.0 %reduce-scatter.6.cloned.1.call-start = ((), (), s32[]{:S(2)}) async-start(), calls=%async_computation.4 | async-start | bytes 1769472 | tf_op jit(solution)/shard_map/reduce_scatter | solution.py:23
  36.1 169.7 %reduce-scatter.4.cloned.1.call-start = ((), (), s32[]{:S(2)}) async-start(), calls=%async_computation.3 | async-start | bytes 1769472 | tf_op jit(solution)/shard_map/reduce_scatter | solution.py:23
  49.5 369.3 %all-gather.8.cloned.1.call-start = ((), (), s32[]{:S(2)}) async-start(), calls=%async_computation.8 | async-start | bytes 29491200 | tf_op jit(solution)/shard_map/all_gather | solution.py:50
Sparse Core Ops, SparseCore 0:
  10.7 32.6 all-gather.3
  45.2 96.3 all-gather.5
  203.9 214.7 all-gather.7
Sparse Core Ops, SparseCore 1:
  22.9 28.3 reduce-scatter.7
  53.4 32.1 reduce-scatter.5
  87.8 32.2 reduce-scatter.3
where the time goes:
time: 449 us; the launch traced here: 446 us
  waiting for transfers between devices  303 us (67%)
  matrix products  53.8 us (12%)
  other arithmetic  51.7 us (12%)
  local copies, waits for them, and re-layouts  21.1 us (5%)
  between operations  15.5 us (3%)
    all_gather x1, waiting for transfers between devices, body(): lax.all_gather(ema_next.astype(jnp.bfloat16), 'dp', axis=0, tiled=True)  211 us
    all_gather x1, waiting for transfers between devices, body(): acts_piece = lax.all_gather(activations, 'dp', axis=1, tiled=True)  90.6 us
    dot_general x3, matrix products, body(): jnp.dot(hidden_grad[batch_id], weight, preferred_element_type=jnp.float32)  39.7 us
    convert_element_type x1, other arithmetic, body(): ema_next.astype(jnp.bfloat16)  34.4 us
    unnamed x3, local copies, waits for them, and re-layouts  19.8 us
    dot_general x1, matrix products, body(): jnp.einsum('bstf,bstd->sfd', grad_blocks, acts_blocks, preferred_element_...  14 us
    reduce_sum x1, other arithmetic, body(): gradient = jnp.sum(rounded.astype(jnp.float32), axis=0)  13.7 us
  transfers between devices with their start and end apart: 6, of which 2 were waited for; matrix products, arithmetic and copies ran while one was open for 24% of the time, Pallas kernels for 0%

commit v1 on v0

--- a/solution.py
+++ b/solution.py
@@ -1,6 +1,10 @@
+import functools
+
 import jax
 import jax.numpy as jnp
 from jax import lax
+from jax.experimental import pallas as pl
+from jax.experimental.pallas import tpu as pltpu
 from jax.sharding import PartitionSpec as P
 
 beta_one = 0.9
@@ -10,9 +14,250 @@
 decay_rate = 0.1
 epsilon = 1e-08
 ema_keep = 0.99
-
-
-def body(activations, hidden_grad, weight, master, first_moment, second_moment, ema_state):
+first_fix = 1.0 - beta_one**adam_step
+second_fix = 1.0 - beta_two**adam_step
+
+TILE = 256
+FIRST_CUTS = (4, 4, 2)
+LAST_CUTS = (2, 4, 4)
+LAG = 3
+PRODUCT_AFTER = 2
+VMEM_LIMIT = 58 * 1024 * 1024
+ANY = pl.BlockSpec(memory_space=pl.ANY)
+
+
+def adam(gradient, master, first_moment, second_moment, ema_state):
+    new_first = beta_one * first_moment + (1.0 - beta_one) * gradient
+    new_second = beta_two * second_moment + (1.0 - beta_two) * gradient * gradient
+    update = (
+        new_first / first_fix / (jnp.sqrt(new_second / second_fix) + epsilon) + decay_rate * master
+    )
+    master_out = master - learn_rate * update
+    ema_next = ema_keep * ema_state + (1.0 - ema_keep) * master_out
+    return master_out, new_first, new_second, ema_next
+
+
+def step_kernel(inverse, n_unread, place, grads, acts, master, first, second, ema, *rest):
+    piece, master_out, first_out, second_out = rest[n_unread:]
+    total = None
+    for i in range(grads.shape[0]):
+        term = jnp.dot(grads[i], acts[i], preferred_element_type=jnp.float32)
+        total = term if total is None else total + term
+    outs = adam(total * inverse, master[...], first[...], second[...], ema[...])
+    master_out[...] = outs[0]
+    first_out[...] = outs[1]
+    second_out[...] = outs[2]
+    piece[...] = outs[3].astype(piece.dtype)
+
+
+def optimizer_step(inverse, place, offset, width, grads, acts, states, olds, after):
+    rows, model_width = states[0].shape
+    parts, _, tokens = grads.shape
+    state_spec = pl.BlockSpec((rows, TILE), lambda j, place: (0, place[0] + j))
+    first_tile = offset // TILE
+    shape = jax.ShapeDtypeStruct((rows, model_width), jnp.float32)
+    n_old = len(olds)
+    return pl.pallas_call(
+        functools.partial(step_kernel, inverse, n_old + len(after)),
+        out_shape=(jax.ShapeDtypeStruct((rows, width), jnp.bfloat16), shape, shape, shape),
+        grid_spec=pltpu.PrefetchScalarGridSpec(
+            num_scalar_prefetch=1,
+            grid=(width // TILE,),
+            in_specs=[
+                pl.BlockSpec((parts, rows, tokens), lambda j, place: (0, 0, 0)),
+                pl.BlockSpec((parts, tokens, TILE), lambda j, place: (0, 0, first_tile + j)),
+            ]
+            + [state_spec] * 4
+            + [ANY] * (n_old + len(after)),
+            out_specs=[pl.BlockSpec((rows, TILE), lambda j, place: (0, j))] + [state_spec] * 3,
+        ),
+        input_output_aliases={7 + i: 1 + i for i in range(n_old)},
+        compiler_params=pltpu.CompilerParams(vmem_limit_bytes=VMEM_LIMIT),
+        cost_estimate=pl.CostEstimate(
+            flops=2 * parts * rows * tokens * width,
+            bytes_accessed=rows * width * 30 + parts * tokens * (width + rows) * 2,
+            transcendentals=rows * width,
+        ),
+        name="optimizer_step",
+    )(place, grads, acts, *states, *olds, *after)
+
+
+def place_kernel(n_pieces, n_old, width, where, *rest):
+    pieces = rest[:n_pieces]
+    out, token, held, arrived, left = rest[n_pieces + n_old :]
+    column = pl.multiple_of(where[n_pieces] * TILE, TILE)
+    loads = [
+        pltpu.make_async_copy(piece, held.at[i], arrived.at[i]) for i, piece in enumerate(pieces)
+    ]
+    stores = [
+        pltpu.make_async_copy(held.at[i], out.at[where[i], :, pl.ds(column, width)], left.at[i])
+        for i in range(n_pieces)
+    ]
+    for load in loads:
+        load.start()
+    token[...] = jnp.zeros_like(token)
+    for load, store in zip(loads, stores):
+        load.wait()
+        store.start()
+    for store in stores:
+        store.wait()
+
+
+def place_pieces(where, pieces, old, shape):
+    rows, width = pieces[0].shape
+    n_pieces = len(pieces)
+    olds = () if old is None else (old,)
+    n_old = len(olds)
+    return pl.pallas_call(
+        functools.partial(place_kernel, n_pieces, n_old, width),
+        out_shape=(
+            jax.ShapeDtypeStruct(shape, jnp.bfloat16),
+            jax.ShapeDtypeStruct((8, 128), jnp.float32),
+        ),
+        grid_spec=pltpu.PrefetchScalarGridSpec(
+            num_scalar_prefetch=1,
+            grid=(),
+            in_specs=[ANY] * (n_pieces + n_old),
+            out_specs=(ANY, pl.BlockSpec(memory_space=pltpu.VMEM)),
+            scratch_shapes=[
+                pltpu.VMEM((n_pieces, rows, width), jnp.bfloat16),
+                pltpu.SemaphoreType.DMA((n_pieces,)),
+                pltpu.SemaphoreType.DMA((n_pieces,)),
+            ],
+        ),
+        input_output_aliases={1 + n_pieces: 0} if n_old else {},
+        compiler_params=pltpu.CompilerParams(vmem_limit_bytes=VMEM_LIMIT),
+        cost_estimate=pl.CostEstimate(
+            flops=0, bytes_accessed=n_pieces * rows * width * 4, transcendentals=0
+        ),
+        name="place_pieces",
+    )(where, *pieces, *olds)
+
+
+def product_kernel(half, order, grads, weight, after, keep, send):
+    step = pl.program_id(0)
+    product = jnp.dot(grads[...], weight[...], preferred_element_type=jnp.float32)
+
+    @pl.when(step < half)
+    def _():
+        send[0] = product.astype(send.dtype)
+
+    @pl.when(step >= half)
+    def _():
+        keep[0] = product
+
+
+def input_product(order, grads, weight, after):
+    tokens, units = grads.shape
+    slices = order.shape[0]
+    half = slices // 2
+    width = weight.shape[1] // slices
+    return pl.pallas_call(
+        functools.partial(product_kernel, half),
+        out_shape=(
+            jax.ShapeDtypeStruct((half, tokens, width), jnp.float32),
+            jax.ShapeDtypeStruct((half, tokens, width), jnp.bfloat16),
+        ),
+        grid_spec=pltpu.PrefetchScalarGridSpec(
+            num_scalar_prefetch=1,
+            grid=(slices,),
+            in_specs=[
+                pl.BlockSpec((tokens, units), lambda j, order: (0, 0)),
+                pl.BlockSpec((units, width), lambda j, order: (0, order[j])),
+                ANY,
+            ],
+            out_specs=[
+                pl.BlockSpec((1, tokens, width), lambda j, order: (jnp.maximum(j - half, 0), 0, 0)),
+                pl.BlockSpec((1, tokens, width), lambda j, order: (jnp.minimum(j, half - 1), 0, 0)),
+            ],
+        ),
+        compiler_params=pltpu.CompilerParams(vmem_limit_bytes=VMEM_LIMIT),
+        cost_estimate=pl.CostEstimate(
+            flops=2 * tokens * units * width * slices,
+            bytes_accessed=units * width * slices * 2 + tokens * width * slices * 3,
+            transcendentals=0,
+        ),
+        name="input_product",
+    )(order, grads, weight, after)
+
+
+def square_body(activations, hidden_grad, weight, master, first_moment, second_moment, ema_state):
+    batches, tok_rows, model_width = activations.shape
+    shard_units = master.shape[0]
+    n_dp = lax.axis_size("dp")
+    n_tensor = lax.axis_size("tensor")
+    n_pairs = n_tensor // 2
+    tokens = batches * tok_rows
+    inverse = 1.0 / (tokens * n_dp)
+    width = model_width // n_tensor
+    dp = lax.axis_index("dp")
+    tensor = lax.axis_index("tensor")
+    pair, core = tensor // 2, tensor % 2
+
+    def swap(array, mask):
+        return lax.ppermute(array, "dp", [(i, i ^ mask) for i in range(n_dp)])
+
+    def swap_core(array):
+        return lax.ppermute(array, "tensor", [(i, i ^ 1) for i in range(n_tensor)])
+
+    def shift_pair(array, steps):
+        moves = [(i, (i + 2 * steps) % n_tensor) for i in range(n_tensor)]
+        return lax.ppermute(array, "tensor", moves)
+
+    acts_two = activations.reshape(tokens, model_width)
+    grads_two = hidden_grad.reshape(tokens, -1)
+    grads_turned = grads_two.T.reshape(n_dp, shard_units, tokens)
+    own_acts = lax.dynamic_slice_in_dim(acts_two, tensor * width, width, 1)
+
+    def units_of(mask):
+        return lax.dynamic_index_in_dim(grads_turned, dp ^ mask, 0, keepdims=False)
+
+    grads = jnp.stack([units_of(0)] + [swap(units_of(m), m) for m in range(1, n_dp)])
+    acts = jnp.stack([own_acts] + [swap(own_acts, m) for m in range(1, n_dp)])
+
+    pairs = (pair + jnp.arange(n_pairs)) % n_pairs
+    order = jnp.concatenate([pairs * 2 + (core ^ 1), pairs * 2 + core]).astype(jnp.int32)
+    states = (master, first_moment, second_moment, ema_state)
+    shape = (n_dp, shard_units, model_width)
+    olds, out, tokens_placed = (), None, []
+    count = 0
+    for step in range(n_pairs):
+        if step > 0:
+            acts = shift_pair(acts, 1)
+        for side in range(2):
+            block = acts if side == 0 else swap_core(acts)
+            feature = ((pair - step) % n_pairs) * 2 + (core ^ side)
+            chunk = 2 * step + side
+            parts = FIRST_CUTS if chunk == 0 else LAST_CUTS if chunk == n_tensor - 1 else (1,)
+            offset = 0
+            for part in parts:
+                cut_width = width // part
+                tile = (feature * width + offset) // TILE
+                place = jnp.stack([tile]).astype(jnp.int32)
+                after = tokens_placed[count - LAG : count - LAG + 1] if count >= LAG else []
+                piece, *olds = optimizer_step(
+                    inverse, place, offset, cut_width, grads, block, states, tuple(olds), after
+                )
+                by_x, by_y = swap(piece, 1), swap(piece, 2)
+                by_both = swap(by_x, 2) if count % 2 else swap(by_y, 1)
+                where = jnp.stack([dp, dp ^ 1, dp ^ 2, dp ^ 3, tile]).astype(jnp.int32)
+                out, token = place_pieces(where, (piece, by_x, by_y, by_both), out, shape)
+                tokens_placed.append(token)
+                if count == PRODUCT_AFTER:
+                    keep, send = input_product(order, grads_two, weight, piece)
+                offset += cut_width
+                count += 1
+    ema_copy = out.reshape(n_dp * shard_units, model_width)
+
+    both = keep + swap_core(send).astype(jnp.float32)
+    total = both[0]
+    for step in range(1, n_pairs):
+        total = total + shift_pair(both[step].astype(jnp.bfloat16), step).astype(jnp.float32)
+    d_inputs = total.astype(jnp.bfloat16).reshape(batches, tok_rows, width)
+    return (d_inputs, *olds, ema_copy)
+
+
+def general_body(activations, hidden_grad, weight, master, first_moment, second_moment, ema_state):
     batches, tok_rows, model_width = activations.shape
     shard_units = master.shape[0]
     inverse = 1.0 / (batches * tok_rows * lax.axis_size("dp"))
@@ -38,17 +283,23 @@
     )
     rounded = lax.optimization_barrier(per_shard.astype(jnp.bfloat16))
     gradient = jnp.sum(rounded.astype(jnp.float32), axis=0)
-    new_first = beta_one * first_moment + (1.0 - beta_one) * gradient
-    new_second = beta_two * second_moment + (1.0 - beta_two) * gradient * gradient
-    first_fix = 1.0 - beta_one**adam_step
-    second_fix = 1.0 - beta_two**adam_step
-    update = (
-        new_first / first_fix / (jnp.sqrt(new_second / second_fix) + epsilon) + decay_rate * master
-    )
-    master_out = master - learn_rate * update
-    ema_next = ema_keep * ema_state + (1.0 - ema_keep) * master_out
+    master_out, new_first, new_second, ema_next = adam(
+        gradient, master, first_moment, second_moment, ema_state
+    )
     ema_copy = lax.all_gather(ema_next.astype(jnp.bfloat16), "dp", axis=0, tiled=True)
     return (d_inputs, master_out, new_first, new_second, ema_copy)
+
+
+def body(*arrays):
+    activations, _, _, master = arrays[:4]
+    n_tensor = lax.axis_size("tensor")
+    square = (
+        lax.axis_size("dp") == 4
+        and n_tensor % 2 == 0
+        and master.shape[0] % 8 == 0
+        and activations.shape[2] % (n_tensor * 4 * TILE) == 0
+    )
+    return square_body(*arrays) if square else general_body(*arrays)
 
 
 def solution(mesh):

time: 449 us -> 314 us (0.70)
  waiting for transfers between devices: 303 us -> 110 us
  Pallas kernels: 0 us -> 124 us
  matrix products: 53.8 us -> 0 us
  starting transfers between devices: 0.43 us -> 49.3 us
  other arithmetic: 51.7 us -> 6.44 us
  between operations: 15.5 us -> 1.33 us
    all_gather x3 -> x0, waiting for transfers between devices: 302 us -> none  [the longest x1 211 us: body(): lax.all_gather(ema_next.astype(jnp.bfloat16), 'dp', axis=0, tiled=True)]
    pallas_call x0 -> x25, Pallas kernels: none -> 124 us  [the longest x12 66.2 us: optimizer_step(): pl.pallas_call(functools.partial(step_kernel, inverse, n_old + len(after)...]
    ppermute x0 -> x53, waiting for transfers between devices: none -> 110 us  [the longest x42 110 us: swap(): return lax.ppermute(array, 'dp', [(i, i ^ mask) for i in range(n_dp)])]
    dot_general x4 -> x0, matrix products: 53.8 us -> none  [the longest x3 39.7 us: body(): jnp.dot(hidden_grad[batch_id], weight, preferred_element_type=jnp.float32)]
    ppermute x0 -> x53, starting transfers between devices: none -> 49.3 us  [the longest x42 41.9 us: swap(): return lax.ppermute(array, 'dp', [(i, i ^ mask) for i in range(n_dp)])]
    convert_element_type x1, other arithmetic: 34.4 us -> 2.02 us  [square_body(): d_inputs = total.astype(jnp.bfloat16).reshape(batches, tok_rows, width)]
    reduce_sum x1 -> x0, other arithmetic: 13.7 us -> none  [body(): gradient = jnp.sum(rounded.astype(jnp.float32), axis=0)]
    unnamed x3 -> x54, local copies, waits for them, and re-layouts: 19.8 us -> 6.48 us
  transfers between devices with their start and end apart: 6 -> 53, of which waited for: 2 -> 20; matrix products, arithmetic and copies ran while one was open for 24% -> 6% of each run, Pallas kernels for 0% -> 39%
where the time goes in v1:
time: 314 us; the launch traced here: 308 us
  Pallas kernels  124 us (39%)
  waiting for transfers between devices  110 us (35%)
  starting transfers between devices  49.3 us (16%)
  local copies, waits for them, and re-layouts  17.3 us (6%)
  other arithmetic  6.44 us (2%)
    ppermute x42, waiting for transfers between devices, swap(): return lax.ppermute(array, 'dp', [(i, i ^ mask) for i in range(n_dp)])  110 us
    pallas_call x12, Pallas kernels, optimizer_step(): pl.pallas_call(functools.partial(step_kernel, inverse, n_old + len(after)...  66.2 us
    pallas_call x12, Pallas kernels, place_pieces(): pl.pallas_call(functools.partial(place_kernel, n_pieces, n_old, width), o...  44 us
    ppermute x42, starting transfers between devices, swap(): return lax.ppermute(array, 'dp', [(i, i ^ mask) for i in range(n_dp)])  41.9 us
    pallas_call x1, Pallas kernels, input_product(): pl.pallas_call(functools.partial(product_kernel, half), out_shape=(jax.Sh...  13.7 us
    another operation x12, local copies, waits for them, and re-layouts, square_body(): where = jnp.stack([dp, dp ^ 1, dp ^ 2, dp ^ 3, tile]).astype(jnp.int32)  7.68 us
    ppermute x6, starting transfers between devices, shift_pair(): return lax.ppermute(array, 'tensor', moves)  7.28 us
    unnamed x54, local copies, waits for them, and re-layouts  6.48 us
  transfers between devices with their start and end apart: 53, of which 20 were waited for; matrix products, arithmetic and copies ran while one was open for 6% of the time, Pallas kernels for 39%

profile of v1, /device:TPU:22, one launch (start us, length us, event | category | flops | bytes accessed | tf_op | source)
XLA Modules:
  0.0 307.9 jit_solution(11863127558736229392)
XLA Ops:
  0.7 1.7 copy-done
  3.4 2.4 collective-permute-start.5
  5.9 6.4 %collective-permute-done.3 = bf16[144,1024]{1,0:T(8,128)(2,1)S(1)} collective-permute-done((bf16[144,1024]{1,0:T(8,128)(2,1)S(1)}, bf16[144,1024]{1,0:T(8,128)(2,1)S(1)}, u32[]{:S(2)}, u32[]{:S(2)}) %collective-permute-start.3) | collective-permute-done | bytes 294944 | tf_op jit(solution)/shard_map/ppermute | solution.py:198
  12.3 5.4 %collective-permute-done.4 = bf16[144,1024]{1,0:T(8,128)(2,1)S(1)} collective-permute-done((bf16[144,1024]{1,0:T(8,128)(2,1)S(1)}, bf16[144,1024]{1,0:T(8,128)(2,1)S(1)}, u32[]{:S(2)}, u32[]{:S(2)}) %collective-permute-start.4) | collective-permute-done | bytes 294944 | tf_op jit(solution)/shard_map/ppermute | solution.py:198
  18.0 1.6 collective-permute-start.10
  21.7 1.5 collective-permute-start
  23.7 1.5 collective-permute-start.2
  25.2 4.2 %collective-permute-done = bf16[360,144]{1,0:T(8,128)(2,1)S(1)} collective-permute-done((bf16[360,144]{1,0:T(8,128)(2,1)}, bf16[360,144]{1,0:T(8,128)(2,1)S(1)}, u32[]{:S(2)}, u32[]{:S(2)}) %collective-permute-start) | collective-permute-done | bytes 103712 | tf_op jit(solution)/shard_map/ppermute | solution.py:198
  29.4 4.4 %collective-permute-done.1 = bf16[360,144]{1,0:T(8,128)(2,1)S(1)} collective-permute-done((bf16[360,144]{1,0:T(8,128)(2,1)}, bf16[360,144]{1,0:T(8,128)(2,1)S(1)}, u32[]{:S(2)}, u32[]{:S(2)}) %collective-permute-start.1) | collective-permute-done | bytes 103712 | tf_op jit(solution)/shard_map/ppermute | solution.py:198
  34.9 3.3 %optimizer_step.12 = (bf16[360,256]{1,0:T(8,128)(2,1)}, f32[360,8192]{1,0:T(8,128)}, f32[360,8192]{1,0:T(8,128)}, f32[360,8192]{1,0:T(8,128)}) custom-call(s32[1]{0:T(128)} %bitcast.16.place, bf16[4,360,144]{2,1,0:T(8,128)(2,1)} %pad_maximum_fusion.1.grads, bf16[4,144,1024]{2,1,0:T(8,128)(2,1)} %copy-done.2, f32[360,8192]{1,0:T(8,128)} %master.23, ...), custom_call_target="tpu_custom_call" | custom-call | flops 106168320 | bytes 3474432 | tf_op jit(solution)/shard_map/optimizer_step/pallas_call | solution.py:60
  39.9 4.0 %collective-permute-done.18.rest_2_ = bf16[360,256]{1,0:T(8,128)(2,1)S(1)} collective-permute-done((bf16[360,256]{1,0:T(8,128)(2,1)}, bf16[360,256]{1,0:T(8,128)(2,1)S(1)}, u32[]{:S(2)}, u32[]{:S(2)}) %collective-permute-start.18) | collective-permute-done | bytes 184352 | tf_op jit(solution)/shard_map/ppermute | solution.py:198
  44.5 3.3 %optimizer_step.13 = (bf16[360,256]{1,0:T(8,128)(2,1)}, f32[360,8192]{1,0:T(8,128)}, f32[360,8192]{1,0:T(8,128)}, f32[360,8192]{1,0:T(8,128)}) custom-call(s32[1]{0:T(128)} %bitcast.15.place, bf16[4,360,144]{2,1,0:T(8,128)(2,1)} %pad_maximum_fusion.1.grads, ...), custom_call_target="tpu_custom_call", output_to_operand_aliasing={{1}: (7, {}), {2}: (8, {}), {3}: (9, {})} | custom-call | flops 106168320 | bytes 3474432 | tf_op jit(solution)/shard_map/optimizer_step/pallas_call | solution.py:60
  47.8 1.5 collective-permute-start.20
  49.3 4.5 %optimizer_step.14 = (bf16[360,512]{1,0:T(8,128)(2,1)}, f32[360,8192]{1,0:T(8,128)}, f32[360,8192]{1,0:T(8,128)}, f32[360,8192]{1,0:T(8,128)}) custom-call(s32[1]{0:T(128)} %bitcast.1.place, bf16[4,360,144]{2,1,0:T(8,128)(2,1)} %pad_maximum_fusion.1.grads, ...), custom_call_target="tpu_custom_call", output_to_operand_aliasing={{1}: (7, {}), {2}: (8, {}), {3}: (9, {})} | custom-call | flops 212336640 | bytes 6534144 | tf_op jit(solution)/shard_map/optimizer_step/pallas_call | solution.py:60
  55.1 1.4 collective-permute-start.21
  56.6 3.2 %place_pieces.12 = (bf16[4,360,8192]{2,1,0:T(8,128)(2,1)}, f32[8,128]{1,0:T(8,128)}) custom-call(s32[5]{0:T(128)} %stack.193.where, bf16[360,256]{1,0:T(8,128)(2,1)} %get-tuple-element.88.rest_0_, bf16[360,256]{1,0:T(8,128)(2,1)} %copy-done.25, bf16[360,256]{1,0:T(8,128)(2,1)} %copy-done.24, bf16[360,256]{1,0:T(8,128)(2,1)} %copy-done.26), custom_call_target="tpu_custom_call" | custom-call | bytes 1474560 | tf_op jit(solution)/shard_map/place_pieces/pallas_call | solution.py:111
  59.8 7.4 %optimizer_step.15 = (bf16[360,1024]{1,0:T(8,128)(2,1)}, f32[360,8192]{1,0:T(8,128)}, f32[360,8192]{1,0:T(8,128)}, f32[360,8192]{1,0:T(8,128)}) custom-call(s32[1]{0:T(128)} %bitcast.30.place, bf16[4,360,144]{2,1,0:T(8,128)(2,1)} %pad_maximum_fusion.1.grads, ...), custom_call_target="tpu_custom_call", output_to_operand_aliasing={{1}: (7, {}), {2}: (8, {}), {3}: (9, {})} | custom-call | flops 424673280 | bytes 12653568 | tf_op jit(solution)/shard_map/optimizer_step/pallas_call | solution.py:60
  67.9 1.4 collective-permute-start.22
  70.6 2.8 collective-permute-done.22.rest_3_
  74.1 3.2 %place_pieces.13 = (bf16[4,360,8192]{2,1,0:T(8,128)(2,1)}, f32[8,128]{1,0:T(8,128)}) custom-call(s32[5]{0:T(128)} %stack.194.where, bf16[360,256]{1,0:T(8,128)(2,1)} %get-tuple-element.93.rest_0_, bf16[360,256]{1,0:T(8,128)(2,1)} %copy-done.17, bf16[360,256]{1,0:T(8,128)(2,1)} %copy-done.18, ...), custom_call_target="tpu_custom_call", output_to_operand_aliasing={{0}: (5, {})} | custom-call | bytes 1474560 | tf_op jit(solution)/shard_map/place_pieces/pallas_call | solution.py:111
  77.3 7.4 %optimizer_step.16 = (bf16[360,1024]{1,0:T(8,128)(2,1)}, f32[360,8192]{1,0:T(8,128)}, f32[360,8192]{1,0:T(8,128)}, f32[360,8192]{1,0:T(8,128)}) custom-call(s32[1]{0:T(128)} %bitcast.29.place, bf16[4,360,144]{2,1,0:T(8,128)(2,1)} %pad_maximum_fusion.1.grads, ...), custom_call_target="tpu_custom_call", output_to_operand_aliasing={{1}: (7, {}), {2}: (8, {}), {3}: (9, {})} | custom-call | flops 424673280 | bytes 12653568 | tf_op jit(solution)/shard_map/optimizer_step/pallas_call | solution.py:60
  84.7 1.5 collective-permute-start.30
  86.8 7.8 %collective-permute-done.23.rest_1_ = bf16[360,512]{1,0:T(8,128)(2,1)} collective-permute-done((bf16[360,512]{1,0:T(8,128)(2,1)S(1)}, bf16[360,512]{1,0:T(8,128)(2,1)}, u32[]{:S(2)}, u32[]{:S(2)}) %collective-permute-start.23) | collective-permute-done | bytes 368672 | tf_op jit(solution)/shard_map/ppermute | solution.py:198
  95.0 3.7 %collective-permute-done.25.rest_3_ = bf16[360,512]{1,0:T(8,128)(2,1)S(1)} collective-permute-done((bf16[360,512]{1,0:T(8,128)(2,1)}, bf16[360,512]{1,0:T(8,128)(2,1)S(1)}, u32[]{:S(2)}, u32[]{:S(2)}) %collective-permute-start.25) | collective-permute-done | bytes 368672 | tf_op jit(solution)/shard_map/ppermute | solution.py:198
  99.4 1.6 collective-permute-start.29
  101.0 3.3 %collective-permute-done.30.rest_2_ = bf16[360,1024]{1,0:T(8,128)(2,1)} collective-permute-done((bf16[360,1024]{1,0:T(8,128)(2,1)}, bf16[360,1024]{1,0:T(8,128)(2,1)}, u32[]{:S(2)}, u32[]{:S(2)}) %collective-permute-start.30) | collective-permute-done | bytes 737312 | tf_op jit(solution)/shard_map/ppermute | solution.py:198
  104.3 1.6 collective-permute-start.28
  106.6 3.4 %place_pieces.14 = (bf16[4,360,8192]{2,1,0:T(8,128)(2,1)}, f32[8,128]{1,0:T(8,128)}) custom-call(s32[5]{0:T(128)} %stack.195.where, bf16[360,512]{1,0:T(8,128)(2,1)} %get-tuple-element.82.after.rest_0_, bf16[360,512]{1,0:T(8,128)(2,1)} %collective-permute-done.23.rest_1_, ...), custom_call_target="tpu_custom_call", output_to_operand_aliasing={{0}: (5, {})} | custom-call | bytes 2949120 | tf_op jit(solution)/shard_map/place_pieces/pallas_call | solution.py:111
  110.1 7.4 %optimizer_step.17 = (bf16[360,1024]{1,0:T(8,128)(2,1)}, f32[360,8192]{1,0:T(8,128)}, f32[360,8192]{1,0:T(8,128)}, f32[360,8192]{1,0:T(8,128)}) custom-call(s32[1]{0:T(128)} %bitcast.28.place, bf16[4,360,144]{2,1,0:T(8,128)(2,1)} %pad_maximum_fusion.1.grads, ...), custom_call_target="tpu_custom_call", output_to_operand_aliasing={{1}: (7, {}), {2}: (8, {}), {3}: (9, {})} | custom-call | flops 424673280 | bytes 12653568 | tf_op jit(solution)/shard_map/optimizer_step/pallas_call | solution.py:60
  117.4 2.7 collective-permute-done.27.rest_2_
  122.4 13.5 %collective-permute-done.28.rest_3_ = bf16[360,1024]{1,0:T(8,128)(2,1)} collective-permute-done((bf16[360,1024]{1,0:T(8,128)(2,1)}, bf16[360,1024]{1,0:T(8,128)(2,1)}, u32[]{:S(2)}, u32[]{:S(2)}) %collective-permute-start.28) | collective-permute-done | bytes 737312 | tf_op jit(solution)/shard_map/ppermute | solution.py:198
  136.2 13.7 %input_product.1 = (f32[4,144,1024]{2,1,0:T(8,128)}, bf16[4,144,1024]{2,1,0:T(8,128)(2,1)}) custom-call(s32[8]{0:T(128)} %pad_add_fusion.order, bf16[144,1440]{1,0:T(8,128)(2,1)} %bitcast.58, bf16[1440,8192]{1,0:T(8,128)(2,1)} %weight.1, bf16[360,512]{1,0:T(8,128)(2,1)} %get-tuple-element.82.after.rest_0_), custom_call_target="tpu_custom_call" | custom-call | flops 3397386240 | bytes 27131904 | tf_op jit(solution)/shard_map/input_product/pallas_call | solution.py:155
  150.7 4.0 %place_pieces.15 = (bf16[4,360,8192]{2,1,0:T(8,128)(2,1)}, f32[8,128]{1,0:T(8,128)}) custom-call(s32[5]{0:T(128)} %stack.196.where, bf16[360,1024]{1,0:T(8,128)(2,1)} %get-tuple-element.104.rest_0_, bf16[360,1024]{1,0:T(8,128)(2,1)} %collective-permute-done.26.rest_1_, ...), custom_call_target="tpu_custom_call", output_to_operand_aliasing={{0}: (5, {})} | custom-call | bytes 5898240 | tf_op jit(solution)/shard_map/place_pieces/pallas_call | solution.py:111
  154.7 7.4 %optimizer_step.18 = (bf16[360,1024]{1,0:T(8,128)(2,1)}, f32[360,8192]{1,0:T(8,128)}, f32[360,8192]{1,0:T(8,128)}, f32[360,8192]{1,0:T(8,128)}) custom-call(s32[1]{0:T(128)} %bitcast.27.place, bf16[4,360,144]{2,1,0:T(8,128)(2,1)} %pad_maximum_fusion.1.grads, ...), custom_call_target="tpu_custom_call", output_to_operand_aliasing={{1}: (7, {}), {2}: (8, {}), {3}: (9, {})} | custom-call | flops 424673280 | bytes 12653568 | tf_op jit(solution)/shard_map/optimizer_step/pallas_call | solution.py:60
  162.1 1.7 collective-permute-start.36
  165.5 4.2 %place_pieces.16 = (bf16[4,360,8192]{2,1,0:T(8,128)(2,1)}, f32[8,128]{1,0:T(8,128)}) custom-call(s32[5]{0:T(128)} %stack.197.where, bf16[360,1024]{1,0:T(8,128)(2,1)} %get-tuple-element.110.rest_0_, bf16[360,1024]{1,0:T(8,128)(2,1)} %collective-permute-done.29.rest_1_, ...), custom_call_target="tpu_custom_call", output_to_operand_aliasing={{0}: (5, {})} | custom-call | bytes 5898240 | tf_op jit(solution)/shard_map/place_pieces/pallas_call | solution.py:111
  169.7 12.1 %collective-permute-done.36.rest_2_ = bf16[360,1024]{1,0:T(8,128)(2,1)} collective-permute-done((bf16[360,1024]{1,0:T(8,128)(2,1)}, bf16[360,1024]{1,0:T(8,128)(2,1)}, u32[]{:S(2)}, u32[]{:S(2)}) %collective-permute-start.36) | collective-permute-done | bytes 737312 | tf_op jit(solution)/shard_map/ppermute | solution.py:198
  183.8 7.3 %optimizer_step.19 = (bf16[360,1024]{1,0:T(8,128)(2,1)}, f32[360,8192]{1,0:T(8,128)}, f32[360,8192]{1,0:T(8,128)}, f32[360,8192]{1,0:T(8,128)}) custom-call(s32[1]{0:T(128)} %bitcast.26.place, bf16[4,360,144]{2,1,0:T(8,128)(2,1)} %pad_maximum_fusion.1.grads, ...), custom_call_target="tpu_custom_call", output_to_operand_aliasing={{1}: (7, {}), {2}: (8, {}), {3}: (9, {})} | custom-call | flops 424673280 | bytes 12653568 | tf_op jit(solution)/shard_map/optimizer_step/pallas_call | solution.py:60
  191.1 6.0 %collective-permute-done.34.rest_3_ = bf16[360,1024]{1,0:T(8,128)(2,1)} collective-permute-done((bf16[360,1024]{1,0:T(8,128)(2,1)}, bf16[360,1024]{1,0:T(8,128)(2,1)}, u32[]{:S(2)}, u32[]{:S(2)}) %collective-permute-start.34) | collective-permute-done | bytes 737312 | tf_op jit(solution)/shard_map/ppermute | solution.py:198
  198.0 4.0 %place_pieces.17 = (bf16[4,360,8192]{2,1,0:T(8,128)(2,1)}, f32[8,128]{1,0:T(8,128)}) custom-call(s32[5]{0:T(128)} %stack.198.where, bf16[360,1024]{1,0:T(8,128)(2,1)} %get-tuple-element.116.rest_0_, bf16[360,1024]{1,0:T(8,128)(2,1)} %collective-permute-done.32.rest_1_, ...), custom_call_target="tpu_custom_call", output_to_operand_aliasing={{0}: (5, {})} | custom-call | bytes 5898240 | tf_op jit(solution)/shard_map/place_pieces/pallas_call | solution.py:111
  203.0 7.3 %optimizer_step.20 = (bf16[360,1024]{1,0:T(8,128)(2,1)}, f32[360,8192]{1,0:T(8,128)}, f32[360,8192]{1,0:T(8,128)}, f32[360,8192]{1,0:T(8,128)}) custom-call(s32[1]{0:T(128)} %bitcast.25.place, bf16[4,360,144]{2,1,0:T(8,128)(2,1)} %pad_maximum_fusion.1.grads, ...), custom_call_target="tpu_custom_call", output_to_operand_aliasing={{1}: (7, {}), {2}: (8, {}), {3}: (9, {})} | custom-call | flops 424673280 | bytes 12653568 | tf_op jit(solution)/shard_map/optimizer_step/pallas_call | solution.py:60
  213.4 3.7 %collective-permute-done.37.rest_3_ = bf16[360,1024]{1,0:T(8,128)(2,1)} collective-permute-done((bf16[360,1024]{1,0:T(8,128)(2,1)}, bf16[360,1024]{1,0:T(8,128)(2,1)}, u32[]{:S(2)}, u32[]{:S(2)}) %collective-permute-start.37) | collective-permute-done | bytes 737312 | tf_op jit(solution)/shard_map/ppermute | solution.py:198
  218.6 14.3 %collective-permute-done.38.rest_1_ = bf16[360,1024]{1,0:T(8,128)(2,1)} collective-permute-done((bf16[360,1024]{1,0:T(8,128)(2,1)}, bf16[360,1024]{1,0:T(8,128)(2,1)}, u32[]{:S(2)}, u32[]{:S(2)}) %collective-permute-start.38) | collective-permute-done | bytes 737312 | tf_op jit(solution)/shard_map/ppermute | solution.py:198
  232.9 1.6 collective-permute-start.40
  234.5 2.6 fusion.6
  238.0 7.9 %collective-permute-done.39.rest_2_ = bf16[360,1024]{1,0:T(8,128)(2,1)} collective-permute-done((bf16[360,1024]{1,0:T(8,128)(2,1)}, bf16[360,1024]{1,0:T(8,128)(2,1)}, u32[]{:S(2)}, u32[]{:S(2)}) %collective-permute-start.39) | collective-permute-done | bytes 737312 | tf_op jit(solution)/shard_map/ppermute | solution.py:198
  246.0 1.6 collective-permute-start.7
  247.5 4.0 %place_pieces.18 = (bf16[4,360,8192]{2,1,0:T(8,128)(2,1)}, f32[8,128]{1,0:T(8,128)}) custom-call(s32[5]{0:T(128)} %stack.199.where, bf16[360,1024]{1,0:T(8,128)(2,1)} %get-tuple-element.122.rest_0_, bf16[360,1024]{1,0:T(8,128)(2,1)} %copy-done.11, bf16[360,1024]{1,0:T(8,128)(2,1)} %collective-permute-done.36.rest_2_, ...), custom_call_target="tpu_custom_call", output_to_operand_aliasing={{0}: (5, {})} | custom-call | bytes 5898240 | tf_op jit(solution)/shard_map/place_pieces/pallas_call | solution.py:111
  251.6 1.7 collective-permute-start.8
  253.3 4.4 %optimizer_step.21 = (bf16[360,512]{1,0:T(8,128)(2,1)}, f32[360,8192]{1,0:T(8,128)}, f32[360,8192]{1,0:T(8,128)}, f32[360,8192]{1,0:T(8,128)}) custom-call(s32[1]{0:T(128)} %bitcast.24.place, bf16[4,360,144]{2,1,0:T(8,128)(2,1)} %pad_maximum_fusion.1.grads, ...), custom_call_target="tpu_custom_call", output_to_operand_aliasing={{1}: (7, {}), {2}: (8, {}), {3}: (9, {})} | custom-call | flops 212336640 | bytes 6534144 | tf_op jit(solution)/shard_map/optimizer_step/pallas_call | solution.py:60
  257.7 1.3 collective-permute-start.50
  261.2 3.3 %collective-permute-done.43.rest_3_ = bf16[360,1024]{1,0:T(8,128)(2,1)} collective-permute-done((bf16[360,1024]{1,0:T(8,128)(2,1)}, bf16[360,1024]{1,0:T(8,128)(2,1)}, u32[]{:S(2)}, u32[]{:S(2)}) %collective-permute-start.43) | collective-permute-done | bytes 737312 | tf_op jit(solution)/shard_map/ppermute | solution.py:198
  264.5 1.8 collective-permute-start.9
  267.5 4.0 %place_pieces.19 = (bf16[4,360,8192]{2,1,0:T(8,128)(2,1)}, f32[8,128]{1,0:T(8,128)}) custom-call(s32[5]{0:T(128)} %stack.200.where, bf16[360,1024]{1,0:T(8,128)(2,1)} %get-tuple-element.128.rest_0_, bf16[360,1024]{1,0:T(8,128)(2,1)} %collective-permute-done.38.rest_1_, ...), custom_call_target="tpu_custom_call", output_to_operand_aliasing={{0}: (5, {})} | custom-call | bytes 5898240 | tf_op jit(solution)/shard_map/place_pieces/pallas_call | solution.py:111
  271.5 3.3 %optimizer_step.22 = (bf16[360,256]{1,0:T(8,128)(2,1)}, f32[360,8192]{1,0:T(8,128)}, f32[360,8192]{1,0:T(8,128)}, f32[360,8192]{1,0:T(8,128)}) custom-call(s32[1]{0:T(128)} %bitcast.23.place, bf16[4,360,144]{2,1,0:T(8,128)(2,1)} %pad_maximum_fusion.1.grads, ...), custom_call_target="tpu_custom_call", output_to_operand_aliasing={{1}: (7, {}), {2}: (8, {}), {3}: (9, {})} | custom-call | flops 106168320 | bytes 3474432 | tf_op jit(solution)/shard_map/optimizer_step/pallas_call | solution.py:60
  274.8 4.0 %place_pieces.20 = (bf16[4,360,8192]{2,1,0:T(8,128)(2,1)}, f32[8,128]{1,0:T(8,128)}) custom-call(s32[5]{0:T(128)} %stack.201.where, bf16[360,1024]{1,0:T(8,128)(2,1)} %get-tuple-element.134.rest_0_, bf16[360,1024]{1,0:T(8,128)(2,1)} %collective-permute-done.41.rest_1_, ...), custom_call_target="tpu_custom_call", output_to_operand_aliasing={{0}: (5, {})} | custom-call | bytes 5898240 | tf_op jit(solution)/shard_map/place_pieces/pallas_call | solution.py:111
  278.9 1.7 collective-permute-start.48
  280.6 3.3 %optimizer_step.23 = (bf16[360,256]{1,0:T(8,128)(2,1)}, f32[360,8192]{1,0:T(8,128)}, f32[360,8192]{1,0:T(8,128)}, f32[360,8192]{1,0:T(8,128)}) custom-call(s32[1]{0:T(128)} %bitcast.22.place, bf16[4,360,144]{2,1,0:T(8,128)(2,1)} %pad_maximum_fusion.1.grads, ...), custom_call_target="tpu_custom_call", output_to_operand_aliasing={{1}: (7, {}), {2}: (8, {}), {3}: (9, {})} | custom-call | flops 106168320 | bytes 3474432 | tf_op jit(solution)/shard_map/optimizer_step/pallas_call | solution.py:60
  290.0 1.5 collective-permute-done.44.rest_1_
  292.2 2.0 fusion.3
  294.2 1.3 collective-permute-done.52.rest_3_
  296.3 3.4 %place_pieces.21 = (bf16[4,360,8192]{2,1,0:T(8,128)(2,1)}, f32[8,128]{1,0:T(8,128)}) custom-call(s32[5]{0:T(128)} %stack.204.where, bf16[360,512]{1,0:T(8,128)(2,1)} %get-tuple-element.142.rest_0_, bf16[360,512]{1,0:T(8,128)(2,1)} %copy-done.12, bf16[360,512]{1,0:T(8,128)(2,1)} %copy-done.13, ...), custom_call_target="tpu_custom_call", output_to_operand_aliasing={{0}: (5, {})} | custom-call | bytes 2949120 | tf_op jit(solution)/shard_map/place_pieces/pallas_call | solution.py:111
  300.5 3.2 %place_pieces.22 = (bf16[4,360,8192]{2,1,0:T(8,128)(2,1)}, f32[8,128]{1,0:T(8,128)}) custom-call(s32[5]{0:T(128)} %stack.203.where, bf16[360,256]{1,0:T(8,128)(2,1)} %get-tuple-element.141.rest_0_, bf16[360,256]{1,0:T(8,128)(2,1)} %copy-done.21, bf16[360,256]{1,0:T(8,128)(2,1)} %collective-permute-done.48.rest_2_, ...), custom_call_target="tpu_custom_call", output_to_operand_aliasing={{0}: (5, {})} | custom-call | bytes 1474560 | tf_op jit(solution)/shard_map/place_pieces/pallas_call | solution.py:111
  304.4 3.3 %place_pieces.23 = (bf16[4,360,8192]{2,1,0:T(8,128)(2,1)}, f32[8,128]{1,0:T(8,128)}) custom-call(s32[5]{0:T(128)} %stack.202.where, bf16[360,256]{1,0:T(8,128)(2,1)} %get-tuple-element.140.rest_0_, bf16[360,256]{1,0:T(8,128)(2,1)} %collective-permute-done.44.rest_1_, bf16[360,256]{1,0:T(8,128)(2,1)} %copy-done.20, ...), custom_call_target="tpu_custom_call", output_to_operand_aliasing={{0}: (5, {})} | custom-call | bytes 1474560 | tf_op jit(solution)/shard_map/place_pieces/pallas_call | solution.py:111
  (144 shorter events, 40.6 us)
Async XLA Ops:
  2.3 10.0 %collective-permute-start.3 = (bf16[144,1024]{1,0:T(8,128)(2,1)S(1)}, bf16[144,1024]{1,0:T(8,128)(2,1)S(1)}, u32[]{:S(2)}, u32[]{:S(2)}) collective-permute-start(bf16[144,1024]{1,0:T(8,128)(2,1)S(1)} %constant_dynamic-slice_fusion), channel_id=1, source_target_pairs={{0,8},{8,0},{16,24},{24,16},{1,9},{9,1},{17,25},{25,17},{2,10},{10... | collective-permute-start | bytes 884744 | tf_op jit(solution)/shard_map/ppermute | solution.py:198
  2.9 14.8 %collective-permute-start.4 = (bf16[144,1024]{1,0:T(8,128)(2,1)S(1)}, bf16[144,1024]{1,0:T(8,128)(2,1)S(1)}, u32[]{:S(2)}, u32[]{:S(2)}) collective-permute-start(bf16[144,1024]{1,0:T(8,128)(2,1)S(1)} %constant_dynamic-slice_fusion), channel_id=1, source_target_pairs={{0,16},{8,24},{16,0},{24,8},{1,17},{9,25},{17,1},{25,9},{2,18},{10... | collective-permute-start | bytes 884744 | tf_op jit(solution)/shard_map/ppermute | solution.py:198
  3.4 14.3 %collective-permute-start.5 = (bf16[144,1024]{1,0:T(8,128)(2,1)S(1)}, bf16[144,1024]{1,0:T(8,128)(2,1)S(1)}, u32[]{:S(2)}, u32[]{:S(2)}) collective-permute-start(bf16[144,1024]{1,0:T(8,128)(2,1)S(1)} %constant_dynamic-slice_fusion), channel_id=1, source_target_pairs={{0,24},{8,16},{16,8},{24,0},{1,25},{9,17},{17,9},{25,1},{2,26},{10... | collective-permute-start | bytes 884744 | tf_op jit(solution)/shard_map/ppermute | solution.py:198
  17.9 17.0 %copy-start.2 = (bf16[4,144,1024]{2,1,0:T(8,128)(2,1)}, bf16[4,144,1024]{2,1,0:T(8,128)(2,1)S(1)}, u32[]{:S(2)}) copy-start(bf16[4,144,1024]{2,1,0:T(8,128)(2,1)S(1)} %pad_maximum_fusion.acts) | copy-start | bytes 3538948
  17.9 41.9 %collective-permute-start.16 = (bf16[4,144,1024]{2,1,0:T(8,128)(2,1)S(1)}, bf16[4,144,1024]{2,1,0:T(8,128)(2,1)}, u32[]{:S(2)}, u32[]{:S(2)}) collective-permute-start(bf16[4,144,1024]{2,1,0:T(8,128)(2,1)S(1)} %pad_maximum_fusion.acts), channel_id=1, source_target_pairs={{0,1},{1,0},{2,3},{3,2},{4,5},{5,4},{6,7},{7,6},{8,9},{9,8},{10,11... | collective-permute-start | bytes 3538952 | tf_op jit(solution)/shard_map/ppermute | solution.py:201
  18.0 51.3 %collective-permute-start.10 = (bf16[4,144,1024]{2,1,0:T(8,128)(2,1)S(1)}, bf16[4,144,1024]{2,1,0:T(8,128)(2,1)S(1)}, u32[]{:S(2)}, u32[]{:S(2)}) collective-permute-start(bf16[4,144,1024]{2,1,0:T(8,128)(2,1)S(1)} %pad_maximum_fusion.acts), channel_id=1, source_target_pairs={{0,2},{1,3},{2,4},{3,5},{4,6},{5,7},{6,0},{7,1},{8,10},{9,11},{10,... | collective-permute-start | bytes 3538952 | tf_op jit(solution)/shard_map/ppermute | solution.py:205
  21.7 7.7 %collective-permute-start = (bf16[360,144]{1,0:T(8,128)(2,1)}, bf16[360,144]{1,0:T(8,128)(2,1)S(1)}, u32[]{:S(2)}, u32[]{:S(2)}) collective-permute-start(bf16[360,144]{1,0:T(8,128)(2,1)} %get-tuple-element.155), channel_id=1, source_target_pairs={{0,8},{8,0},{16,24},{24,16},{1,9},{9,1},{17,25},{25,17},{2,10},{10... | collective-permute-start | bytes 311048 | tf_op jit(solution)/shard_map/ppermute | solution.py:198
  23.2 10.6 %collective-permute-start.1 = (bf16[360,144]{1,0:T(8,128)(2,1)}, bf16[360,144]{1,0:T(8,128)(2,1)S(1)}, u32[]{:S(2)}, u32[]{:S(2)}) collective-permute-start(bf16[360,144]{1,0:T(8,128)(2,1)} %get-tuple-element.154), channel_id=1, source_target_pairs={{0,16},{8,24},{16,0},{24,8},{1,17},{9,25},{17,1},{25,9},{2,18},{10... | collective-permute-start | bytes 311048 | tf_op jit(solution)/shard_map/ppermute | solution.py:198
  23.7 10.1 %collective-permute-start.2 = (bf16[360,144]{1,0:T(8,128)(2,1)S(1)}, bf16[360,144]{1,0:T(8,128)(2,1)S(1)}, u32[]{:S(2)}, u32[]{:S(2)}) collective-permute-start(bf16[360,144]{1,0:T(8,128)(2,1)S(1)} %get-tuple-element.153), channel_id=1, source_target_pairs={{0,24},{8,16},{16,8},{24,0},{1,25},{9,17},{17,9},{25,1},{2,26},{10... | collective-permute-start | bytes 311048 | tf_op jit(solution)/shard_map/ppermute | solution.py:198
  38.2 5.7 %collective-permute-start.18 = (bf16[360,256]{1,0:T(8,128)(2,1)}, bf16[360,256]{1,0:T(8,128)(2,1)S(1)}, u32[]{:S(2)}, u32[]{:S(2)}) collective-permute-start(bf16[360,256]{1,0:T(8,128)(2,1)} %get-tuple-element.88.rest_0_), channel_id=1, source_target_pairs={{0,16},{8,24},{16,0},{24,8},{1,17},{9,25},{17,1},{25,9},{2,18},{10... | collective-permute-start | bytes 552968 | tf_op jit(solution)/shard_map/ppermute | solution.py:198
  38.7 15.1 %collective-permute-start.17 = (bf16[360,256]{1,0:T(8,128)(2,1)}, bf16[360,256]{1,0:T(8,128)(2,1)S(1)}, u32[]{:S(2)}, u32[]{:S(2)}) collective-permute-start(bf16[360,256]{1,0:T(8,128)(2,1)} %get-tuple-element.88.rest_0_), channel_id=1, source_target_pairs={{0,8},{8,0},{16,24},{24,16},{1,9},{9,1},{17,25},{25,17},{2,10},{10... | collective-permute-start | bytes 552968 | tf_op jit(solution)/shard_map/ppermute | solution.py:198
  43.9 11.2 %collective-permute-start.19 = (bf16[360,256]{1,0:T(8,128)(2,1)S(1)}, bf16[360,256]{1,0:T(8,128)(2,1)S(1)}, u32[]{:S(2)}, u32[]{:S(2)}) collective-permute-start(bf16[360,256]{1,0:T(8,128)(2,1)S(1)} %collective-permute-done.18.rest_2_), channel_id=1, source_target_pairs={{0,8},{8,0},{16,24},{24,16},{1,9},{9,1},{17,25},{25,17},{2,10},{10... | collective-permute-start | bytes 552968 | tf_op jit(solution)/shard_map/ppermute | solution.py:198
  47.8 20.1 %collective-permute-start.20 = (bf16[360,256]{1,0:T(8,128)(2,1)}, bf16[360,256]{1,0:T(8,128)(2,1)S(1)}, u32[]{:S(2)}, u32[]{:S(2)}) collective-permute-start(bf16[360,256]{1,0:T(8,128)(2,1)} %get-tuple-element.93.rest_0_), channel_id=1, source_target_pairs={{0,8},{8,0},{16,24},{24,16},{1,9},{9,1},{17,25},{25,17},{2,10},{10... | collective-permute-start | bytes 552968 | tf_op jit(solution)/shard_map/ppermute | solution.py:198
  49.3 5.8 %copy-start.16 = (bf16[360,256]{1,0:T(8,128)(2,1)S(1)}, bf16[360,256]{1,0:T(8,128)(2,1)}, u32[]{:S(2)}) copy-start(bf16[360,256]{1,0:T(8,128)(2,1)} %get-tuple-element.93.rest_0_) | copy-start | bytes 552964
  53.8 32.4 %collective-permute-start.24 = (bf16[360,512]{1,0:T(8,128)(2,1)}, bf16[360,512]{1,0:T(8,128)(2,1)}, u32[]{:S(2)}, u32[]{:S(2)}) collective-permute-start(bf16[360,512]{1,0:T(8,128)(2,1)} %get-tuple-element.82.after.rest_0_), channel_id=1, source_target_pairs={{0,16},{8,24},{16,0},{24,8},{1,17},{9,25},{17,1},{25,9},{2,18},{10... | collective-permute-start | bytes 1105928 | tf_op jit(solution)/shard_map/ppermute | solution.py:198
  55.1 14.2 %collective-permute-start.21 = (bf16[360,256]{1,0:T(8,128)(2,1)S(1)}, bf16[360,256]{1,0:T(8,128)(2,1)S(1)}, u32[]{:S(2)}, u32[]{:S(2)}) collective-permute-start(bf16[360,256]{1,0:T(8,128)(2,1)S(1)} %copy-done.16), channel_id=1, source_target_pairs={{0,16},{8,24},{16,0},{24,8},{1,17},{9,25},{17,1},{25,9},{2,18},{10... | collective-permute-start | bytes 552968 | tf_op jit(solution)/shard_map/ppermute | solution.py:198
  59.8 9.6 %copy-start.4 = (bf16[360,512]{1,0:T(8,128)(2,1)S(1)}, bf16[360,512]{1,0:T(8,128)(2,1)}, u32[]{:S(2)}) copy-start(bf16[360,512]{1,0:T(8,128)(2,1)} %get-tuple-element.82.after.rest_0_) | copy-start | bytes 1105924
  67.2 32.2 %collective-permute-start.26 = (bf16[360,1024]{1,0:T(8,128)(2,1)}, bf16[360,1024]{1,0:T(8,128)(2,1)}, u32[]{:S(2)}, u32[]{:S(2)}) collective-permute-start(bf16[360,1024]{1,0:T(8,128)(2,1)} %get-tuple-element.104.rest_0_), channel_id=1, source_target_pairs={{0,8},{8,0},{16,24},{24,16},{1,9},{9,1},{17,25},{25,17},{2,10},{10... | collective-permute-start | bytes 2211848 | tf_op jit(solution)/shard_map/ppermute | solution.py:198
  67.9 5.5 %collective-permute-start.22 = (bf16[360,256]{1,0:T(8,128)(2,1)S(1)}, bf16[360,256]{1,0:T(8,128)(2,1)S(1)}, u32[]{:S(2)}, u32[]{:S(2)}) collective-permute-start(bf16[360,256]{1,0:T(8,128)(2,1)S(1)} %collective-permute-done.20.rest_1_), channel_id=1, source_target_pairs={{0,16},{8,24},{16,0},{24,8},{1,17},{9,25},{17,1},{25,9},{2,18},{10... | collective-permute-start | bytes 552968 | tf_op jit(solution)/shard_map/ppermute | solution.py:198
  69.3 8.0 %copy-start.6 = (bf16[4,144,1024]{2,1,0:T(8,128)(2,1)}, bf16[4,144,1024]{2,1,0:T(8,128)(2,1)S(1)}, u32[]{:S(2)}) copy-start(bf16[4,144,1024]{2,1,0:T(8,128)(2,1)S(1)} %collective-permute-done.10.acts) | copy-start | bytes 3538948
  69.3 36.7 %collective-permute-start.15 = (bf16[4,144,1024]{2,1,0:T(8,128)(2,1)S(1)}, bf16[4,144,1024]{2,1,0:T(8,128)(2,1)}, u32[]{:S(2)}, u32[]{:S(2)}) collective-permute-start(bf16[4,144,1024]{2,1,0:T(8,128)(2,1)S(1)} %collective-permute-done.10.acts), channel_id=1, source_target_pairs={{0,1},{1,0},{2,3},{3,2},{4,5},{5,4},{6,7},{7,6},{8,9},{9,8},{10,11... | collective-permute-start | bytes 3538952 | tf_op jit(solution)/shard_map/ppermute | solution.py:201
  69.3 25.3 %collective-permute-start.23 = (bf16[360,512]{1,0:T(8,128)(2,1)S(1)}, bf16[360,512]{1,0:T(8,128)(2,1)}, u32[]{:S(2)}, u32[]{:S(2)}) collective-permute-start(bf16[360,512]{1,0:T(8,128)(2,1)S(1)} %copy-done.4), channel_id=1, source_target_pairs={{0,8},{8,0},{16,24},{24,16},{1,9},{9,1},{17,25},{25,17},{2,10},{10... | collective-permute-start | bytes 1105928 | tf_op jit(solution)/shard_map/ppermute | solution.py:198
  77.3 17.3 %copy-start.7 = (bf16[4,144,1024]{2,1,0:T(8,128)(2,1)S(1)}, bf16[4,144,1024]{2,1,0:T(8,128)(2,1)}, u32[]{:S(2)}) copy-start(bf16[4,144,1024]{2,1,0:T(8,128)(2,1)} %copy-done.6) | copy-start | bytes 3538948
  84.7 19.6 %collective-permute-start.30 = (bf16[360,1024]{1,0:T(8,128)(2,1)}, bf16[360,1024]{1,0:T(8,128)(2,1)}, u32[]{:S(2)}, u32[]{:S(2)}) collective-permute-start(bf16[360,1024]{1,0:T(8,128)(2,1)} %get-tuple-element.110.rest_0_), channel_id=1, source_target_pairs={{0,16},{8,24},{16,0},{24,8},{1,17},{9,25},{17,1},{25,9},{2,18},{10... | collective-permute-start | bytes 2211848 | tf_op jit(solution)/shard_map/ppermute | solution.py:198
  86.2 12.4 %collective-permute-start.25 = (bf16[360,512]{1,0:T(8,128)(2,1)}, bf16[360,512]{1,0:T(8,128)(2,1)S(1)}, u32[]{:S(2)}, u32[]{:S(2)}) collective-permute-start(bf16[360,512]{1,0:T(8,128)(2,1)} %collective-permute-done.24.rest_2_), channel_id=1, source_target_pairs={{0,8},{8,0},{16,24},{24,16},{1,9},{9,1},{17,25},{25,17},{2,10},{10... | collective-permute-start | bytes 1105928 | tf_op jit(solution)/shard_map/ppermute | solution.py:198
  94.6 27.7 %collective-permute-start.11 = (bf16[4,144,1024]{2,1,0:T(8,128)(2,1)S(1)}, bf16[4,144,1024]{2,1,0:T(8,128)(2,1)S(1)}, u32[]{:S(2)}, u32[]{:S(2)}) collective-permute-start(bf16[4,144,1024]{2,1,0:T(8,128)(2,1)S(1)} %copy-done.7), channel_id=1, source_target_pairs={{0,2},{1,3},{2,4},{3,5},{4,6},{5,7},{6,0},{7,1},{8,10},{9,11},{10,... | collective-permute-start | bytes 3538952 | tf_op jit(solution)/shard_map/ppermute | solution.py:205
  98.7 7.3 %copy-start.14 = (bf16[360,512]{1,0:T(8,128)(2,1)}, bf16[360,512]{1,0:T(8,128)(2,1)S(1)}, u32[]{:S(2)}) copy-start(bf16[360,512]{1,0:T(8,128)(2,1)S(1)} %collective-permute-done.25.rest_3_) | copy-start | bytes 1105924
  98.7 21.5 %collective-permute-start.27 = (bf16[360,1024]{1,0:T(8,128)(2,1)}, bf16[360,1024]{1,0:T(8,128)(2,1)}, u32[]{:S(2)}, u32[]{:S(2)}) collective-permute-start(bf16[360,1024]{1,0:T(8,128)(2,1)} %get-tuple-element.104.rest_0_), channel_id=1, source_target_pairs={{0,16},{8,24},{16,0},{24,8},{1,17},{9,25},{17,1},{25,9},{2,18},{10... | collective-permute-start | bytes 2211848 | tf_op jit(solution)/shard_map/ppermute | solution.py:198
  99.4 21.5 %collective-permute-start.29 = (bf16[360,1024]{1,0:T(8,128)(2,1)}, bf16[360,1024]{1,0:T(8,128)(2,1)}, u32[]{:S(2)}, u32[]{:S(2)}) collective-permute-start(bf16[360,1024]{1,0:T(8,128)(2,1)} %get-tuple-element.110.rest_0_), channel_id=1, source_target_pairs={{0,8},{8,0},{16,24},{24,16},{1,9},{9,1},{17,25},{25,17},{2,10},{10... | collective-permute-start | bytes 2211848 | tf_op jit(solution)/shard_map/ppermute | solution.py:198
  104.3 31.6 %collective-permute-start.28 = (bf16[360,1024]{1,0:T(8,128)(2,1)}, bf16[360,1024]{1,0:T(8,128)(2,1)}, u32[]{:S(2)}, u32[]{:S(2)}) collective-permute-start(bf16[360,1024]{1,0:T(8,128)(2,1)} %collective-permute-done.26.rest_1_), channel_id=1, source_target_pairs={{0,16},{8,24},{16,0},{24,8},{1,17},{9,25},{17,1},{25,9},{2,18},{10... | collective-permute-start | bytes 2211848 | tf_op jit(solution)/shard_map/ppermute | solution.py:198
  106.0 44.0 %collective-permute-start.31 = (bf16[360,1024]{1,0:T(8,128)(2,1)}, bf16[360,1024]{1,0:T(8,128)(2,1)}, u32[]{:S(2)}, u32[]{:S(2)}) collective-permute-start(bf16[360,1024]{1,0:T(8,128)(2,1)} %collective-permute-done.30.rest_2_), channel_id=1, source_target_pairs={{0,8},{8,0},{16,24},{24,16},{1,9},{9,1},{17,25},{25,17},{2,10},{10... | collective-permute-start | bytes 2211848 | tf_op jit(solution)/shard_map/ppermute | solution.py:198
  120.1 41.9 %collective-permute-start.32 = (bf16[360,1024]{1,0:T(8,128)(2,1)}, bf16[360,1024]{1,0:T(8,128)(2,1)}, u32[]{:S(2)}, u32[]{:S(2)}) collective-permute-start(bf16[360,1024]{1,0:T(8,128)(2,1)} %get-tuple-element.116.rest_0_), channel_id=1, source_target_pairs={{0,8},{8,0},{16,24},{24,16},{1,9},{9,1},{17,25},{25,17},{2,10},{10... | collective-permute-start | bytes 2211848 | tf_op jit(solution)/shard_map/ppermute | solution.py:198
  120.9 42.8 %collective-permute-start.33 = (bf16[360,1024]{1,0:T(8,128)(2,1)}, bf16[360,1024]{1,0:T(8,128)(2,1)}, u32[]{:S(2)}, u32[]{:S(2)}) collective-permute-start(bf16[360,1024]{1,0:T(8,128)(2,1)} %get-tuple-element.116.rest_0_), channel_id=1, source_target_pairs={{0,16},{8,24},{16,0},{24,8},{1,17},{9,25},{17,1},{25,9},{2,18},{10... | collective-permute-start | bytes 2211848 | tf_op jit(solution)/shard_map/ppermute | solution.py:198
  122.4 27.6 %copy-start.8 = (bf16[4,144,1024]{2,1,0:T(8,128)(2,1)}, bf16[4,144,1024]{2,1,0:T(8,128)(2,1)S(1)}, u32[]{:S(2)}) copy-start(bf16[4,144,1024]{2,1,0:T(8,128)(2,1)S(1)} %collective-permute-done.11.acts) | copy-start | bytes 3538948
  122.4 60.2 %collective-permute-start.14 = (bf16[4,144,1024]{2,1,0:T(8,128)(2,1)S(1)}, bf16[4,144,1024]{2,1,0:T(8,128)(2,1)}, u32[]{:S(2)}, u32[]{:S(2)}) collective-permute-start(bf16[4,144,1024]{2,1,0:T(8,128)(2,1)S(1)} %collective-permute-done.11.acts), channel_id=1, source_target_pairs={{0,1},{1,0},{2,3},{3,2},{4,5},{5,4},{6,7},{7,6},{8,9},{9,8},{10,11... | collective-permute-start | bytes 3538952 | tf_op jit(solution)/shard_map/ppermute | solution.py:201
  135.9 66.1 %collective-permute-start.12 = (bf16[4,144,1024]{2,1,0:T(8,128)(2,1)S(1)}, bf16[4,144,1024]{2,1,0:T(8,128)(2,1)S(1)}, u32[]{:S(2)}, u32[]{:S(2)}) collective-permute-start(bf16[4,144,1024]{2,1,0:T(8,128)(2,1)S(1)} %collective-permute-done.11.acts), channel_id=1, source_target_pairs={{0,2},{1,3},{2,4},{3,5},{4,6},{5,7},{6,0},{7,1},{8,10},{9,11},{10,... | collective-permute-start | bytes 3538952 | tf_op jit(solution)/shard_map/ppermute | solution.py:205
  149.9 61.3 %collective-permute-start.6 = (bf16[4,144,1024]{2,1,0:T(8,128)(2,1)}, bf16[4,144,1024]{2,1,0:T(8,128)(2,1)S(1)}, u32[]{:S(2)}, u32[]{:S(2)}) collective-permute-start(bf16[4,144,1024]{2,1,0:T(8,128)(2,1)} %get-tuple-element.84), channel_id=1, source_target_pairs={{0,1},{1,0},{2,3},{3,2},{4,5},{5,4},{6,7},{7,6},{8,9},{9,8},{10,11... | collective-permute-start | bytes 3538952 | tf_op jit(solution)/shard_map/ppermute | solution.py:201
  162.1 19.7 %collective-permute-start.36 = (bf16[360,1024]{1,0:T(8,128)(2,1)}, bf16[360,1024]{1,0:T(8,128)(2,1)}, u32[]{:S(2)}, u32[]{:S(2)}) collective-permute-start(bf16[360,1024]{1,0:T(8,128)(2,1)} %get-tuple-element.122.rest_0_), channel_id=1, source_target_pairs={{0,16},{8,24},{16,0},{24,8},{1,17},{9,25},{17,1},{25,9},{2,18},{10... | collective-permute-start | bytes 2211848 | tf_op jit(solution)/shard_map/ppermute | solution.py:198
  163.7 33.4 %collective-permute-start.34 = (bf16[360,1024]{1,0:T(8,128)(2,1)}, bf16[360,1024]{1,0:T(8,128)(2,1)}, u32[]{:S(2)}, u32[]{:S(2)}) collective-permute-start(bf16[360,1024]{1,0:T(8,128)(2,1)} %collective-permute-done.32.rest_1_), channel_id=1, source_target_pairs={{0,16},{8,24},{16,0},{24,8},{1,17},{9,25},{17,1},{25,9},{2,18},{10... | collective-permute-start | bytes 2211848 | tf_op jit(solution)/shard_map/ppermute | solution.py:198
  165.5 16.3 %copy-start.10 = (bf16[360,1024]{1,0:T(8,128)(2,1)S(1)}, bf16[360,1024]{1,0:T(8,128)(2,1)}, u32[]{:S(2)}) copy-start(bf16[360,1024]{1,0:T(8,128)(2,1)} %get-tuple-element.122.rest_0_) | copy-start | bytes 2211844
  181.7 29.5 %collective-permute-start.35 = (bf16[360,1024]{1,0:T(8,128)(2,1)S(1)}, bf16[360,1024]{1,0:T(8,128)(2,1)S(1)}, u32[]{:S(2)}, u32[]{:S(2)}) collective-permute-start(bf16[360,1024]{1,0:T(8,128)(2,1)S(1)} %copy-done.10), channel_id=1, source_target_pairs={{0,8},{8,0},{16,24},{24,16},{1,9},{9,1},{17,25},{25,17},{2,10},{10... | collective-permute-start | bytes 2211848 | tf_op jit(solution)/shard_map/ppermute | solution.py:198
  182.6 34.5 %collective-permute-start.37 = (bf16[360,1024]{1,0:T(8,128)(2,1)}, bf16[360,1024]{1,0:T(8,128)(2,1)}, u32[]{:S(2)}, u32[]{:S(2)}) collective-permute-start(bf16[360,1024]{1,0:T(8,128)(2,1)} %collective-permute-done.36.rest_2_), channel_id=1, source_target_pairs={{0,8},{8,0},{16,24},{24,16},{1,9},{9,1},{17,25},{25,17},{2,10},{10... | collective-permute-start | bytes 2211848 | tf_op jit(solution)/shard_map/ppermute | solution.py:198
  197.2 35.7 %collective-permute-start.38 = (bf16[360,1024]{1,0:T(8,128)(2,1)}, bf16[360,1024]{1,0:T(8,128)(2,1)}, u32[]{:S(2)}, u32[]{:S(2)}) collective-permute-start(bf16[360,1024]{1,0:T(8,128)(2,1)} %get-tuple-element.128.rest_0_), channel_id=1, source_target_pairs={{0,8},{8,0},{16,24},{24,16},{1,9},{9,1},{17,25},{25,17},{2,10},{10... | collective-permute-start | bytes 2211848 | tf_op jit(solution)/shard_map/ppermute | solution.py:198
  210.4 24.1 %collective-permute-start.42 = (bf16[360,1024]{1,0:T(8,128)(2,1)}, bf16[360,1024]{1,0:T(8,128)(2,1)}, u32[]{:S(2)}, u32[]{:S(2)}) collective-permute-start(bf16[360,1024]{1,0:T(8,128)(2,1)} %get-tuple-element.134.rest_0_), channel_id=1, source_target_pairs={{0,16},{8,24},{16,0},{24,8},{1,17},{9,25},{17,1},{25,9},{2,18},{10... | collective-permute-start | bytes 2211848 | tf_op jit(solution)/shard_map/ppermute | solution.py:198
  211.2 23.3 %copy-start.5 = (bf16[4,144,1024]{2,1,0:T(8,128)(2,1)}, bf16[4,144,1024]{2,1,0:T(8,128)(2,1)S(1)}, u32[]{:S(2)}) copy-start(bf16[4,144,1024]{2,1,0:T(8,128)(2,1)S(1)} %collective-permute-done.6) | copy-start | bytes 3538948
  211.2 40.4 %collective-permute-start.13 = (bf16[4,144,1024]{2,1,0:T(8,128)(2,1)}, bf16[4,144,1024]{2,1,0:T(8,128)(2,1)S(1)}, u32[]{:S(2)}, u32[]{:S(2)}) collective-permute-start(bf16[4,144,1024]{2,1,0:T(8,128)(2,1)} %copy-done.9), channel_id=1, source_target_pairs={{0,1},{1,0},{2,3},{3,2},{4,5},{5,4},{6,7},{7,6},{8,9},{9,8},{10,11... | collective-permute-start | bytes 3538952 | tf_op jit(solution)/shard_map/ppermute | solution.py:201
  212.1 33.8 %collective-permute-start.39 = (bf16[360,1024]{1,0:T(8,128)(2,1)}, bf16[360,1024]{1,0:T(8,128)(2,1)}, u32[]{:S(2)}, u32[]{:S(2)}) collective-permute-start(bf16[360,1024]{1,0:T(8,128)(2,1)} %get-tuple-element.128.rest_0_), channel_id=1, source_target_pairs={{0,16},{8,24},{16,0},{24,8},{1,17},{9,25},{17,1},{25,9},{2,18},{10... | collective-permute-start | bytes 2211848 | tf_op jit(solution)/shard_map/ppermute | solution.py:198
  217.1 40.6 %collective-permute-start.41 = (bf16[360,1024]{1,0:T(8,128)(2,1)}, bf16[360,1024]{1,0:T(8,128)(2,1)}, u32[]{:S(2)}, u32[]{:S(2)}) collective-permute-start(bf16[360,1024]{1,0:T(8,128)(2,1)} %get-tuple-element.134.rest_0_), channel_id=1, source_target_pairs={{0,8},{8,0},{16,24},{24,16},{1,9},{9,1},{17,25},{25,17},{2,10},{10... | collective-permute-start | bytes 2211848 | tf_op jit(solution)/shard_map/ppermute | solution.py:198
  232.9 27.3 %collective-permute-start.40 = (bf16[360,1024]{1,0:T(8,128)(2,1)}, bf16[360,1024]{1,0:T(8,128)(2,1)}, u32[]{:S(2)}, u32[]{:S(2)}) collective-permute-start(bf16[360,1024]{1,0:T(8,128)(2,1)} %collective-permute-done.38.rest_1_), channel_id=1, source_target_pairs={{0,16},{8,24},{16,0},{24,8},{1,17},{9,25},{17,1},{25,9},{2,18},{10... | collective-permute-start | bytes 2211848 | tf_op jit(solution)/shard_map/ppermute | solution.py:198
  234.5 30.0 %collective-permute-start.43 = (bf16[360,1024]{1,0:T(8,128)(2,1)}, bf16[360,1024]{1,0:T(8,128)(2,1)}, u32[]{:S(2)}, u32[]{:S(2)}) collective-permute-start(bf16[360,1024]{1,0:T(8,128)(2,1)} %collective-permute-done.42.rest_2_), channel_id=1, source_target_pairs={{0,8},{8,0},{16,24},{24,16},{1,9},{9,1},{17,25},{25,17},{2,10},{10... | collective-permute-start | bytes 2211848 | tf_op jit(solution)/shard_map/ppermute | solution.py:198
  246.0 32.9 %collective-permute-start.7 = (bf16[144,1024]{1,0:T(8,128)(2,1)}, bf16[144,1024]{1,0:T(8,128)(2,1)}, u32[]{:S(2)}, u32[]{:S(2)}) collective-permute-start(bf16[144,1024]{1,0:T(8,128)(2,1)} %get-tuple-element.149), channel_id=1, source_target_pairs={{0,2},{1,3},{2,4},{3,5},{4,6},{5,7},{6,0},{7,1},{8,10},{9,11},{10,... | collective-permute-start | bytes 884744 | tf_op jit(solution)/shard_map/ppermute | solution.py:205
  251.6 32.3 %collective-permute-start.8 = (bf16[144,1024]{1,0:T(8,128)(2,1)}, bf16[144,1024]{1,0:T(8,128)(2,1)}, u32[]{:S(2)}, u32[]{:S(2)}) collective-permute-start(bf16[144,1024]{1,0:T(8,128)(2,1)} %get-tuple-element.151), channel_id=1, source_target_pairs={{0,4},{1,5},{2,6},{3,7},{4,0},{5,1},{6,2},{7,3},{8,12},{9,13},{10,... | collective-permute-start | bytes 884744 | tf_op jit(solution)/shard_map/ppermute | solution.py:205
  257.7 26.3 %collective-permute-start.50 = (bf16[360,512]{1,0:T(8,128)(2,1)}, bf16[360,512]{1,0:T(8,128)(2,1)S(1)}, u32[]{:S(2)}, u32[]{:S(2)}) collective-permute-start(bf16[360,512]{1,0:T(8,128)(2,1)} %get-tuple-element.142.rest_0_), channel_id=1, source_target_pairs={{0,8},{8,0},{16,24},{24,16},{1,9},{9,1},{17,25},{25,17},{2,10},{10... | collective-permute-start | bytes 1105928 | tf_op jit(solution)/shard_map/ppermute | solution.py:198
  260.2 29.0 %collective-permute-start.51 = (bf16[360,512]{1,0:T(8,128)(2,1)}, bf16[360,512]{1,0:T(8,128)(2,1)S(1)}, u32[]{:S(2)}, u32[]{:S(2)}) collective-permute-start(bf16[360,512]{1,0:T(8,128)(2,1)} %get-tuple-element.142.rest_0_), channel_id=1, source_target_pairs={{0,16},{8,24},{16,0},{24,8},{1,17},{9,25},{17,1},{25,9},{2,18},{10... | collective-permute-start | bytes 1105928 | tf_op jit(solution)/shard_map/ppermute | solution.py:198
  264.5 22.6 %collective-permute-start.9 = (bf16[144,1024]{1,0:T(8,128)(2,1)}, bf16[144,1024]{1,0:T(8,128)(2,1)}, u32[]{:S(2)}, u32[]{:S(2)}) collective-permute-start(bf16[144,1024]{1,0:T(8,128)(2,1)} %get-tuple-element.150), channel_id=1, source_target_pairs={{0,6},{1,7},{2,0},{3,1},{4,2},{5,3},{6,4},{7,5},{8,14},{9,15},{10,... | collective-permute-start | bytes 884744 | tf_op jit(solution)/shard_map/ppermute | solution.py:205
  278.9 9.4 %collective-permute-start.48 = (bf16[360,256]{1,0:T(8,128)(2,1)}, bf16[360,256]{1,0:T(8,128)(2,1)}, u32[]{:S(2)}, u32[]{:S(2)}) collective-permute-start(bf16[360,256]{1,0:T(8,128)(2,1)} %get-tuple-element.141.rest_0_), channel_id=1, source_target_pairs={{0,16},{8,24},{16,0},{24,8},{1,17},{9,25},{17,1},{25,9},{2,18},{10... | collective-permute-start | bytes 552968 | tf_op jit(solution)/shard_map/ppermute | solution.py:198
  283.9 7.6 %collective-permute-start.44 = (bf16[360,256]{1,0:T(8,128)(2,1)}, bf16[360,256]{1,0:T(8,128)(2,1)}, u32[]{:S(2)}, u32[]{:S(2)}) collective-permute-start(bf16[360,256]{1,0:T(8,128)(2,1)} %get-tuple-element.140.rest_0_), channel_id=1, source_target_pairs={{0,8},{8,0},{16,24},{24,16},{1,9},{9,1},{17,25},{25,17},{2,10},{10... | collective-permute-start | bytes 552968 | tf_op jit(solution)/shard_map/ppermute | solution.py:198
  284.0 11.6 %copy-start.12 = (bf16[360,512]{1,0:T(8,128)(2,1)}, bf16[360,512]{1,0:T(8,128)(2,1)S(1)}, u32[]{:S(2)}) copy-start(bf16[360,512]{1,0:T(8,128)(2,1)S(1)} %collective-permute-done.50.rest_1_) | copy-start | bytes 1105924
  284.0 11.6 %collective-permute-start.52 = (bf16[360,512]{1,0:T(8,128)(2,1)S(1)}, bf16[360,512]{1,0:T(8,128)(2,1)S(1)}, u32[]{:S(2)}, u32[]{:S(2)}) collective-permute-start(bf16[360,512]{1,0:T(8,128)(2,1)S(1)} %collective-permute-done.50.rest_1_), channel_id=1, source_target_pairs={{0,16},{8,24},{16,0},{24,8},{1,17},{9,25},{17,1},{25,9},{2,18},{10... | collective-permute-start | bytes 1105928 | tf_op jit(solution)/shard_map/ppermute | solution.py:198
  287.1 12.6 %collective-permute-start.47 = (bf16[360,256]{1,0:T(8,128)(2,1)}, bf16[360,256]{1,0:T(8,128)(2,1)S(1)}, u32[]{:S(2)}, u32[]{:S(2)}) collective-permute-start(bf16[360,256]{1,0:T(8,128)(2,1)} %get-tuple-element.141.rest_0_), channel_id=1, source_target_pairs={{0,8},{8,0},{16,24},{24,16},{1,9},{9,1},{17,25},{25,17},{2,10},{10... | collective-permute-start | bytes 552968 | tf_op jit(solution)/shard_map/ppermute | solution.py:198
  288.3 11.4 %collective-permute-start.49 = (bf16[360,256]{1,0:T(8,128)(2,1)}, bf16[360,256]{1,0:T(8,128)(2,1)S(1)}, u32[]{:S(2)}, u32[]{:S(2)}) collective-permute-start(bf16[360,256]{1,0:T(8,128)(2,1)} %collective-permute-done.48.rest_2_), channel_id=1, source_target_pairs={{0,8},{8,0},{16,24},{24,16},{1,9},{9,1},{17,25},{25,17},{2,10},{10... | collective-permute-start | bytes 552968 | tf_op jit(solution)/shard_map/ppermute | solution.py:198
  289.2 6.4 %copy-start.13 = (bf16[360,512]{1,0:T(8,128)(2,1)}, bf16[360,512]{1,0:T(8,128)(2,1)S(1)}, u32[]{:S(2)}) copy-start(bf16[360,512]{1,0:T(8,128)(2,1)S(1)} %collective-permute-done.51.rest_2_) | copy-start | bytes 1105924
  289.2 14.5 %collective-permute-start.45 = (bf16[360,256]{1,0:T(8,128)(2,1)}, bf16[360,256]{1,0:T(8,128)(2,1)S(1)}, u32[]{:S(2)}, u32[]{:S(2)}) collective-permute-start(bf16[360,256]{1,0:T(8,128)(2,1)} %get-tuple-element.140.rest_0_), channel_id=1, source_target_pairs={{0,16},{8,24},{16,0},{24,8},{1,17},{9,25},{17,1},{25,9},{2,18},{10... | collective-permute-start | bytes 552968 | tf_op jit(solution)/shard_map/ppermute | solution.py:198
  291.5 12.2 %collective-permute-start.46 = (bf16[360,256]{1,0:T(8,128)(2,1)}, bf16[360,256]{1,0:T(8,128)(2,1)S(1)}, u32[]{:S(2)}, u32[]{:S(2)}) collective-permute-start(bf16[360,256]{1,0:T(8,128)(2,1)} %collective-permute-done.44.rest_1_), channel_id=1, source_target_pairs={{0,16},{8,24},{16,0},{24,8},{1,17},{9,25},{17,1},{25,9},{2,18},{10... | collective-permute-start | bytes 552968 | tf_op jit(solution)/shard_map/ppermute | solution.py:198
  (16 other events, 31.3 us)

commit v2 on v0

--- a/solution.py
+++ b/solution.py
@@ -1,6 +1,10 @@
+import functools
+
 import jax
 import jax.numpy as jnp
 from jax import lax
+from jax.experimental import pallas as pl
+from jax.experimental.pallas import tpu as pltpu
 from jax.sharding import PartitionSpec as P
 
 beta_one = 0.9
@@ -10,9 +14,433 @@
 decay_rate = 0.1
 epsilon = 1e-08
 ema_keep = 0.99
-
-
-def body(activations, hidden_grad, weight, master, first_moment, second_moment, ema_state):
+first_fix = 1.0 - beta_one**adam_step
+second_fix = 1.0 - beta_two**adam_step
+
+LEAD = 256
+LAG = 3
+PRODUCT_FIRST = 6
+PRODUCT_AT = 3
+FIRST_CUTS = (2, 2)
+LAST_CUTS = (4,)
+UNPACK_AT = 0
+GATE = 2
+FORWARD_BY_X = (1,0,1,0,1,0,1,0,1,0,1,0)
+LAST_MORE = 0
+TAIL_SPLIT = 2
+STEP_COST = 8000000
+PLACE_COST = 850
+PRODUCT_COST = 6000000
+VMEM_LIMIT = 58 * 1024 * 1024
+ANY = pl.BlockSpec(memory_space=pl.ANY)
+PARAMS = pltpu.CompilerParams(vmem_limit_bytes=VMEM_LIMIT)
+
+
+def adam(gradient, master, first_moment, second_moment, ema_state):
+    new_first = beta_one * first_moment + (1.0 - beta_one) * gradient
+    new_second = beta_two * second_moment + (1.0 - beta_two) * gradient * gradient
+    update = (
+        new_first / first_fix / (jnp.sqrt(new_second / second_fix) + epsilon) + decay_rate * master
+    )
+    master_out = master - learn_rate * update
+    ema_next = ema_keep * ema_state + (1.0 - ema_keep) * master_out
+    return master_out, new_first, new_second, ema_next
+
+
+def feature_of(ids, n_tensor, step, side):
+    n_pairs = n_tensor // 2
+    pair = lax.rem(lax.div(ids[1], 2) + (n_pairs - step), n_pairs)
+    core = lax.rem(ids[1], 2)
+    return 2 * pair + (1 - core if side else core)
+
+
+def peer_of(dp, mask):
+    high, low = lax.div(dp, 2), lax.rem(dp, 2)
+    return 2 * (1 - high if mask & 2 else high) + (1 - low if mask & 1 else low)
+
+
+def pack_kernel(units, width, ids, acts, grads, *messages):
+    for mask, message in enumerate(messages):
+        message[:, :width] = acts[...]
+        for owner in range(len(messages)):
+
+            @pl.when(peer_of(ids[0], mask) == owner)
+            def _(owner=owner, message=message):
+                message[:, width : width + units] = grads[:, owner * units : (owner + 1) * units]
+
+
+def pack_messages(ids, acts, grads, n_dp, width):
+    tokens, all_units = grads.shape
+    units = all_units // n_dp
+    message = jax.ShapeDtypeStruct((tokens, width + pl.cdiv(units, 128) * 128), acts.dtype)
+    return pl.pallas_call(
+        functools.partial(pack_kernel, units, width),
+        out_shape=(message,) * n_dp,
+        grid_spec=pltpu.PrefetchScalarGridSpec(
+            num_scalar_prefetch=1,
+            grid=(1,),
+            in_specs=[
+                pl.BlockSpec((tokens, width), lambda j, ids: (0, ids[1])),
+                pl.BlockSpec((tokens, all_units), lambda j, ids: (0, 0)),
+            ],
+            out_specs=[pl.BlockSpec(message.shape, lambda j, ids: (0, 0))] * n_dp,
+        ),
+        compiler_params=PARAMS,
+        cost_estimate=pl.CostEstimate(
+            flops=0, bytes_accessed=tokens * all_units * 8, transcendentals=0
+        ),
+        name="pack_messages",
+    )(ids, acts, grads)
+
+
+def column_of(ids, where, slice_width):
+    n_tensor, step, side, offset = where
+    return pl.multiple_of(feature_of(ids, n_tensor, step, side) * slice_width + offset, LEAD)
+
+
+def place_scratch(groups):
+    scratch = []
+    for _, masks, pieces in groups:
+        scratch.append(pltpu.VMEM((len(masks),) + pieces[0].shape, pieces[0].dtype))
+        scratch.append(pltpu.SemaphoreType.DMA((len(masks),)))
+        scratch.append(pltpu.SemaphoreType.DMA((len(masks),)))
+    return scratch
+
+
+def placements(ids, slice_width, layout, pieces, out, scratch):
+    loads, stores = [], []
+    for i, (where, masks) in enumerate(layout):
+        held, arrived, left = scratch[3 * i : 3 * i + 3]
+        column = column_of(ids, where, slice_width)
+        for j, mask in enumerate(masks):
+            piece = pieces[len(loads)]
+            goal = out.at[peer_of(ids[0], mask), :, pl.ds(column, piece.shape[1])]
+            loads.append(pltpu.make_async_copy(piece, held.at[j], arrived.at[j]))
+            stores.append(pltpu.make_async_copy(held.at[j], goal, left.at[j]))
+    return loads, stores
+
+
+def forward_copies(loads, stores):
+    for load, store in zip(loads, stores):
+        load.wait()
+        store.start()
+
+
+def step_kernel(
+    inverse, units, slice_width, offset, unpack, n_acts, n_unread, layout, n_steps, ids, *refs
+):
+    acts = refs[:n_acts]
+    refs = refs[n_acts:]
+    if units is None:
+        gradient = lambda: jnp.dot(refs[0][...], acts[0][...], preferred_element_type=jnp.float32)
+        refs_states = refs[1:5]
+        rest = refs[5:]
+    else:
+
+        def gradient():
+            total = None
+            for message in acts:
+                term = lax.dot_general(
+                    message[:, slice_width : slice_width + units],
+                    message[:, offset : offset + tile],
+                    (((0,), (0,)), ((), ())),
+                    preferred_element_type=jnp.float32,
+                )
+                total = term if total is None else total + term
+            return total
+
+        refs_states = refs[:4]
+        rest = refs[4:]
+    master, first, second, ema = refs_states
+    n_pieces = sum(len(masks) for _, masks in layout)
+    pieces = rest[:n_pieces]
+    rest = rest[n_pieces + n_unread :]
+    piece, master_out, first_out, second_out = rest[:4]
+    tile = piece.shape[1]
+    step = pl.program_id(0)
+    if n_pieces:
+        loads, stores = placements(ids, slice_width, layout, pieces, rest[4], rest[5:])
+
+        @pl.when(step == 0)
+        def _():
+            for load in loads:
+                load.start()
+
+        if n_steps > 1:
+
+            @pl.when(step == n_steps - 1)
+            def _():
+                forward_copies(loads, stores)
+
+    outs = adam(gradient() * inverse, master[...], first[...], second[...], ema[...])
+    master_out[...] = outs[0]
+    first_out[...] = outs[1]
+    second_out[...] = outs[2]
+    piece[...] = outs[3].astype(piece.dtype)
+    if unpack:
+        all_acts, all_grads = rest[-2:]
+        tokens = acts[0].shape[0]
+        for i, message in enumerate(acts):
+            rows = slice(i * tokens, (i + 1) * tokens)
+            all_acts[rows, :] = message[:, :slice_width]
+            all_grads[:, rows] = message[:, slice_width : slice_width + units].T
+    if n_pieces:
+
+        @pl.when(step == n_steps - 1)
+        def _():
+            if n_steps == 1:
+                forward_copies(loads, stores)
+            for store in stores:
+                store.wait()
+
+
+def optimizer_step(
+    inverse, units, unpack, ids, where, width, acts, grads, states, olds, unread, groups, whole_shape, out
+):
+    rows, model_width = states[0].shape
+    n_tensor, step, side, offset = where
+    slice_width = model_width // n_tensor
+    tile = 2 * LEAD if width % (2 * LEAD) == 0 and offset % (2 * LEAD) == 0 else LEAD
+    n_steps = width // tile
+
+    def state_at(j, ids):
+        return 0, feature_of(ids, n_tensor, step, side) * (slice_width // tile) + offset // tile + j
+
+    def whole(array):
+        return pl.BlockSpec(array.shape, lambda j, ids: (0,) * array.ndim)
+
+    state_spec = pl.BlockSpec((rows, tile), state_at)
+    if units is None:
+        first_tile = offset // tile
+        in_specs = [
+            pl.BlockSpec((acts[0].shape[0], tile), lambda j, ids: (0, first_tile + j)),
+            whole(grads),
+        ]
+        operands = [acts[0], grads]
+    else:
+        in_specs = [whole(message) for message in acts]
+        operands = list(acts)
+    n_acts = len(acts)
+    operands += list(states)
+    in_specs += [state_spec] * 4
+    out_shapes = [jax.ShapeDtypeStruct((rows, width), jnp.bfloat16)]
+    out_shapes += [jax.ShapeDtypeStruct((rows, model_width), jnp.float32)] * 3
+    out_specs = [pl.BlockSpec((rows, tile), lambda j, ids: (0, j))] + [state_spec] * 3
+    pieces = [piece for group in groups for piece in group[2]]
+    if groups:
+        out_shapes.append(jax.ShapeDtypeStruct(whole_shape, jnp.bfloat16))
+        out_specs.append(ANY)
+    if unpack:
+        tokens = n_acts * acts[0].shape[0]
+        for shape in ((tokens, slice_width), (units, tokens)):
+            out_shapes.append(jax.ShapeDtypeStruct(shape, jnp.bfloat16))
+            out_specs.append(pl.BlockSpec(shape, lambda j, ids: (0, 0)))
+    operands += pieces
+    aliases = {}
+    extra = list(olds)
+    for i in range(len(olds)):
+        aliases[1 + len(operands) + i] = 1 + i
+    if out is not None:
+        aliases[1 + len(operands) + len(extra)] = 4
+        extra.append(out)
+    extra += list(unread)
+    in_specs += [ANY] * (len(pieces) + len(extra))
+    operands += extra
+    return pl.pallas_call(
+        functools.partial(
+            step_kernel,
+            inverse,
+            units,
+            slice_width,
+            offset,
+            unpack,
+            n_acts,
+            len(extra),
+            [group[:2] for group in groups],
+            n_steps,
+        ),
+        out_shape=tuple(out_shapes),
+        grid_spec=pltpu.PrefetchScalarGridSpec(
+            num_scalar_prefetch=1,
+            grid=(n_steps,),
+            in_specs=in_specs,
+            out_specs=out_specs,
+            scratch_shapes=place_scratch(groups),
+        ),
+        input_output_aliases=aliases,
+        compiler_params=PARAMS,
+        cost_estimate=pl.CostEstimate(
+            flops=STEP_COST * width,
+            bytes_accessed=rows * width * 30 + sum(piece.size for piece in pieces) * 4,
+            transcendentals=rows * width,
+        ),
+        name="optimizer_step",
+    )(ids, *operands)
+
+
+def place_kernel(slice_width, layout, ids, *refs):
+    n_pieces = sum(len(masks) for _, masks in layout)
+    scratch = refs[n_pieces + 3 :]
+    loads, stores = placements(
+        ids, slice_width, layout, refs[:n_pieces], refs[n_pieces + 2], scratch
+    )
+    for load in loads:
+        load.start()
+    forward_copies(loads, stores)
+    for store in stores:
+        store.wait()
+
+
+def place_pieces(ids, groups, slice_width, out, after):
+    pieces = [piece for group in groups for piece in group[2]]
+    size = sum(piece.size for piece in pieces)
+    return pl.pallas_call(
+        functools.partial(place_kernel, slice_width, [group[:2] for group in groups]),
+        out_shape=jax.ShapeDtypeStruct(out.shape, out.dtype),
+        grid_spec=pltpu.PrefetchScalarGridSpec(
+            num_scalar_prefetch=1,
+            grid=(),
+            in_specs=[ANY] * (len(pieces) + 2),
+            out_specs=ANY,
+            scratch_shapes=place_scratch(groups),
+        ),
+        input_output_aliases={1 + len(pieces): 0},
+        compiler_params=PARAMS,
+        cost_estimate=pl.CostEstimate(
+            flops=PLACE_COST * size, bytes_accessed=size * 4, transcendentals=0
+        ),
+        name="place_pieces",
+    )(ids, *pieces, out, after)
+
+
+def product_kernel(grads, weight, *rest):
+    terms = rest[-1]
+    product = jnp.dot(grads[...], weight[...], preferred_element_type=jnp.float32)
+    terms[0] = product.astype(terms.dtype)
+
+
+def input_product(grads, weight, slices, first, last, old, after):
+    tokens, units = grads.shape
+    width = weight.shape[1] // slices
+    n_old = 0 if old is None else 1
+    return pl.pallas_call(
+        product_kernel,
+        out_shape=jax.ShapeDtypeStruct((slices, tokens, width), jnp.bfloat16),
+        grid=(last - first,),
+        in_specs=[
+            pl.BlockSpec((tokens, units), lambda j: (0, 0)),
+            pl.BlockSpec((units, width), lambda j: (0, first + j)),
+        ]
+        + [ANY] * (n_old + 1),
+        out_specs=pl.BlockSpec((1, tokens, width), lambda j: (first + j, 0, 0)),
+        input_output_aliases={3: 0} if n_old else {},
+        compiler_params=PARAMS,
+        cost_estimate=pl.CostEstimate(
+            flops=PRODUCT_COST * width * (last - first),
+            bytes_accessed=units * width * (last - first) * 2,
+            transcendentals=0,
+        ),
+        name="input_product",
+    )(grads, weight, after, *([old] if n_old else []))
+
+
+def square_body(activations, hidden_grad, weight, master, first_moment, second_moment, ema_state):
+    batches, tok_rows, model_width = activations.shape
+    shard_units = master.shape[0]
+    n_dp = lax.axis_size("dp")
+    n_tensor = lax.axis_size("tensor")
+    n_pairs = n_tensor // 2
+    tokens = batches * tok_rows
+    inverse = 1.0 / (tokens * n_dp)
+    width = model_width // n_tensor
+    ids = jnp.stack([lax.axis_index("dp"), lax.axis_index("tensor")]).astype(jnp.int32)
+
+    def swap(array, mask):
+        return lax.ppermute(array, "dp", [(i, i ^ mask) for i in range(n_dp)])
+
+    def swap_core(array):
+        return lax.ppermute(array, "tensor", [(i, i ^ 1) for i in range(n_tensor)])
+
+    def shift_pair(array, steps):
+        moves = [(i, (i + 2 * steps) % n_tensor) for i in range(n_tensor)]
+        return lax.ppermute(array, "tensor", moves)
+
+    acts_two = activations.reshape(tokens, model_width)
+    grads_two = hidden_grad.reshape(tokens, -1)
+    messages = pack_messages(ids, acts_two, grads_two, n_dp, width)
+    messages = [messages[0]] + [swap(messages[m], m) for m in range(1, n_dp)]
+    acts, grads = None, None
+    terms = input_product(grads_two, weight, n_tensor, 0, PRODUCT_FIRST, None, messages[0])
+
+    states = (master, first_moment, second_moment, ema_state)
+    shape = (n_dp, shard_units, model_width)
+    olds, out, unread, sent, placed = (), None, (terms,), [], 0
+    masks = tuple(range(n_dp))
+    n_cuts = len(FIRST_CUTS) + len(LAST_CUTS) + n_tensor - 2
+    for step in range(n_pairs):
+        if step > 0:
+            acts = shift_pair(acts, 1)
+        for side in range(2):
+            block = swap_core(acts) if side else acts
+            chunk = 2 * step + side
+            parts = FIRST_CUTS if chunk == 0 else LAST_CUTS if chunk == n_tensor - 1 else (4,)
+            offset = 0
+            for part in parts:
+                cut = width * part // 4
+                count = len(sent)
+                where = (n_tensor, step, side, offset)
+                until = max(count - LAG + 1, 0) + (LAST_MORE if count == n_cuts - 1 else 0)
+                groups, placed = [(w, masks, p) for p, w in sent[placed:until]], max(until, placed)
+                early = count < len(FIRST_CUTS)
+                unpack = count == UNPACK_AT
+                gate = tuple(sent[count - GATE][0][1:3]) if 0 < GATE <= count else ()
+                results = optimizer_step(
+                    inverse,
+                    shard_units if early else None,
+                    unpack,
+                    ids,
+                    where,
+                    cut,
+                    messages if early else [block],
+                    grads,
+                    states,
+                    olds,
+                    unread + gate,
+                    groups,
+                    shape,
+                    out,
+                )
+                piece, olds = results[0], results[1:4]
+                out = results[4] if groups else None
+                if unpack:
+                    acts, grads = results[-2:]
+                unread = ()
+                by_x, by_y = swap(piece, 1), swap(piece, 2)
+                by_both = swap(by_y, 1) if FORWARD_BY_X[count] else swap(by_x, 2)
+                sent.append(((piece, by_x, by_y, by_both), where))
+                if count == PRODUCT_AT:
+                    terms = input_product(
+                        grads_two, weight, n_tensor, PRODUCT_FIRST, n_tensor, terms, piece
+                    )
+                    unread = (terms,)
+                offset += cut
+    terms = lax.all_to_all(terms, "tensor", 0, 0)
+    d_inputs = jnp.sum(terms.astype(jnp.float32), axis=0).astype(jnp.bfloat16)
+    groups = [(w, masks, p) for p, w in sent[placed:-1]]
+    pieces, where = sent[-1]
+    groups.append((where, masks[:3], pieces[:3]))
+    if TAIL_SPLIT:
+        out = place_pieces(ids, groups[:-TAIL_SPLIT], width, out, d_inputs)
+        groups = groups[-TAIL_SPLIT:]
+    out = place_pieces(ids, groups, width, out, d_inputs)
+    out = place_pieces(ids, [(where, masks[3:], pieces[3:])], width, out, d_inputs)
+    d_inputs = d_inputs.reshape(batches, tok_rows, width)
+    ema_copy = out.reshape(n_dp * shard_units, model_width)
+
+    return (d_inputs, *olds, ema_copy)
+
+
+def general_body(activations, hidden_grad, weight, master, first_moment, second_moment, ema_state):
     batches, tok_rows, model_width = activations.shape
     shard_units = master.shape[0]
     inverse = 1.0 / (batches * tok_rows * lax.axis_size("dp"))
@@ -38,17 +466,23 @@
     )
     rounded = lax.optimization_barrier(per_shard.astype(jnp.bfloat16))
     gradient = jnp.sum(rounded.astype(jnp.float32), axis=0)
-    new_first = beta_one * first_moment + (1.0 - beta_one) * gradient
-    new_second = beta_two * second_moment + (1.0 - beta_two) * gradient * gradient
-    first_fix = 1.0 - beta_one**adam_step
-    second_fix = 1.0 - beta_two**adam_step
-    update = (
-        new_first / first_fix / (jnp.sqrt(new_second / second_fix) + epsilon) + decay_rate * master
+    master_out, new_first, new_second, ema_next = adam(
+        gradient, master, first_moment, second_moment, ema_state
     )
-    master_out = master - learn_rate * update
-    ema_next = ema_keep * ema_state + (1.0 - ema_keep) * master_out
     ema_copy = lax.all_gather(ema_next.astype(jnp.bfloat16), "dp", axis=0, tiled=True)
     return (d_inputs, master_out, new_first, new_second, ema_copy)
+
+
+def body(*arrays):
+    activations, _, _, master = arrays[:4]
+    n_tensor = lax.axis_size("tensor")
+    square = (
+        lax.axis_size("dp") == 4
+        and n_tensor % 2 == 0
+        and master.shape[0] % 8 == 0
+        and activations.shape[2] % (n_tensor * 4 * LEAD) == 0
+    )
+    return square_body(*arrays) if square else general_body(*arrays)
 
 
 def solution(mesh):

time: 449 us -> 249 us (0.55)
  waiting for transfers between devices: 303 us -> 108 us
  Pallas kernels: 0 us -> 93.7 us
  matrix products: 53.8 us -> 0 us
  other arithmetic: 51.7 us -> 1.81 us
  starting transfers between devices: 0.43 us -> 37.4 us
  local copies, waits for them, and re-layouts: 21.1 us -> 5.84 us
  between operations: 15.5 us -> 1.04 us
    all_gather x3 -> x0, waiting for transfers between devices: 302 us -> none  [the longest x1 211 us: body(): lax.all_gather(ema_next.astype(jnp.bfloat16), 'dp', axis=0, tiled=True)]
    ppermute x0 -> x37, waiting for transfers between devices: none -> 108 us  [the longest x30 101 us: swap(): return lax.ppermute(array, 'dp', [(i, i ^ mask) for i in range(n_dp)])]
    pallas_call x0 -> x15, Pallas kernels: none -> 93.7 us  [the longest x9 65 us: optimizer_step(): pl.pallas_call(functools.partial(step_kernel, inverse, units, slice_width...]
    dot_general x4 -> x0, matrix products: 53.8 us -> none  [the longest x3 39.7 us: body(): jnp.dot(hidden_grad[batch_id], weight, preferred_element_type=jnp.float32)]
    convert_element_type x1 -> x0, other arithmetic: 34.4 us -> none  [body(): ema_next.astype(jnp.bfloat16)]
    ppermute x0 -> x37, starting transfers between devices: none -> 33.2 us  [the longest x30 29.6 us: swap(): return lax.ppermute(array, 'dp', [(i, i ^ mask) for i in range(n_dp)])]
    unnamed x3 -> x42, local copies, waits for them, and re-layouts: 19.8 us -> 5.84 us
    reduce_sum x1, other arithmetic: 13.7 us -> 1.19 us  [square_body(): d_inputs = jnp.sum(terms.astype(jnp.float32), axis=0).astype(jnp.bfloat16)]
  transfers between devices with their start and end apart: 6 -> 38, of which waited for: 2 -> 15; matrix products, arithmetic and copies ran while one was open for 24% -> 0% of each run, Pallas kernels for 0% -> 33%
where the time goes in v2:
time: 249 us; the launch traced here: 248 us
  waiting for transfers between devices  108 us (43%)
  Pallas kernels  93.7 us (38%)
  starting transfers between devices  37.4 us (15%)
  local copies, waits for them, and re-layouts  5.84 us (2%)
    ppermute x30, waiting for transfers between devices, swap(): return lax.ppermute(array, 'dp', [(i, i ^ mask) for i in range(n_dp)])  101 us
    pallas_call x9, Pallas kernels, optimizer_step(): pl.pallas_call(functools.partial(step_kernel, inverse, units, slice_width...  65 us
    ppermute x30, starting transfers between devices, swap(): return lax.ppermute(array, 'dp', [(i, i ^ mask) for i in range(n_dp)])  29.6 us
    pallas_call x2, Pallas kernels, input_product(): pl.pallas_call(product_kernel, out_shape=jax.ShapeDtypeStruct((slices, to...  14.1 us
    pallas_call x3, Pallas kernels, place_pieces(): pl.pallas_call(functools.partial(place_kernel, slice_width, [group[:2] fo...  11.2 us
    ppermute x3, waiting for transfers between devices, shift_pair(): return lax.ppermute(array, 'tensor', moves)  7.21 us
    unnamed x42, local copies, waits for them, and re-layouts  5.84 us
  transfers between devices with their start and end apart: 38, of which 15 were waited for; matrix products, arithmetic and copies ran while one was open for 0% of the time, Pallas kernels for 33%

profile of v2, /device:TPU:22, one launch (start us, length us, event | category | flops | bytes accessed | tf_op | source)
XLA Modules:
  0.0 247.7 jit_solution(15722001373685502512)
XLA Ops:
  0.6 0.6 pad_add_fusion.ids
  1.3 3.4 %pack_messages.1 = (bf16[144,1408]{1,0:T(8,128)(2,1)}, bf16[144,1408]{1,0:T(8,128)(2,1)}, bf16[144,1408]{1,0:T(8,128)(2,1)}, bf16[144,1408]{1,0:T(8,128)(2,1)}) custom-call(s32[2]{0:T(128)} %pad_add_fusion.ids, bf16[144,8192]{1,0:T(8,128)(2,1)} %bitcast.8, bf16[144,1440]{1,0:T(8,128)(2,1)} %bitcast.9), custom_call_target="tpu_custom_call" | custom-call | bytes 1658880 | tf_op jit(solution)/shard_map/pack_messages/pallas_call | solution.py:76
  4.7 0.5 collective-permute-start
  5.2 0.5 collective-permute-start.1
  5.7 2.4 collective-permute-start.2
  8.2 9.8 %input_product.2.refs_8_.rest_1_ = bf16[8,144,1024]{2,1,0:T(8,128)(2,1)} custom-call(bf16[144,1440]{1,0:T(8,128)(2,1)} %bitcast.10, bf16[1440,8192]{1,0:T(8,128)(2,1)} %weight.3, bf16[144,1408]{1,0:T(8,128)(2,1)} %get-tuple-element.53.rest_0_.refs_0_), custom_call_target="tpu_custom_call" | custom-call | flops 36864000000 | bytes 17694720 | tf_op jit(solution)/shard_map/input_product/pallas_call | solution.py:326
  18.0 6.9 %collective-permute-done.1.refs_2_ = bf16[144,1408]{1,0:T(8,128)(2,1)S(1)} collective-permute-done((bf16[144,1408]{1,0:T(8,128)(2,1)}, bf16[144,1408]{1,0:T(8,128)(2,1)S(1)}, u32[]{:S(2)}, u32[]{:S(2)}) %collective-permute-start.1) | collective-permute-done | bytes 405536 | tf_op jit(solution)/shard_map/ppermute | solution.py:359
  25.0 0.7 copy-done.9
  25.7 0.8 copy-done.10
  26.5 6.2 %optimizer_step.9 = (bf16[360,512]{1,0:T(8,128)(2,1)}, f32[360,8192]{1,0:T(8,128)}, f32[360,8192]{1,0:T(8,128)}, f32[360,8192]{1,0:T(8,128)}, bf16[576,1024]{1,0:T(8,128)(2,1)}, /*index=5*/bf16[360,576]{1,0:T(8,128)(2,1)}) custom-call(s32[2]{0:T(128)} %pad_add_fusion.ids, bf16[144,1408]{1,0:T(8,128)(2,1)} %get-tuple-element.53.rest_0_.refs_0_, ...), custom_call_target="tpu_custom_call" | custom-call | flops 4096000000 | bytes 5529600 | tf_op jit(solution)/shard_map/optimizer_step/pallas_call | solution.py:249
  32.7 0.5 collective-permute-start.5
  33.2 1.5 collective-permute-start.4
  34.8 1.6 collective-permute-start.3
  36.3 5.6 %optimizer_step.10 = (bf16[360,512]{1,0:T(8,128)(2,1)}, f32[360,8192]{1,0:T(8,128)}, f32[360,8192]{1,0:T(8,128)}, f32[360,8192]{1,0:T(8,128)}) custom-call(s32[2]{0:T(128)} %pad_add_fusion.ids, bf16[144,1408]{1,0:T(8,128)(2,1)} %get-tuple-element.53.rest_0_.refs_0_, ...), custom_call_target="tpu_custom_call", output_to_operand_aliasing={{1}: (9, {}), {2}: (10, {}), {3}: (11, {})} | custom-call | flops 4096000000 | bytes 5529600 | tf_op jit(solution)/shard_map/optimizer_step/pallas_call | solution.py:249
  42.5 1.4 collective-permute-done.5.refs_10_.refs_8_
  44.4 1.9 collective-permute-start.6
  46.3 7.4 %collective-permute-done.8.refs_13_.refs_7_ = bf16[360,512]{1,0:T(8,128)(2,1)S(1)} collective-permute-done((bf16[360,512]{1,0:T(8,128)(2,1)}, bf16[360,512]{1,0:T(8,128)(2,1)S(1)}, u32[]{:S(2)}, u32[]{:S(2)}) %collective-permute-start.8) | collective-permute-done | bytes 368672 | tf_op jit(solution)/shard_map/ppermute | solution.py:359
  53.7 1.5 collective-permute-start.17
  55.2 1.0 copy-done.17
  56.2 6.6 %optimizer_step.11 = (bf16[360,1024]{1,0:T(8,128)(2,1)}, f32[360,8192]{1,0:T(8,128)}, f32[360,8192]{1,0:T(8,128)}, f32[360,8192]{1,0:T(8,128)}) custom-call(s32[2]{0:T(128)} %pad_add_fusion.ids, bf16[576,1024]{1,0:T(8,128)(2,1)} %copy-done.17, ...), custom_call_target="tpu_custom_call", output_to_operand_aliasing={{1}: (7, {}), {2}: (8, {}), {3}: (9, {})} | custom-call | flops 8192000000 | bytes 11059200 | tf_op jit(solution)/shard_map/optimizer_step/pallas_call | solution.py:249
  62.8 0.6 collective-permute-start.13
  64.2 0.8 copy-done.15
  65.1 7.4 %optimizer_step.12 = (bf16[360,1024]{1,0:T(8,128)(2,1)}, f32[360,8192]{1,0:T(8,128)}, f32[360,8192]{1,0:T(8,128)}, f32[360,8192]{1,0:T(8,128)}, bf16[4,360,8192]{2,1,0:T(8,128)(2,1)}) custom-call(s32[2]{0:T(128)} %pad_add_fusion.ids, bf16[576,1024]{1,0:T(8,128)(2,1)} %copy-done.15, ...), custom_call_target="tpu_custom_call", output_to_operand_aliasing={{1}: (11, {}), {2}: (12, {}), {3}: (13, {})} | custom-call | flops 8192000000 | bytes 14008320 | tf_op jit(solution)/shard_map/optimizer_step/pallas_call | solution.py:249
  72.5 1.6 collective-permute-start.18
  74.1 0.6 collective-permute-start.10
  74.7 4.2 %input_product.3.refs_14_ = bf16[8,144,1024]{2,1,0:T(8,128)(2,1)} custom-call(bf16[144,1440]{1,0:T(8,128)(2,1)} %bitcast.11, bf16[1440,8192]{1,0:T(8,128)(2,1)} %weight.3, bf16[360,1024]{1,0:T(8,128)(2,1)} %get-tuple-element.70.rest_0_.refs_6_, bf16[8,144,1024]{2,1,0:T(8,128)(2,1)} %input_product.2.refs_8_.rest_1_), custom_call_target="tpu_custom_call", output_to_operand_aliasing={{}: (3, {})} | custom-call | flops 12288000000 | bytes 5898240 | tf_op jit(solution)/shard_map/input_product/pallas_call | solution.py:326
  79.0 2.9 %collective-permute-done.13.refs_15_.refs_7_ = bf16[360,1024]{1,0:T(8,128)(2,1)S(1)} collective-permute-done((bf16[360,1024]{1,0:T(8,128)(2,1)}, bf16[360,1024]{1,0:T(8,128)(2,1)S(1)}, u32[]{:S(2)}, u32[]{:S(2)}) %collective-permute-start.13) | collective-permute-done | bytes 737312 | tf_op jit(solution)/shard_map/ppermute | solution.py:359
  81.9 1.5 collective-permute-start.15
  83.3 14.3 %collective-permute-done.18.refs_14_.refs_7_ = bf16[360,1024]{1,0:T(8,128)(2,1)S(1)} collective-permute-done((bf16[360,1024]{1,0:T(8,128)(2,1)}, bf16[360,1024]{1,0:T(8,128)(2,1)S(1)}, u32[]{:S(2)}, u32[]{:S(2)}) %collective-permute-start.18) | collective-permute-done | bytes 737312 | tf_op jit(solution)/shard_map/ppermute | solution.py:359
  97.7 1.0 copy-done.16
  98.7 7.4 %optimizer_step.13 = (bf16[360,1024]{1,0:T(8,128)(2,1)}, f32[360,8192]{1,0:T(8,128)}, f32[360,8192]{1,0:T(8,128)}, f32[360,8192]{1,0:T(8,128)}, bf16[4,360,8192]{2,1,0:T(8,128)(2,1)}) custom-call(s32[2]{0:T(128)} %pad_add_fusion.ids, bf16[576,1024]{1,0:T(8,128)(2,1)} %copy-done.16, ...), custom_call_target="tpu_custom_call", output_to_operand_aliasing={{1}: (11, {}), {2}: (12, {}), {3}: (13, {}), {4}: (14, {})} | custom-call | flops 8192000000 | bytes 14008320 | tf_op jit(solution)/shard_map/optimizer_step/pallas_call | solution.py:249
  106.2 1.5 collective-permute-start.23
  107.7 1.7 collective-permute-start.24
  109.4 4.1 %collective-permute-done.15.refs_9_ = bf16[360,1024]{1,0:T(8,128)(2,1)} collective-permute-done((bf16[360,1024]{1,0:T(8,128)(2,1)S(1)}, bf16[360,1024]{1,0:T(8,128)(2,1)}, u32[]{:S(2)}, u32[]{:S(2)}) %collective-permute-start.15) | collective-permute-done | bytes 737312 | tf_op jit(solution)/shard_map/ppermute | solution.py:359
  113.5 1.4 collective-permute-start.11
  114.9 7.9 %optimizer_step.14 = (bf16[360,1024]{1,0:T(8,128)(2,1)}, f32[360,8192]{1,0:T(8,128)}, f32[360,8192]{1,0:T(8,128)}, f32[360,8192]{1,0:T(8,128)}, bf16[4,360,8192]{2,1,0:T(8,128)(2,1)}) custom-call(s32[2]{0:T(128)} %pad_add_fusion.ids, ...), custom_call_target="tpu_custom_call", output_to_operand_aliasing={{1}: (11, {}), {2}: (12, {}), {3}: (13, {}), {4}: (14, {})} | custom-call | flops 8192000000 | bytes 16957440 | tf_op jit(solution)/shard_map/optimizer_step/pallas_call | solution.py:249
  122.8 1.6 collective-permute-start.20
  124.4 4.2 %all-to-all-start = ((bf16[8,144,1024]{2,1,0:T(8,128)(2,1)}), bf16[8,144,1024]{2,1,0:T(8,128)(2,1)S(1)}, u32[]{:S(2)}, u32[]{:S(2)}) async-start(bf16[8,144,1024]{2,1,0:T(8,128)(2,1)} %input_product.3.refs_14_), calls=%async_computation | async-start | bytes 4718592 | tf_op jit(solution)/shard_map/all_to_all | solution.py:427
  128.6 0.8 collective-permute-done.23.refs_14_.refs_7_
  129.4 1.5 collective-permute-start.25
  130.8 14.2 %collective-permute-done.20.refs_14_.refs_7_ = bf16[360,1024]{1,0:T(8,128)(2,1)S(1)} collective-permute-done((bf16[360,1024]{1,0:T(8,128)(2,1)}, bf16[360,1024]{1,0:T(8,128)(2,1)S(1)}, u32[]{:S(2)}, u32[]{:S(2)}) %collective-permute-start.20) | collective-permute-done | bytes 737312 | tf_op jit(solution)/shard_map/ppermute | solution.py:359
  145.0 7.2 %collective-permute-done.11.refs_0_ = bf16[576,1024]{1,0:T(8,128)(2,1)} collective-permute-done((bf16[576,1024]{1,0:T(8,128)(2,1)}, bf16[576,1024]{1,0:T(8,128)(2,1)}, u32[]{:S(2)}, u32[]{:S(2)}) %collective-permute-start.11) | collective-permute-done | bytes 1179680 | tf_op jit(solution)/shard_map/ppermute | solution.py:366
  152.3 7.9 %optimizer_step.15 = (bf16[360,1024]{1,0:T(8,128)(2,1)}, f32[360,8192]{1,0:T(8,128)}, f32[360,8192]{1,0:T(8,128)}, f32[360,8192]{1,0:T(8,128)}, bf16[4,360,8192]{2,1,0:T(8,128)(2,1)}) custom-call(s32[2]{0:T(128)} %pad_add_fusion.ids, ...), custom_call_target="tpu_custom_call", output_to_operand_aliasing={{1}: (11, {}), {2}: (12, {}), {3}: (13, {}), {4}: (14, {})} | custom-call | flops 8192000000 | bytes 16957440 | tf_op jit(solution)/shard_map/optimizer_step/pallas_call | solution.py:249
  160.2 1.9 collective-permute-start.28
  162.1 0.7 collective-permute-start.29
  163.0 7.9 %optimizer_step.16 = (bf16[360,1024]{1,0:T(8,128)(2,1)}, f32[360,8192]{1,0:T(8,128)}, f32[360,8192]{1,0:T(8,128)}, f32[360,8192]{1,0:T(8,128)}, bf16[4,360,8192]{2,1,0:T(8,128)(2,1)}) custom-call(s32[2]{0:T(128)} %pad_add_fusion.ids, ...), custom_call_target="tpu_custom_call", output_to_operand_aliasing={{1}: (11, {}), {2}: (12, {}), {3}: (13, {}), {4}: (14, {})} | custom-call | flops 8192000000 | bytes 16957440 | tf_op jit(solution)/shard_map/optimizer_step/pallas_call | solution.py:249
  171.1 8.7 %collective-permute-done.28.refs_14_.refs_1_ = bf16[360,1024]{1,0:T(8,128)(2,1)S(1)} collective-permute-done((bf16[360,1024]{1,0:T(8,128)(2,1)}, bf16[360,1024]{1,0:T(8,128)(2,1)S(1)}, u32[]{:S(2)}, u32[]{:S(2)}) %collective-permute-start.28) | collective-permute-done | bytes 737312 | tf_op jit(solution)/shard_map/ppermute | solution.py:359
  179.8 1.1 collective-permute-done.29.refs_15_.refs_2_
  181.0 0.9 copy-done.7
  181.9 8.0 %optimizer_step.17 = (bf16[360,1024]{1,0:T(8,128)(2,1)}, f32[360,8192]{1,0:T(8,128)}, f32[360,8192]{1,0:T(8,128)}, f32[360,8192]{1,0:T(8,128)}, bf16[4,360,8192]{2,1,0:T(8,128)(2,1)}) custom-call(s32[2]{0:T(128)} %pad_add_fusion.ids, ...), custom_call_target="tpu_custom_call", output_to_operand_aliasing={{1}: (11, {}), {2}: (12, {}), {3}: (13, {}), {4}: (14, {})} | custom-call | flops 8192000000 | bytes 16957440 | tf_op jit(solution)/shard_map/optimizer_step/pallas_call | solution.py:249
  189.9 0.8 collective-permute-start.30
  190.7 0.9 collective-permute-start.36
  191.5 1.3 collective-permute-start.33
  192.9 2.8 %collective-permute-done.32.refs_1_ = bf16[360,1024]{1,0:T(8,128)(2,1)} collective-permute-done((bf16[360,1024]{1,0:T(8,128)(2,1)}, bf16[360,1024]{1,0:T(8,128)(2,1)}, u32[]{:S(2)}, u32[]{:S(2)}) %collective-permute-start.32) | collective-permute-done | bytes 737312 | tf_op jit(solution)/shard_map/ppermute | solution.py:359
  195.7 0.5 collective-permute-start.34
  196.3 1.9 collective-permute-start.35
  198.2 11.5 %collective-permute-done.30.refs_6_ = bf16[360,1024]{1,0:T(8,128)(2,1)} collective-permute-done((bf16[360,1024]{1,0:T(8,128)(2,1)}, bf16[360,1024]{1,0:T(8,128)(2,1)}, u32[]{:S(2)}, u32[]{:S(2)}) %collective-permute-start.30) | collective-permute-done | bytes 737312 | tf_op jit(solution)/shard_map/ppermute | solution.py:359
  209.7 0.9 collective-permute-start.31
  210.6 1.2 reduce_sum.12.refs_5_.refs_8_.refs_2_
  211.8 3.4 %place_pieces.3.refs_7_ = bf16[4,360,8192]{2,1,0:T(8,128)(2,1)} custom-call(s32[2]{0:T(128)} %pad_add_fusion.ids, bf16[360,1024]{1,0:T(8,128)(2,1)} %get-tuple-element.94.refs_0_, bf16[360,1024]{1,0:T(8,128)(2,1)} %copy-done.6, bf16[360,1024]{1,0:T(8,128)(2,1)} %copy-done.7, ...), custom_call_target="tpu_custom_call", output_to_operand_aliasing={{}: (5, {})} | custom-call | flops 1253376000 | bytes 5898240 | tf_op jit(solution)/shard_map/place_pieces/pallas_call | solution.py:297
  215.2 10.3 %collective-permute-done.33.refs_2_ = bf16[360,1024]{1,0:T(8,128)(2,1)} collective-permute-done((bf16[360,1024]{1,0:T(8,128)(2,1)S(1)}, bf16[360,1024]{1,0:T(8,128)(2,1)}, u32[]{:S(2)}, u32[]{:S(2)}) %collective-permute-start.33) | collective-permute-done | bytes 737312 | tf_op jit(solution)/shard_map/ppermute | solution.py:359
  225.5 14.3 %collective-permute-done.34.refs_3_ = bf16[360,1024]{1,0:T(8,128)(2,1)} collective-permute-done((bf16[360,1024]{1,0:T(8,128)(2,1)}, bf16[360,1024]{1,0:T(8,128)(2,1)}, u32[]{:S(2)}, u32[]{:S(2)}) %collective-permute-start.34) | collective-permute-done | bytes 737312 | tf_op jit(solution)/shard_map/ppermute | solution.py:359
  239.8 5.1 %place_pieces.4.refs_1_ = bf16[4,360,8192]{2,1,0:T(8,128)(2,1)} custom-call(s32[2]{0:T(128)} %pad_add_fusion.ids, bf16[360,1024]{1,0:T(8,128)(2,1)} %get-tuple-element.99.refs_0_, bf16[360,1024]{1,0:T(8,128)(2,1)} %collective-permute-done.32.refs_1_, bf16[360,1024]{1,0:T(8,128)(2,1)} %collective-permute-done.33.refs_2_, ...), custom_call_target="tpu_custom_call", output_to_operand_aliasing={{}: (8, {})} | custom-call | flops 2193408000 | bytes 10321920 | tf_op jit(solution)/shard_map/place_pieces/pallas_call | solution.py:297
  244.9 2.7 %place_pieces.5 = bf16[4,360,8192]{2,1,0:T(8,128)(2,1)} custom-call(s32[2]{0:T(128)} %pad_add_fusion.ids, bf16[360,1024]{1,0:T(8,128)(2,1)} %collective-permute-done.31.refs_0_, bf16[4,360,8192]{2,1,0:T(8,128)(2,1)} %place_pieces.4.refs_1_, bf16[144,1024]{1,0:T(8,128)(2,1)} %reduce_sum.12.refs_5_.refs_8_.refs_2_), custom_call_target="tpu_custom_call", output_to_operand_aliasing={{}: (2, {})} | custom-call | flops 313344000 | bytes 1474560 | tf_op jit(solution)/shard_map/place_pieces/pallas_call | solution.py:297
  (71 shorter events, 2.3 us)
Async XLA Ops:
  4.7 13.3 %collective-permute-start = (bf16[144,1408]{1,0:T(8,128)(2,1)}, bf16[144,1408]{1,0:T(8,128)(2,1)S(1)}, u32[]{:S(2)}, u32[]{:S(2)}) collective-permute-start(bf16[144,1408]{1,0:T(8,128)(2,1)} %get-tuple-element.54), channel_id=1, source_target_pairs={{0,8},{8,0},{16,24},{24,16},{1,9},{9,1},{17,25},{25,17},{2,10},{10... | collective-permute-start | bytes 1216520 | tf_op jit(solution)/shard_map/ppermute | solution.py:359
  5.2 19.7 %collective-permute-start.1 = (bf16[144,1408]{1,0:T(8,128)(2,1)}, bf16[144,1408]{1,0:T(8,128)(2,1)S(1)}, u32[]{:S(2)}, u32[]{:S(2)}) collective-permute-start(bf16[144,1408]{1,0:T(8,128)(2,1)} %get-tuple-element.55), channel_id=1, source_target_pairs={{0,16},{8,24},{16,0},{24,8},{1,17},{9,25},{17,1},{25,9},{2,18},{10... | collective-permute-start | bytes 1216520 | tf_op jit(solution)/shard_map/ppermute | solution.py:359
  5.7 19.2 %collective-permute-start.2 = (bf16[144,1408]{1,0:T(8,128)(2,1)}, bf16[144,1408]{1,0:T(8,128)(2,1)S(1)}, u32[]{:S(2)}, u32[]{:S(2)}) collective-permute-start(bf16[144,1408]{1,0:T(8,128)(2,1)} %get-tuple-element.56), channel_id=1, source_target_pairs={{0,24},{8,16},{16,8},{24,0},{1,25},{9,17},{17,9},{25,1},{2,26},{10... | collective-permute-start | bytes 1216520 | tf_op jit(solution)/shard_map/ppermute | solution.py:359
  18.0 7.0 %copy-start.8 = (bf16[144,1408]{1,0:T(8,128)(2,1)}, bf16[144,1408]{1,0:T(8,128)(2,1)S(1)}, u32[]{:S(2)}) copy-start(bf16[144,1408]{1,0:T(8,128)(2,1)S(1)} %collective-permute-done.refs_1_) | copy-start | bytes 1216516
  24.9 0.8 copy-start.9
  25.7 0.8 copy-start.10
  32.7 22.5 %collective-permute-start.7 = (bf16[576,1024]{1,0:T(8,128)(2,1)}, bf16[576,1024]{1,0:T(8,128)(2,1)S(1)}, u32[]{:S(2)}, u32[]{:S(2)}) collective-permute-start(bf16[576,1024]{1,0:T(8,128)(2,1)} %get-tuple-element.57), channel_id=1, source_target_pairs={{0,1},{1,0},{2,3},{3,2},{4,5},{5,4},{6,7},{7,6},{8,9},{9,8},{10,11... | collective-permute-start | bytes 3538952 | tf_op jit(solution)/shard_map/ppermute | solution.py:362
  32.7 11.2 %collective-permute-start.5 = (bf16[360,512]{1,0:T(8,128)(2,1)}, bf16[360,512]{1,0:T(8,128)(2,1)S(1)}, u32[]{:S(2)}, u32[]{:S(2)}) collective-permute-start(bf16[360,512]{1,0:T(8,128)(2,1)} %get-tuple-element.59.refs_6_), channel_id=1, source_target_pairs={{0,16},{8,24},{16,0},{24,8},{1,17},{9,25},{17,1},{25,9},{2,18},{10... | collective-permute-start | bytes 1105928 | tf_op jit(solution)/shard_map/ppermute | solution.py:359
  33.2 11.1 %collective-permute-start.4 = (bf16[360,512]{1,0:T(8,128)(2,1)}, bf16[360,512]{1,0:T(8,128)(2,1)S(1)}, u32[]{:S(2)}, u32[]{:S(2)}) collective-permute-start(bf16[360,512]{1,0:T(8,128)(2,1)} %get-tuple-element.59.refs_6_), channel_id=1, source_target_pairs={{0,8},{8,0},{16,24},{24,16},{1,9},{9,1},{17,25},{25,17},{2,10},{10... | collective-permute-start | bytes 1105928 | tf_op jit(solution)/shard_map/ppermute | solution.py:359
  34.8 29.1 %collective-permute-start.3 = (bf16[576,1024]{1,0:T(8,128)(2,1)}, bf16[576,1024]{1,0:T(8,128)(2,1)S(1)}, u32[]{:S(2)}, u32[]{:S(2)}) collective-permute-start(bf16[576,1024]{1,0:T(8,128)(2,1)} %get-tuple-element.57), channel_id=1, source_target_pairs={{0,2},{1,3},{2,4},{3,5},{4,6},{5,7},{6,0},{7,1},{8,10},{9,11},{10,... | collective-permute-start | bytes 3538952 | tf_op jit(solution)/shard_map/ppermute | solution.py:366
  42.0 11.7 %collective-permute-start.8 = (bf16[360,512]{1,0:T(8,128)(2,1)}, bf16[360,512]{1,0:T(8,128)(2,1)S(1)}, u32[]{:S(2)}, u32[]{:S(2)}) collective-permute-start(bf16[360,512]{1,0:T(8,128)(2,1)} %get-tuple-element.69.refs_6_), channel_id=1, source_target_pairs={{0,8},{8,0},{16,24},{24,16},{1,9},{9,1},{17,25},{25,17},{2,10},{10... | collective-permute-start | bytes 1105928 | tf_op jit(solution)/shard_map/ppermute | solution.py:359
  43.9 11.3 %copy-start.13 = (bf16[360,512]{1,0:T(8,128)(2,1)}, bf16[360,512]{1,0:T(8,128)(2,1)S(1)}, u32[]{:S(2)}) copy-start(bf16[360,512]{1,0:T(8,128)(2,1)S(1)} %collective-permute-done.5.refs_10_.refs_8_) | copy-start | bytes 1105924
  43.9 19.5 %collective-permute-start.9 = (bf16[360,512]{1,0:T(8,128)(2,1)}, bf16[360,512]{1,0:T(8,128)(2,1)S(1)}, u32[]{:S(2)}, u32[]{:S(2)}) collective-permute-start(bf16[360,512]{1,0:T(8,128)(2,1)} %get-tuple-element.69.refs_6_), channel_id=1, source_target_pairs={{0,16},{8,24},{16,0},{24,8},{1,17},{9,25},{17,1},{25,9},{2,18},{10... | collective-permute-start | bytes 1105928 | tf_op jit(solution)/shard_map/ppermute | solution.py:359
  44.4 10.9 %copy-start.14 = (bf16[360,512]{1,0:T(8,128)(2,1)}, bf16[360,512]{1,0:T(8,128)(2,1)S(1)}, u32[]{:S(2)}) copy-start(bf16[360,512]{1,0:T(8,128)(2,1)S(1)} %collective-permute-done.4.refs_9_.refs_7_) | copy-start | bytes 1105924
  44.4 19.6 %collective-permute-start.6 = (bf16[360,512]{1,0:T(8,128)(2,1)S(1)}, bf16[360,512]{1,0:T(8,128)(2,1)S(1)}, u32[]{:S(2)}, u32[]{:S(2)}) collective-permute-start(bf16[360,512]{1,0:T(8,128)(2,1)S(1)} %collective-permute-done.5.refs_10_.refs_8_), channel_id=1, source_target_pairs={{0,8},{8,0},{16,24},{24,16},{1,9},{9,1},{17,25},{25,17},{2,10},{10... | collective-permute-start | bytes 1105928 | tf_op jit(solution)/shard_map/ppermute | solution.py:359
  53.7 9.1 %copy-start.11 = (bf16[360,512]{1,0:T(8,128)(2,1)}, bf16[360,512]{1,0:T(8,128)(2,1)S(1)}, u32[]{:S(2)}) copy-start(bf16[360,512]{1,0:T(8,128)(2,1)S(1)} %collective-permute-done.8.refs_13_.refs_7_) | copy-start | bytes 1105924
  53.7 20.4 %collective-permute-start.17 = (bf16[360,512]{1,0:T(8,128)(2,1)S(1)}, bf16[360,512]{1,0:T(8,128)(2,1)}, u32[]{:S(2)}, u32[]{:S(2)}) collective-permute-start(bf16[360,512]{1,0:T(8,128)(2,1)S(1)} %collective-permute-done.8.refs_13_.refs_7_), channel_id=1, source_target_pairs={{0,16},{8,24},{16,0},{24,8},{1,17},{9,25},{17,1},{25,9},{2,18},{10... | collective-permute-start | bytes 1105928 | tf_op jit(solution)/shard_map/ppermute | solution.py:359
  55.2 1.0 copy-start.17
  62.8 19.0 %collective-permute-start.13 = (bf16[360,1024]{1,0:T(8,128)(2,1)}, bf16[360,1024]{1,0:T(8,128)(2,1)S(1)}, u32[]{:S(2)}, u32[]{:S(2)}) collective-permute-start(bf16[360,1024]{1,0:T(8,128)(2,1)} %get-tuple-element.71.refs_6_), channel_id=1, source_target_pairs={{0,8},{8,0},{16,24},{24,16},{1,9},{9,1},{17,25},{25,17},{2,10},{10... | collective-permute-start | bytes 2211848 | tf_op jit(solution)/shard_map/ppermute | solution.py:359
  63.4 0.7 copy-start.12
  63.4 18.4 %collective-permute-start.14 = (bf16[360,1024]{1,0:T(8,128)(2,1)}, bf16[360,1024]{1,0:T(8,128)(2,1)S(1)}, u32[]{:S(2)}, u32[]{:S(2)}) collective-permute-start(bf16[360,1024]{1,0:T(8,128)(2,1)} %get-tuple-element.71.refs_6_), channel_id=1, source_target_pairs={{0,16},{8,24},{16,0},{24,8},{1,17},{9,25},{17,1},{25,9},{2,18},{10... | collective-permute-start | bytes 2211848 | tf_op jit(solution)/shard_map/ppermute | solution.py:359
  63.9 1.1 copy-start.15
  63.9 33.7 %collective-permute-start.16 = (bf16[576,1024]{1,0:T(8,128)(2,1)S(1)}, bf16[576,1024]{1,0:T(8,128)(2,1)S(1)}, u32[]{:S(2)}, u32[]{:S(2)}) collective-permute-start(bf16[576,1024]{1,0:T(8,128)(2,1)S(1)} %collective-permute-done.3.refs_0_), channel_id=1, source_target_pairs={{0,1},{1,0},{2,3},{3,2},{4,5},{5,4},{6,7},{7,6},{8,9},{9,8},{10,11... | collective-permute-start | bytes 3538952 | tf_op jit(solution)/shard_map/ppermute | solution.py:362
  63.9 1.1 copy-start.20
  72.5 9.3 %copy-start.18 = (bf16[360,1024]{1,0:T(8,128)(2,1)S(1)}, bf16[360,1024]{1,0:T(8,128)(2,1)}, u32[]{:S(2)}) copy-start(bf16[360,1024]{1,0:T(8,128)(2,1)} %get-tuple-element.70.rest_0_.refs_6_) | copy-start | bytes 2211844
  72.5 25.1 %collective-permute-start.18 = (bf16[360,1024]{1,0:T(8,128)(2,1)}, bf16[360,1024]{1,0:T(8,128)(2,1)S(1)}, u32[]{:S(2)}, u32[]{:S(2)}) collective-permute-start(bf16[360,1024]{1,0:T(8,128)(2,1)} %get-tuple-element.70.rest_0_.refs_6_), channel_id=1, source_target_pairs={{0,8},{8,0},{16,24},{24,16},{1,9},{9,1},{17,25},{25,17},{2,10},{10... | collective-permute-start | bytes 2211848 | tf_op jit(solution)/shard_map/ppermute | solution.py:359
  74.1 35.3 %collective-permute-start.10 = (bf16[576,1024]{1,0:T(8,128)(2,1)}, bf16[576,1024]{1,0:T(8,128)(2,1)}, u32[]{:S(2)}, u32[]{:S(2)}) collective-permute-start(bf16[576,1024]{1,0:T(8,128)(2,1)} %copy-done.15), channel_id=1, source_target_pairs={{0,2},{1,3},{2,4},{3,5},{4,6},{5,7},{6,0},{7,1},{8,10},{9,11},{10,... | collective-permute-start | bytes 3538952 | tf_op jit(solution)/shard_map/ppermute | solution.py:366
  81.8 15.8 %copy-start.2 = (bf16[360,1024]{1,0:T(8,128)(2,1)}, bf16[360,1024]{1,0:T(8,128)(2,1)S(1)}, u32[]{:S(2)}) copy-start(bf16[360,1024]{1,0:T(8,128)(2,1)S(1)} %collective-permute-done.13.refs_15_.refs_7_) | copy-start | bytes 2211844
  81.8 25.8 %collective-permute-start.19 = (bf16[360,1024]{1,0:T(8,128)(2,1)S(1)}, bf16[360,1024]{1,0:T(8,128)(2,1)S(1)}, u32[]{:S(2)}, u32[]{:S(2)}) collective-permute-start(bf16[360,1024]{1,0:T(8,128)(2,1)S(1)} %copy-done.18), channel_id=1, source_target_pairs={{0,16},{8,24},{16,0},{24,8},{1,17},{9,25},{17,1},{25,9},{2,18},{10... | collective-permute-start | bytes 2211848 | tf_op jit(solution)/shard_map/ppermute | solution.py:359
  81.9 15.8 %copy-start.3 = (bf16[360,1024]{1,0:T(8,128)(2,1)}, bf16[360,1024]{1,0:T(8,128)(2,1)S(1)}, u32[]{:S(2)}) copy-start(bf16[360,1024]{1,0:T(8,128)(2,1)S(1)} %collective-permute-done.14.refs_16_.refs_8_) | copy-start | bytes 2211844
  81.9 31.7 %collective-permute-start.15 = (bf16[360,1024]{1,0:T(8,128)(2,1)S(1)}, bf16[360,1024]{1,0:T(8,128)(2,1)}, u32[]{:S(2)}, u32[]{:S(2)}) collective-permute-start(bf16[360,1024]{1,0:T(8,128)(2,1)S(1)} %collective-permute-done.14.refs_16_.refs_8_), channel_id=1, source_target_pairs={{0,8},{8,0},{16,24},{24,16},{1,9},{9,1},{17,25},{25,17},{2,10},{10... | collective-permute-start | bytes 2211848 | tf_op jit(solution)/shard_map/ppermute | solution.py:359
  97.6 8.5 %copy-start = (bf16[360,1024]{1,0:T(8,128)(2,1)}, bf16[360,1024]{1,0:T(8,128)(2,1)S(1)}, u32[]{:S(2)}) copy-start(bf16[360,1024]{1,0:T(8,128)(2,1)S(1)} %collective-permute-done.18.refs_14_.refs_7_) | copy-start | bytes 2211844
  97.6 25.2 %collective-permute-start.27 = (bf16[360,1024]{1,0:T(8,128)(2,1)S(1)}, bf16[360,1024]{1,0:T(8,128)(2,1)}, u32[]{:S(2)}, u32[]{:S(2)}) collective-permute-start(bf16[360,1024]{1,0:T(8,128)(2,1)S(1)} %collective-permute-done.18.refs_14_.refs_7_), channel_id=1, source_target_pairs={{0,16},{8,24},{16,0},{24,8},{1,17},{9,25},{17,1},{25,9},{2,18},{10... | collective-permute-start | bytes 2211848 | tf_op jit(solution)/shard_map/ppermute | solution.py:359
  97.7 1.1 copy-start.16
  106.2 23.2 %collective-permute-start.23 = (bf16[360,1024]{1,0:T(8,128)(2,1)}, bf16[360,1024]{1,0:T(8,128)(2,1)}, u32[]{:S(2)}, u32[]{:S(2)}) collective-permute-start(bf16[360,1024]{1,0:T(8,128)(2,1)} %get-tuple-element.81.refs_6_), channel_id=1, source_target_pairs={{0,8},{8,0},{16,24},{24,16},{1,9},{9,1},{17,25},{25,17},{2,10},{10... | collective-permute-start | bytes 2211848 | tf_op jit(solution)/shard_map/ppermute | solution.py:359
  107.7 7.2 %copy-start.1 = (bf16[360,1024]{1,0:T(8,128)(2,1)}, bf16[360,1024]{1,0:T(8,128)(2,1)S(1)}, u32[]{:S(2)}) copy-start(bf16[360,1024]{1,0:T(8,128)(2,1)S(1)} %collective-permute-done.19.refs_15_.refs_8_) | copy-start | bytes 2211844
  107.7 21.7 %collective-permute-start.24 = (bf16[360,1024]{1,0:T(8,128)(2,1)}, bf16[360,1024]{1,0:T(8,128)(2,1)}, u32[]{:S(2)}, u32[]{:S(2)}) collective-permute-start(bf16[360,1024]{1,0:T(8,128)(2,1)} %get-tuple-element.81.refs_6_), channel_id=1, source_target_pairs={{0,16},{8,24},{16,0},{24,8},{1,17},{9,25},{17,1},{25,9},{2,18},{10... | collective-permute-start | bytes 2211848 | tf_op jit(solution)/shard_map/ppermute | solution.py:359
  109.4 42.8 %collective-permute-start.26 = (bf16[576,1024]{1,0:T(8,128)(2,1)}, bf16[576,1024]{1,0:T(8,128)(2,1)}, u32[]{:S(2)}, u32[]{:S(2)}) collective-permute-start(bf16[576,1024]{1,0:T(8,128)(2,1)} %collective-permute-done.10.refs_0_), channel_id=1, source_target_pairs={{0,1},{1,0},{2,3},{3,2},{4,5},{5,4},{6,7},{7,6},{8,9},{9,8},{10,11... | collective-permute-start | bytes 3538952 | tf_op jit(solution)/shard_map/ppermute | solution.py:362
  113.5 38.7 %collective-permute-start.11 = (bf16[576,1024]{1,0:T(8,128)(2,1)}, bf16[576,1024]{1,0:T(8,128)(2,1)}, u32[]{:S(2)}, u32[]{:S(2)}) collective-permute-start(bf16[576,1024]{1,0:T(8,128)(2,1)} %collective-permute-done.10.refs_0_), channel_id=1, source_target_pairs={{0,2},{1,3},{2,4},{3,5},{4,6},{5,7},{6,0},{7,1},{8,10},{9,11},{10,... | collective-permute-start | bytes 3538952 | tf_op jit(solution)/shard_map/ppermute | solution.py:366
  122.8 22.2 %collective-permute-start.20 = (bf16[360,1024]{1,0:T(8,128)(2,1)}, bf16[360,1024]{1,0:T(8,128)(2,1)S(1)}, u32[]{:S(2)}, u32[]{:S(2)}) collective-permute-start(bf16[360,1024]{1,0:T(8,128)(2,1)} %get-tuple-element.80.refs_6_), channel_id=1, source_target_pairs={{0,8},{8,0},{16,24},{24,16},{1,9},{9,1},{17,25},{25,17},{2,10},{10... | collective-permute-start | bytes 2211848 | tf_op jit(solution)/shard_map/ppermute | solution.py:359
  124.4 86.2 %all-to-all-start = ((bf16[8,144,1024]{2,1,0:T(8,128)(2,1)}), bf16[8,144,1024]{2,1,0:T(8,128)(2,1)S(1)}, u32[]{:S(2)}, u32[]{:S(2)}) async-start(bf16[8,144,1024]{2,1,0:T(8,128)(2,1)} %input_product.3.refs_14_), calls=%async_computation | async-start | bytes 4718592 | tf_op jit(solution)/shard_map/all_to_all | solution.py:427
  129.3 32.8 %collective-permute-start.21 = (bf16[360,1024]{1,0:T(8,128)(2,1)}, bf16[360,1024]{1,0:T(8,128)(2,1)S(1)}, u32[]{:S(2)}, u32[]{:S(2)}) collective-permute-start(bf16[360,1024]{1,0:T(8,128)(2,1)} %get-tuple-element.80.refs_6_), channel_id=1, source_target_pairs={{0,16},{8,24},{16,0},{24,8},{1,17},{9,25},{17,1},{25,9},{2,18},{10... | collective-permute-start | bytes 2211848 | tf_op jit(solution)/shard_map/ppermute | solution.py:359
  129.4 33.5 %collective-permute-start.25 = (bf16[360,1024]{1,0:T(8,128)(2,1)}, bf16[360,1024]{1,0:T(8,128)(2,1)}, u32[]{:S(2)}, u32[]{:S(2)}) collective-permute-start(bf16[360,1024]{1,0:T(8,128)(2,1)} %collective-permute-done.24.refs_15_.refs_8_), channel_id=1, source_target_pairs={{0,8},{8,0},{16,24},{24,16},{1,9},{9,1},{17,25},{25,17},{2,10},{10... | collective-permute-start | bytes 2211848 | tf_op jit(solution)/shard_map/ppermute | solution.py:359
  145.0 15.1 %copy-start.4 = (bf16[360,1024]{1,0:T(8,128)(2,1)}, bf16[360,1024]{1,0:T(8,128)(2,1)S(1)}, u32[]{:S(2)}) copy-start(bf16[360,1024]{1,0:T(8,128)(2,1)S(1)} %collective-permute-done.20.refs_14_.refs_7_) | copy-start | bytes 2211844
  145.0 26.1 %collective-permute-start.22 = (bf16[360,1024]{1,0:T(8,128)(2,1)S(1)}, bf16[360,1024]{1,0:T(8,128)(2,1)}, u32[]{:S(2)}, u32[]{:S(2)}) collective-permute-start(bf16[360,1024]{1,0:T(8,128)(2,1)S(1)} %collective-permute-done.20.refs_14_.refs_7_), channel_id=1, source_target_pairs={{0,16},{8,24},{16,0},{24,8},{1,17},{9,25},{17,1},{25,9},{2,18},{10... | collective-permute-start | bytes 2211848 | tf_op jit(solution)/shard_map/ppermute | solution.py:359
  152.3 28.7 %collective-permute-start.12 = (bf16[576,1024]{1,0:T(8,128)(2,1)}, bf16[576,1024]{1,0:T(8,128)(2,1)}, u32[]{:S(2)}, u32[]{:S(2)}) collective-permute-start(bf16[576,1024]{1,0:T(8,128)(2,1)} %collective-permute-done.11.refs_0_), channel_id=1, source_target_pairs={{0,1},{1,0},{2,3},{3,2},{4,5},{5,4},{6,7},{7,6},{8,9},{9,8},{10,11... | collective-permute-start | bytes 3538952 | tf_op jit(solution)/shard_map/ppermute | solution.py:362
  160.2 19.6 %collective-permute-start.28 = (bf16[360,1024]{1,0:T(8,128)(2,1)}, bf16[360,1024]{1,0:T(8,128)(2,1)S(1)}, u32[]{:S(2)}, u32[]{:S(2)}) collective-permute-start(bf16[360,1024]{1,0:T(8,128)(2,1)} %get-tuple-element.94.refs_0_), channel_id=1, source_target_pairs={{0,8},{8,0},{16,24},{24,16},{1,9},{9,1},{17,25},{25,17},{2,10},{10... | collective-permute-start | bytes 2211848 | tf_op jit(solution)/shard_map/ppermute | solution.py:359
  162.1 0.9 copy-start.5
  162.1 18.8 %collective-permute-start.29 = (bf16[360,1024]{1,0:T(8,128)(2,1)}, bf16[360,1024]{1,0:T(8,128)(2,1)S(1)}, u32[]{:S(2)}, u32[]{:S(2)}) collective-permute-start(bf16[360,1024]{1,0:T(8,128)(2,1)} %get-tuple-element.94.refs_0_), channel_id=1, source_target_pairs={{0,16},{8,24},{16,0},{24,8},{1,17},{9,25},{17,1},{25,9},{2,18},{10... | collective-permute-start | bytes 2211848 | tf_op jit(solution)/shard_map/ppermute | solution.py:359
  170.9 24.8 %collective-permute-start.32 = (bf16[360,1024]{1,0:T(8,128)(2,1)}, bf16[360,1024]{1,0:T(8,128)(2,1)}, u32[]{:S(2)}, u32[]{:S(2)}) collective-permute-start(bf16[360,1024]{1,0:T(8,128)(2,1)} %get-tuple-element.99.refs_0_), channel_id=1, source_target_pairs={{0,8},{8,0},{16,24},{24,16},{1,9},{9,1},{17,25},{25,17},{2,10},{10... | collective-permute-start | bytes 2211848 | tf_op jit(solution)/shard_map/ppermute | solution.py:359
  179.8 1.2 copy-start.6
  181.0 0.9 copy-start.7
  181.9 9.7 %copy-start.19 = (bf16[360,1024]{1,0:T(8,128)(2,1)S(1)}, bf16[360,1024]{1,0:T(8,128)(2,1)}, u32[]{:S(2)}) copy-start(bf16[360,1024]{1,0:T(8,128)(2,1)} %get-tuple-element.99.refs_0_) | copy-start | bytes 2211844
  189.9 19.8 %collective-permute-start.30 = (bf16[360,1024]{1,0:T(8,128)(2,1)}, bf16[360,1024]{1,0:T(8,128)(2,1)}, u32[]{:S(2)}, u32[]{:S(2)}) collective-permute-start(bf16[360,1024]{1,0:T(8,128)(2,1)} %get-tuple-element.98.refs_4_), channel_id=1, source_target_pairs={{0,16},{8,24},{16,0},{24,8},{1,17},{9,25},{17,1},{25,9},{2,18},{10... | collective-permute-start | bytes 2211848 | tf_op jit(solution)/shard_map/ppermute | solution.py:359
  190.7 21.1 %collective-permute-start.36 = (bf16[360,1024]{1,0:T(8,128)(2,1)}, bf16[360,1024]{1,0:T(8,128)(2,1)}, u32[]{:S(2)}, u32[]{:S(2)}) collective-permute-start(bf16[360,1024]{1,0:T(8,128)(2,1)} %copy-done.7), channel_id=1, source_target_pairs={{0,8},{8,0},{16,24},{24,16},{1,9},{9,1},{17,25},{25,17},{2,10},{10... | collective-permute-start | bytes 2211848 | tf_op jit(solution)/shard_map/ppermute | solution.py:359
  191.5 34.0 %collective-permute-start.33 = (bf16[360,1024]{1,0:T(8,128)(2,1)S(1)}, bf16[360,1024]{1,0:T(8,128)(2,1)}, u32[]{:S(2)}, u32[]{:S(2)}) collective-permute-start(bf16[360,1024]{1,0:T(8,128)(2,1)S(1)} %copy-done.19), channel_id=1, source_target_pairs={{0,16},{8,24},{16,0},{24,8},{1,17},{9,25},{17,1},{25,9},{2,18},{10... | collective-permute-start | bytes 2211848 | tf_op jit(solution)/shard_map/ppermute | solution.py:359
  195.7 44.1 %collective-permute-start.34 = (bf16[360,1024]{1,0:T(8,128)(2,1)}, bf16[360,1024]{1,0:T(8,128)(2,1)}, u32[]{:S(2)}, u32[]{:S(2)}) collective-permute-start(bf16[360,1024]{1,0:T(8,128)(2,1)} %collective-permute-done.32.refs_1_), channel_id=1, source_target_pairs={{0,16},{8,24},{16,0},{24,8},{1,17},{9,25},{17,1},{25,9},{2,18},{10... | collective-permute-start | bytes 2211848 | tf_op jit(solution)/shard_map/ppermute | solution.py:359
  196.3 43.5 %collective-permute-start.35 = (bf16[360,1024]{1,0:T(8,128)(2,1)}, bf16[360,1024]{1,0:T(8,128)(2,1)}, u32[]{:S(2)}, u32[]{:S(2)}) collective-permute-start(bf16[360,1024]{1,0:T(8,128)(2,1)} %get-tuple-element.98.refs_4_), channel_id=1, source_target_pairs={{0,8},{8,0},{16,24},{24,16},{1,9},{9,1},{17,25},{25,17},{2,10},{10... | collective-permute-start | bytes 2211848 | tf_op jit(solution)/shard_map/ppermute | solution.py:359
  209.7 35.2 %collective-permute-start.31 = (bf16[360,1024]{1,0:T(8,128)(2,1)}, bf16[360,1024]{1,0:T(8,128)(2,1)}, u32[]{:S(2)}, u32[]{:S(2)}) collective-permute-start(bf16[360,1024]{1,0:T(8,128)(2,1)} %collective-permute-done.30.refs_6_), channel_id=1, source_target_pairs={{0,8},{8,0},{16,24},{24,16},{1,9},{9,1},{17,25},{25,17},{2,10},{10... | collective-permute-start | bytes 2211848 | tf_op jit(solution)/shard_map/ppermute | solution.py:359

commit v3 on v2

--- a/solution.py
+++ b/solution.py
@@ -25,13 +25,16 @@
 LAST_CUTS = (4,)
 UNPACK_AT = 0
 GATE = 2
-FORWARD_BY_X = (1,0,1,0,1,0,1,0,1,0,1,0)
+FORWARD_BY_X = (0, 1, 0, 1, 0, 1, 0, 1, 0, 1, 0, 1)
 LAST_MORE = 0
-TAIL_SPLIT = 2
+TAIL = 2
+GATE_MASKS = (2,)
+Y_FIRST = 0
+SPLIT_LAST = 0
 STEP_COST = 8000000
 PLACE_COST = 850
 PRODUCT_COST = 6000000
-VMEM_LIMIT = 58 * 1024 * 1024
+VMEM_LIMIT = 63 * 1024 * 1024
 ANY = pl.BlockSpec(memory_space=pl.ANY)
 PARAMS = pltpu.CompilerParams(vmem_limit_bytes=VMEM_LIMIT)
 
@@ -390,10 +393,12 @@
                 count = len(sent)
                 where = (n_tensor, step, side, offset)
                 until = max(count - LAG + 1, 0) + (LAST_MORE if count == n_cuts - 1 else 0)
-                groups, placed = [(w, masks, p) for p, w in sent[placed:until]], max(until, placed)
+                groups, placed = sum(sent[placed:until], []), max(until, placed)
                 early = count < len(FIRST_CUTS)
                 unpack = count == UNPACK_AT
-                gate = tuple(sent[count - GATE][0][1:3]) if 0 < GATE <= count else ()
+                gate = ()
+                if 0 < GATE <= count:
+                    gate = tuple(sent[count - GATE][0][2][m] for m in GATE_MASKS)
                 results = optimizer_step(
                     inverse,
                     shard_units if early else None,
@@ -415,9 +420,23 @@
                 if unpack:
                     acts, grads = results[-2:]
                 unread = ()
-                by_x, by_y = swap(piece, 1), swap(piece, 2)
-                by_both = swap(by_y, 1) if FORWARD_BY_X[count] else swap(by_x, 2)
-                sent.append(((piece, by_x, by_y, by_both), where))
+                if Y_FIRST:
+                    by_y, by_x = swap(piece, 2), swap(piece, 1)
+                else:
+                    by_x, by_y = swap(piece, 1), swap(piece, 2)
+                if count < n_cuts - SPLIT_LAST:
+                    by_both = swap(by_y, 1) if FORWARD_BY_X[count] else swap(by_x, 2)
+                    sent.append([(where, masks, (piece, by_x, by_y, by_both))])
+                else:
+                    half = cut // 2
+                    middle = where[:3] + (offset + half,)
+                    sent.append(
+                        [
+                            (where, masks[:3], (piece, by_x, by_y)),
+                            (where, masks[3:], (swap(by_x[:, :half], 2),)),
+                            (middle, masks[3:], (swap(by_y[:, half:], 1),)),
+                        ]
+                    )
                 if count == PRODUCT_AT:
                     terms = input_product(
                         grads_two, weight, n_tensor, PRODUCT_FIRST, n_tensor, terms, piece
@@ -426,14 +445,15 @@
                 offset += cut
     terms = lax.all_to_all(terms, "tensor", 0, 0)
     d_inputs = jnp.sum(terms.astype(jnp.float32), axis=0).astype(jnp.bfloat16)
-    groups = [(w, masks, p) for p, w in sent[placed:-1]]
-    pieces, where = sent[-1]
-    groups.append((where, masks[:3], pieces[:3]))
-    if TAIL_SPLIT:
-        out = place_pieces(ids, groups[:-TAIL_SPLIT], width, out, d_inputs)
-        groups = groups[-TAIL_SPLIT:]
+    if n_cuts - placed > TAIL:
+        groups = sum(sent[placed : n_cuts - TAIL], [])
+        out = place_pieces(ids, groups, width, out, d_inputs)
+        placed = n_cuts - TAIL
+    where, _, pieces = sent[-1][0]
+    groups = sum(sent[placed:-1], []) + [(where, masks[:3], pieces[:3])]
     out = place_pieces(ids, groups, width, out, d_inputs)
-    out = place_pieces(ids, [(where, masks[3:], pieces[3:])], width, out, d_inputs)
+    groups = sent[-1][1:] if SPLIT_LAST else [(where, masks[3:], pieces[3:])]
+    out = place_pieces(ids, groups, width, out, d_inputs)
     d_inputs = d_inputs.reshape(batches, tok_rows, width)
     ema_copy = out.reshape(n_dp * shard_units, model_width)
 

time: 249 us -> 247 us (level)
  waiting for transfers between devices: 108 us -> 118 us
  starting transfers between devices: 37.4 us -> 29.9 us
  local copies, waits for them, and re-layouts: 5.84 us -> 0.78 us
    ppermute x30, waiting for transfers between devices: 101 us -> 109 us  [swap(): return lax.ppermute(array, 'dp', [(i, i ^ mask) for i in range(n_dp)])]
    ppermute x30, starting transfers between devices: 29.6 us -> 22.1 us  [swap(): return lax.ppermute(array, 'dp', [(i, i ^ mask) for i in range(n_dp)])]
    unnamed x42 -> x14, local copies, waits for them, and re-layouts: 5.84 us -> 0.78 us
  transfers between devices with their start and end apart: 38 -> 38, of which waited for: 15 -> 16; matrix products, arithmetic and copies ran while one was open for 0% -> 1% of each run, Pallas kernels for 33% -> 33%
where the time goes in v3:
time: 247 us
  waiting for transfers between devices  118 us (48%)
  Pallas kernels  93.6 us (38%)
  starting transfers between devices  29.9 us (12%)
  other arithmetic  3.44 us (1%)
    ppermute x30, waiting for transfers between devices, swap(): return lax.ppermute(array, 'dp', [(i, i ^ mask) for i in range(n_dp)])  109 us
    pallas_call x9, Pallas kernels, optimizer_step(): pl.pallas_call(functools.partial(step_kernel, inverse, units, slice_width...  65 us
    ppermute x30, starting transfers between devices, swap(): return lax.ppermute(array, 'dp', [(i, i ^ mask) for i in range(n_dp)])  22.1 us
    pallas_call x2, Pallas kernels, input_product(): pl.pallas_call(product_kernel, out_shape=jax.ShapeDtypeStruct((slices, to...  14 us
    pallas_call x3, Pallas kernels, place_pieces(): pl.pallas_call(functools.partial(place_kernel, slice_width, [group[:2] fo...  11.2 us
    ppermute x3, waiting for transfers between devices, shift_pair(): return lax.ppermute(array, 'tensor', moves)  8.78 us
    all_to_all x1, starting transfers between devices, square_body(): terms = lax.all_to_all(terms, 'tensor', 0, 0)  5.69 us
  transfers between devices with their start and end apart: 38, of which 16 were waited for; matrix products, arithmetic and copies ran while one was open for 1% of the time, Pallas kernels for 33%

profile of v3, /device:TPU:22, one launch (start us, length us, event | category | flops | bytes accessed | tf_op | source)
XLA Modules:
  0.0 246.8 jit_solution(3980414859426999655)
XLA Ops:
  0.6 0.6 pad_add_fusion.ids
  1.2 3.4 %pack_messages.1 = (bf16[144,1408]{1,0:T(8,128)(2,1)}, bf16[144,1408]{1,0:T(8,128)(2,1)}, bf16[144,1408]{1,0:T(8,128)(2,1)}, bf16[144,1408]{1,0:T(8,128)(2,1)}) custom-call(s32[2]{0:T(128)} %pad_add_fusion.ids, bf16[144,8192]{1,0:T(8,128)(2,1)} %bitcast.8, bf16[144,1440]{1,0:T(8,128)(2,1)} %bitcast.9), custom_call_target="tpu_custom_call" | custom-call | bytes 1658880 | tf_op jit(solution)/shard_map/pack_messages/pallas_call | solution.py:79
  4.6 0.5 collective-permute-start
  5.1 0.5 collective-permute-start.1
  5.7 2.4 collective-permute-start.2
  8.1 9.8 %input_product.2.refs_8_.rest_1_ = bf16[8,144,1024]{2,1,0:T(8,128)(2,1)} custom-call(bf16[144,1440]{1,0:T(8,128)(2,1)} %bitcast.10, bf16[1440,8192]{1,0:T(8,128)(2,1)} %weight.3, bf16[144,1408]{1,0:T(8,128)(2,1)} %get-tuple-element.53.rest_0_.refs_0_), custom_call_target="tpu_custom_call" | custom-call | flops 36864000000 | bytes 17694720 | tf_op jit(solution)/shard_map/input_product/pallas_call | solution.py:329
  17.9 7.0 %collective-permute-done.1.refs_2_ = bf16[144,1408]{1,0:T(8,128)(2,1)S(1)} collective-permute-done((bf16[144,1408]{1,0:T(8,128)(2,1)}, bf16[144,1408]{1,0:T(8,128)(2,1)S(1)}, u32[]{:S(2)}, u32[]{:S(2)}) %collective-permute-start.1) | collective-permute-done | bytes 405536 | tf_op jit(solution)/shard_map/ppermute | solution.py:362
  24.9 0.8 copy-done.3
  25.7 6.2 %optimizer_step.9 = (bf16[360,512]{1,0:T(8,128)(2,1)}, f32[360,8192]{1,0:T(8,128)}, f32[360,8192]{1,0:T(8,128)}, f32[360,8192]{1,0:T(8,128)}, bf16[576,1024]{1,0:T(8,128)(2,1)}, /*index=5*/bf16[360,576]{1,0:T(8,128)(2,1)}) custom-call(s32[2]{0:T(128)} %pad_add_fusion.ids, bf16[144,1408]{1,0:T(8,128)(2,1)} %get-tuple-element.53.rest_0_.refs_0_, ...), custom_call_target="tpu_custom_call" | custom-call | flops 4096000000 | bytes 5529600 | tf_op jit(solution)/shard_map/optimizer_step/pallas_call | solution.py:252
  31.9 1.6 collective-permute-start.3
  33.5 0.6 collective-permute-start.5
  34.1 1.4 collective-permute-start.4
  35.5 5.6 %optimizer_step.10 = (bf16[360,512]{1,0:T(8,128)(2,1)}, f32[360,8192]{1,0:T(8,128)}, f32[360,8192]{1,0:T(8,128)}, f32[360,8192]{1,0:T(8,128)}) custom-call(s32[2]{0:T(128)} %pad_add_fusion.ids, bf16[144,1408]{1,0:T(8,128)(2,1)} %get-tuple-element.53.rest_0_.refs_0_, ...), custom_call_target="tpu_custom_call", output_to_operand_aliasing={{1}: (9, {}), {2}: (10, {}), {3}: (11, {})} | custom-call | flops 4096000000 | bytes 5529600 | tf_op jit(solution)/shard_map/optimizer_step/pallas_call | solution.py:252
  41.1 1.5 collective-permute-start.8
  42.6 2.5 %collective-permute-done.5.refs_9_.refs_8_ = bf16[360,512]{1,0:T(8,128)(2,1)S(1)} collective-permute-done((bf16[360,512]{1,0:T(8,128)(2,1)}, bf16[360,512]{1,0:T(8,128)(2,1)S(1)}, u32[]{:S(2)}, u32[]{:S(2)}) %collective-permute-start.5) | collective-permute-done | bytes 368672 | tf_op jit(solution)/shard_map/ppermute | solution.py:362
  45.2 1.5 collective-permute-start.16
  46.6 0.5 collective-permute-start.6
  47.2 6.0 %collective-permute-done.8.refs_13_.refs_8_ = bf16[360,512]{1,0:T(8,128)(2,1)} collective-permute-done((bf16[360,512]{1,0:T(8,128)(2,1)}, bf16[360,512]{1,0:T(8,128)(2,1)}, u32[]{:S(2)}, u32[]{:S(2)}) %collective-permute-start.8) | collective-permute-done | bytes 368672 | tf_op jit(solution)/shard_map/ppermute | solution.py:362
  53.2 1.5 collective-permute-start.17
  54.7 6.6 %optimizer_step.11 = (bf16[360,1024]{1,0:T(8,128)(2,1)}, f32[360,8192]{1,0:T(8,128)}, f32[360,8192]{1,0:T(8,128)}, f32[360,8192]{1,0:T(8,128)}) custom-call(s32[2]{0:T(128)} %pad_add_fusion.ids, bf16[576,1024]{1,0:T(8,128)(2,1)} %collective-permute-done.7.refs_0_, ...), custom_call_target="tpu_custom_call", output_to_operand_aliasing={{1}: (7, {}), {2}: (8, {}), {3}: (9, {})} | custom-call | flops 8192000000 | bytes 11059200 | tf_op jit(solution)/shard_map/optimizer_step/pallas_call | solution.py:252
  61.3 0.6 collective-permute-start.13
  61.8 1.3 collective-permute-start.12
  63.2 7.4 %optimizer_step.12 = (bf16[360,1024]{1,0:T(8,128)(2,1)}, f32[360,8192]{1,0:T(8,128)}, f32[360,8192]{1,0:T(8,128)}, f32[360,8192]{1,0:T(8,128)}, bf16[4,360,8192]{2,1,0:T(8,128)(2,1)}) custom-call(s32[2]{0:T(128)} %pad_add_fusion.ids, bf16[576,1024]{1,0:T(8,128)(2,1)} %collective-permute-done.3.refs_0_, ...), custom_call_target="tpu_custom_call", output_to_operand_aliasing={{1}: (11, {}), {2}: (12, {}), {3}: (13, {})} | custom-call | flops 8192000000 | bytes 14008320 | tf_op jit(solution)/shard_map/optimizer_step/pallas_call | solution.py:252
  70.6 0.8 collective-permute-start.18
  71.4 0.2 collective-permute-start.9
  71.6 4.2 %input_product.3.refs_14_ = bf16[8,144,1024]{2,1,0:T(8,128)(2,1)} custom-call(bf16[144,1440]{1,0:T(8,128)(2,1)} %bitcast.11, bf16[1440,8192]{1,0:T(8,128)(2,1)} %weight.3, bf16[360,1024]{1,0:T(8,128)(2,1)} %get-tuple-element.70.rest_0_.refs_6_, bf16[8,144,1024]{2,1,0:T(8,128)(2,1)} %input_product.2.refs_8_.rest_1_), custom_call_target="tpu_custom_call", output_to_operand_aliasing={{}: (3, {})} | custom-call | flops 12288000000 | bytes 5898240 | tf_op jit(solution)/shard_map/input_product/pallas_call | solution.py:329
  75.8 5.2 %collective-permute-done.13.refs_15_.refs_8_ = bf16[360,1024]{1,0:T(8,128)(2,1)} collective-permute-done((bf16[360,1024]{1,0:T(8,128)(2,1)}, bf16[360,1024]{1,0:T(8,128)(2,1)}, u32[]{:S(2)}, u32[]{:S(2)}) %collective-permute-start.13) | collective-permute-done | bytes 737312 | tf_op jit(solution)/shard_map/ppermute | solution.py:362
  81.1 0.5 collective-permute-start.26
  81.6 0.4 collective-permute-start.14
  82.0 14.8 %collective-permute-done.18.refs_14_.refs_8_ = bf16[360,1024]{1,0:T(8,128)(2,1)S(1)} collective-permute-done((bf16[360,1024]{1,0:T(8,128)(2,1)}, bf16[360,1024]{1,0:T(8,128)(2,1)S(1)}, u32[]{:S(2)}, u32[]{:S(2)}) %collective-permute-start.18) | collective-permute-done | bytes 737312 | tf_op jit(solution)/shard_map/ppermute | solution.py:362
  96.8 0.5 collective-permute-start.27
  97.3 7.4 %optimizer_step.13 = (bf16[360,1024]{1,0:T(8,128)(2,1)}, f32[360,8192]{1,0:T(8,128)}, f32[360,8192]{1,0:T(8,128)}, f32[360,8192]{1,0:T(8,128)}, bf16[4,360,8192]{2,1,0:T(8,128)(2,1)}) custom-call(s32[2]{0:T(128)} %pad_add_fusion.ids, ...), custom_call_target="tpu_custom_call", output_to_operand_aliasing={{1}: (11, {}), {2}: (12, {}), {3}: (13, {}), {4}: (14, {})} | custom-call | flops 8192000000 | bytes 14008320 | tf_op jit(solution)/shard_map/optimizer_step/pallas_call | solution.py:252
  104.7 0.4 collective-permute-start.23
  105.2 7.5 %collective-permute-done.14.refs_9_ = bf16[360,1024]{1,0:T(8,128)(2,1)} collective-permute-done((bf16[360,1024]{1,0:T(8,128)(2,1)}, bf16[360,1024]{1,0:T(8,128)(2,1)}, u32[]{:S(2)}, u32[]{:S(2)}) %collective-permute-start.14) | collective-permute-done | bytes 737312 | tf_op jit(solution)/shard_map/ppermute | solution.py:362
  112.7 0.2 collective-permute-start.10
  112.9 7.9 %optimizer_step.14 = (bf16[360,1024]{1,0:T(8,128)(2,1)}, f32[360,8192]{1,0:T(8,128)}, f32[360,8192]{1,0:T(8,128)}, f32[360,8192]{1,0:T(8,128)}, bf16[4,360,8192]{2,1,0:T(8,128)(2,1)}) custom-call(s32[2]{0:T(128)} %pad_add_fusion.ids, ...), custom_call_target="tpu_custom_call", output_to_operand_aliasing={{1}: (11, {}), {2}: (12, {}), {3}: (13, {}), {4}: (14, {})} | custom-call | flops 8192000000 | bytes 16957440 | tf_op jit(solution)/shard_map/optimizer_step/pallas_call | solution.py:252
  120.8 0.6 collective-permute-start.22
  121.4 0.6 collective-permute-start.20
  122.0 5.7 %all-to-all-start = ((bf16[8,144,1024]{2,1,0:T(8,128)(2,1)}), bf16[8,144,1024]{2,1,0:T(8,128)(2,1)}, u32[]{:S(2)}, u32[]{:S(2)}) async-start(bf16[8,144,1024]{2,1,0:T(8,128)(2,1)} %input_product.3.refs_14_), calls=%async_computation | async-start | bytes 4718592 | tf_op jit(solution)/shard_map/all_to_all | solution.py:446
  127.7 0.8 collective-permute-done.23.refs_14_.refs_8_
  128.5 0.9 collective-permute-start.19
  129.4 8.2 %collective-permute-done.22.refs_7_ = bf16[360,1024]{1,0:T(8,128)(2,1)} collective-permute-done((bf16[360,1024]{1,0:T(8,128)(2,1)}, bf16[360,1024]{1,0:T(8,128)(2,1)}, u32[]{:S(2)}, u32[]{:S(2)}) %collective-permute-start.22) | collective-permute-done | bytes 737312 | tf_op jit(solution)/shard_map/ppermute | solution.py:362
  137.6 6.6 %collective-permute-done.20.refs_14_.refs_8_ = bf16[360,1024]{1,0:T(8,128)(2,1)S(1)} collective-permute-done((bf16[360,1024]{1,0:T(8,128)(2,1)}, bf16[360,1024]{1,0:T(8,128)(2,1)S(1)}, u32[]{:S(2)}, u32[]{:S(2)}) %collective-permute-start.20) | collective-permute-done | bytes 737312 | tf_op jit(solution)/shard_map/ppermute | solution.py:362
  144.2 0.5 collective-permute-start.21
  144.7 8.8 %collective-permute-done.10.refs_0_ = bf16[576,1024]{1,0:T(8,128)(2,1)} collective-permute-done((bf16[576,1024]{1,0:T(8,128)(2,1)}, bf16[576,1024]{1,0:T(8,128)(2,1)}, u32[]{:S(2)}, u32[]{:S(2)}) %collective-permute-start.10) | collective-permute-done | bytes 1179680 | tf_op jit(solution)/shard_map/ppermute | solution.py:369
  153.5 7.9 %optimizer_step.15 = (bf16[360,1024]{1,0:T(8,128)(2,1)}, f32[360,8192]{1,0:T(8,128)}, f32[360,8192]{1,0:T(8,128)}, f32[360,8192]{1,0:T(8,128)}, bf16[4,360,8192]{2,1,0:T(8,128)(2,1)}) custom-call(s32[2]{0:T(128)} %pad_add_fusion.ids, ...), custom_call_target="tpu_custom_call", output_to_operand_aliasing={{1}: (11, {}), {2}: (12, {}), {3}: (13, {}), {4}: (14, {})} | custom-call | flops 8192000000 | bytes 16957440 | tf_op jit(solution)/shard_map/optimizer_step/pallas_call | solution.py:252
  161.4 0.1 collective-permute-start.28
  161.6 7.9 %optimizer_step.16 = (bf16[360,1024]{1,0:T(8,128)(2,1)}, f32[360,8192]{1,0:T(8,128)}, f32[360,8192]{1,0:T(8,128)}, f32[360,8192]{1,0:T(8,128)}, bf16[4,360,8192]{2,1,0:T(8,128)(2,1)}) custom-call(s32[2]{0:T(128)} %pad_add_fusion.ids, ...), custom_call_target="tpu_custom_call", output_to_operand_aliasing={{1}: (11, {}), {2}: (12, {}), {3}: (13, {}), {4}: (14, {})} | custom-call | flops 8192000000 | bytes 16957440 | tf_op jit(solution)/shard_map/optimizer_step/pallas_call | solution.py:252
  169.5 2.0 collective-permute-start.32
  171.5 9.6 %collective-permute-done.28.refs_14_.refs_2_ = bf16[360,1024]{1,0:T(8,128)(2,1)} collective-permute-done((bf16[360,1024]{1,0:T(8,128)(2,1)}, bf16[360,1024]{1,0:T(8,128)(2,1)}, u32[]{:S(2)}, u32[]{:S(2)}) %collective-permute-start.28) | collective-permute-done | bytes 737312 | tf_op jit(solution)/shard_map/ppermute | solution.py:362
  181.1 8.0 %optimizer_step.17 = (bf16[360,1024]{1,0:T(8,128)(2,1)}, f32[360,8192]{1,0:T(8,128)}, f32[360,8192]{1,0:T(8,128)}, f32[360,8192]{1,0:T(8,128)}, bf16[4,360,8192]{2,1,0:T(8,128)(2,1)}) custom-call(s32[2]{0:T(128)} %pad_add_fusion.ids, ...), custom_call_target="tpu_custom_call", output_to_operand_aliasing={{1}: (11, {}), {2}: (12, {}), {3}: (13, {}), {4}: (14, {})} | custom-call | flops 8192000000 | bytes 16957440 | tf_op jit(solution)/shard_map/optimizer_step/pallas_call | solution.py:252
  189.1 0.1 collective-permute-start.29
  189.2 0.1 collective-permute-start.36
  189.4 1.9 collective-permute-start.31
  191.3 5.6 %collective-permute-done.32.refs_2_ = bf16[360,1024]{1,0:T(8,128)(2,1)} collective-permute-done((bf16[360,1024]{1,0:T(8,128)(2,1)}, bf16[360,1024]{1,0:T(8,128)(2,1)}, u32[]{:S(2)}, u32[]{:S(2)}) %collective-permute-start.32) | collective-permute-done | bytes 737312 | tf_op jit(solution)/shard_map/ppermute | solution.py:362
  196.9 0.1 collective-permute-start.34
  197.0 12.0 %collective-permute-done.29.refs_5_ = bf16[360,1024]{1,0:T(8,128)(2,1)} collective-permute-done((bf16[360,1024]{1,0:T(8,128)(2,1)}, bf16[360,1024]{1,0:T(8,128)(2,1)}, u32[]{:S(2)}, u32[]{:S(2)}) %collective-permute-start.29) | collective-permute-done | bytes 737312 | tf_op jit(solution)/shard_map/ppermute | solution.py:362
  209.0 2.9 %reduce_sum.12.refs_5_.refs_8_.refs_2_ = bf16[144,1024]{1,0:T(8,128)(2,1)} reduce(bf16[8,144,1024]{2,1,0:T(8,128)(2,1)} %all-to-all-done, bf16[]{:T(256)} %constant.10.clone.1), dimensions={0}, to_apply=%region_0.0 | reduce | flops 1032192 | bytes 2654210 | tf_op jit(solution)/shard_map/reduce_sum | solution.py:447
  211.9 0.8 collective-permute-done.36.refs_3_
  212.7 3.4 %place_pieces.3.refs_7_ = bf16[4,360,8192]{2,1,0:T(8,128)(2,1)} custom-call(s32[2]{0:T(128)} %pad_add_fusion.ids, bf16[360,1024]{1,0:T(8,128)(2,1)} %get-tuple-element.94.refs_0_, bf16[360,1024]{1,0:T(8,128)(2,1)} %collective-permute-done.35.refs_1_, bf16[360,1024]{1,0:T(8,128)(2,1)} %collective-permute-done.28.refs_14_.refs_2_, ...), custom_call_target="tpu_custom_call", output_to_operand_aliasing={{}: (5, {})} | custom-call | flops 1253376000 | bytes 5898240 | tf_op jit(solution)/shard_map/place_pieces/pallas_call | solution.py:300
  216.1 8.6 %collective-permute-done.31.refs_1_ = bf16[360,1024]{1,0:T(8,128)(2,1)} collective-permute-done((bf16[360,1024]{1,0:T(8,128)(2,1)S(1)}, bf16[360,1024]{1,0:T(8,128)(2,1)}, u32[]{:S(2)}, u32[]{:S(2)}) %collective-permute-start.31) | collective-permute-done | bytes 737312 | tf_op jit(solution)/shard_map/ppermute | solution.py:362
  224.7 14.1 %collective-permute-done.33.refs_3_ = bf16[360,1024]{1,0:T(8,128)(2,1)} collective-permute-done((bf16[360,1024]{1,0:T(8,128)(2,1)}, bf16[360,1024]{1,0:T(8,128)(2,1)}, u32[]{:S(2)}, u32[]{:S(2)}) %collective-permute-start.33) | collective-permute-done | bytes 737312 | tf_op jit(solution)/shard_map/ppermute | solution.py:362
  238.8 5.1 %place_pieces.4.refs_1_ = bf16[4,360,8192]{2,1,0:T(8,128)(2,1)} custom-call(s32[2]{0:T(128)} %pad_add_fusion.ids, bf16[360,1024]{1,0:T(8,128)(2,1)} %get-tuple-element.99.refs_0_, bf16[360,1024]{1,0:T(8,128)(2,1)} %collective-permute-done.31.refs_1_, bf16[360,1024]{1,0:T(8,128)(2,1)} %collective-permute-done.32.refs_2_, ...), custom_call_target="tpu_custom_call", output_to_operand_aliasing={{}: (8, {})} | custom-call | flops 2193408000 | bytes 10321920 | tf_op jit(solution)/shard_map/place_pieces/pallas_call | solution.py:300
  243.9 2.7 %place_pieces.5 = bf16[4,360,8192]{2,1,0:T(8,128)(2,1)} custom-call(s32[2]{0:T(128)} %pad_add_fusion.ids, bf16[360,1024]{1,0:T(8,128)(2,1)} %collective-permute-done.30.refs_0_, bf16[4,360,8192]{2,1,0:T(8,128)(2,1)} %place_pieces.4.refs_1_, bf16[144,1024]{1,0:T(8,128)(2,1)} %reduce_sum.12.refs_5_.refs_8_.refs_2_), custom_call_target="tpu_custom_call", output_to_operand_aliasing={{}: (2, {})} | custom-call | flops 313344000 | bytes 1474560 | tf_op jit(solution)/shard_map/place_pieces/pallas_call | solution.py:300
  (43 shorter events, 0.2 us)
Async XLA Ops:
  4.6 13.3 %collective-permute-start = (bf16[144,1408]{1,0:T(8,128)(2,1)}, bf16[144,1408]{1,0:T(8,128)(2,1)S(1)}, u32[]{:S(2)}, u32[]{:S(2)}) collective-permute-start(bf16[144,1408]{1,0:T(8,128)(2,1)} %get-tuple-element.54), channel_id=1, source_target_pairs={{0,8},{8,0},{16,24},{24,16},{1,9},{9,1},{17,25},{25,17},{2,10},{10... | collective-permute-start | bytes 1216520 | tf_op jit(solution)/shard_map/ppermute | solution.py:362
  5.1 19.7 %collective-permute-start.1 = (bf16[144,1408]{1,0:T(8,128)(2,1)}, bf16[144,1408]{1,0:T(8,128)(2,1)S(1)}, u32[]{:S(2)}, u32[]{:S(2)}) collective-permute-start(bf16[144,1408]{1,0:T(8,128)(2,1)} %get-tuple-element.55), channel_id=1, source_target_pairs={{0,16},{8,24},{16,0},{24,8},{1,17},{9,25},{17,1},{25,9},{2,18},{10... | collective-permute-start | bytes 1216520 | tf_op jit(solution)/shard_map/ppermute | solution.py:362
  5.7 19.2 %collective-permute-start.2 = (bf16[144,1408]{1,0:T(8,128)(2,1)}, bf16[144,1408]{1,0:T(8,128)(2,1)}, u32[]{:S(2)}, u32[]{:S(2)}) collective-permute-start(bf16[144,1408]{1,0:T(8,128)(2,1)} %get-tuple-element.56), channel_id=1, source_target_pairs={{0,24},{8,16},{16,8},{24,0},{1,25},{9,17},{17,9},{25,1},{2,26},{10... | collective-permute-start | bytes 1216520 | tf_op jit(solution)/shard_map/ppermute | solution.py:362
  17.9 7.0 %copy-start.2 = (bf16[144,1408]{1,0:T(8,128)(2,1)}, bf16[144,1408]{1,0:T(8,128)(2,1)S(1)}, u32[]{:S(2)}) copy-start(bf16[144,1408]{1,0:T(8,128)(2,1)S(1)} %collective-permute-done.refs_1_) | copy-start | bytes 1216516
  24.9 0.8 copy-start.3
  31.9 22.8 %collective-permute-start.7 = (bf16[576,1024]{1,0:T(8,128)(2,1)}, bf16[576,1024]{1,0:T(8,128)(2,1)}, u32[]{:S(2)}, u32[]{:S(2)}) collective-permute-start(bf16[576,1024]{1,0:T(8,128)(2,1)} %get-tuple-element.57), channel_id=1, source_target_pairs={{0,1},{1,0},{2,3},{3,2},{4,5},{5,4},{6,7},{7,6},{8,9},{9,8},{10,11... | collective-permute-start | bytes 3538952 | tf_op jit(solution)/shard_map/ppermute | solution.py:365
  31.9 31.3 %collective-permute-start.3 = (bf16[576,1024]{1,0:T(8,128)(2,1)}, bf16[576,1024]{1,0:T(8,128)(2,1)}, u32[]{:S(2)}, u32[]{:S(2)}) collective-permute-start(bf16[576,1024]{1,0:T(8,128)(2,1)} %get-tuple-element.57), channel_id=1, source_target_pairs={{0,2},{1,3},{2,4},{3,5},{4,6},{5,7},{6,0},{7,1},{8,10},{9,11},{10,... | collective-permute-start | bytes 3538952 | tf_op jit(solution)/shard_map/ppermute | solution.py:369
  33.5 11.6 %collective-permute-start.5 = (bf16[360,512]{1,0:T(8,128)(2,1)}, bf16[360,512]{1,0:T(8,128)(2,1)S(1)}, u32[]{:S(2)}, u32[]{:S(2)}) collective-permute-start(bf16[360,512]{1,0:T(8,128)(2,1)} %get-tuple-element.59.refs_6_), channel_id=1, source_target_pairs={{0,16},{8,24},{16,0},{24,8},{1,17},{9,25},{17,1},{25,9},{2,18},{10... | collective-permute-start | bytes 1105928 | tf_op jit(solution)/shard_map/ppermute | solution.py:362
  34.1 12.6 %collective-permute-start.4 = (bf16[360,512]{1,0:T(8,128)(2,1)}, bf16[360,512]{1,0:T(8,128)(2,1)S(1)}, u32[]{:S(2)}, u32[]{:S(2)}) collective-permute-start(bf16[360,512]{1,0:T(8,128)(2,1)} %get-tuple-element.59.refs_6_), channel_id=1, source_target_pairs={{0,8},{8,0},{16,24},{24,16},{1,9},{9,1},{17,25},{25,17},{2,10},{10... | collective-permute-start | bytes 1105928 | tf_op jit(solution)/shard_map/ppermute | solution.py:362
  41.1 12.0 %collective-permute-start.8 = (bf16[360,512]{1,0:T(8,128)(2,1)}, bf16[360,512]{1,0:T(8,128)(2,1)}, u32[]{:S(2)}, u32[]{:S(2)}) collective-permute-start(bf16[360,512]{1,0:T(8,128)(2,1)} %get-tuple-element.69.refs_6_), channel_id=1, source_target_pairs={{0,16},{8,24},{16,0},{24,8},{1,17},{9,25},{17,1},{25,9},{2,18},{10... | collective-permute-start | bytes 1105928 | tf_op jit(solution)/shard_map/ppermute | solution.py:362
  45.1 9.5 %copy-start.4 = (bf16[360,512]{1,0:T(8,128)(2,1)}, bf16[360,512]{1,0:T(8,128)(2,1)S(1)}, u32[]{:S(2)}) copy-start(bf16[360,512]{1,0:T(8,128)(2,1)S(1)} %collective-permute-done.5.refs_9_.refs_8_) | copy-start | bytes 1105924
  45.2 25.4 %collective-permute-start.16 = (bf16[360,512]{1,0:T(8,128)(2,1)}, bf16[360,512]{1,0:T(8,128)(2,1)}, u32[]{:S(2)}, u32[]{:S(2)}) collective-permute-start(bf16[360,512]{1,0:T(8,128)(2,1)} %get-tuple-element.69.refs_6_), channel_id=1, source_target_pairs={{0,8},{8,0},{16,24},{24,16},{1,9},{9,1},{17,25},{25,17},{2,10},{10... | collective-permute-start | bytes 1105928 | tf_op jit(solution)/shard_map/ppermute | solution.py:362
  46.6 14.6 %copy-start.6 = (bf16[360,512]{1,0:T(8,128)(2,1)}, bf16[360,512]{1,0:T(8,128)(2,1)S(1)}, u32[]{:S(2)}) copy-start(bf16[360,512]{1,0:T(8,128)(2,1)S(1)} %collective-permute-done.4.refs_7_) | copy-start | bytes 1105924
  46.6 15.2 %collective-permute-start.6 = (bf16[360,512]{1,0:T(8,128)(2,1)S(1)}, bf16[360,512]{1,0:T(8,128)(2,1)}, u32[]{:S(2)}, u32[]{:S(2)}) collective-permute-start(bf16[360,512]{1,0:T(8,128)(2,1)S(1)} %collective-permute-done.4.refs_7_), channel_id=1, source_target_pairs={{0,16},{8,24},{16,0},{24,8},{1,17},{9,25},{17,1},{25,9},{2,18},{10... | collective-permute-start | bytes 1105928 | tf_op jit(solution)/shard_map/ppermute | solution.py:362
  53.2 18.2 %collective-permute-start.17 = (bf16[360,512]{1,0:T(8,128)(2,1)}, bf16[360,512]{1,0:T(8,128)(2,1)}, u32[]{:S(2)}, u32[]{:S(2)}) collective-permute-start(bf16[360,512]{1,0:T(8,128)(2,1)} %collective-permute-done.8.refs_13_.refs_8_), channel_id=1, source_target_pairs={{0,8},{8,0},{16,24},{24,16},{1,9},{9,1},{17,25},{25,17},{2,10},{10... | collective-permute-start | bytes 1105928 | tf_op jit(solution)/shard_map/ppermute | solution.py:362
  61.3 19.8 %collective-permute-start.13 = (bf16[360,1024]{1,0:T(8,128)(2,1)}, bf16[360,1024]{1,0:T(8,128)(2,1)}, u32[]{:S(2)}, u32[]{:S(2)}) collective-permute-start(bf16[360,1024]{1,0:T(8,128)(2,1)} %get-tuple-element.71.refs_6_), channel_id=1, source_target_pairs={{0,16},{8,24},{16,0},{24,8},{1,17},{9,25},{17,1},{25,9},{2,18},{10... | collective-permute-start | bytes 2211848 | tf_op jit(solution)/shard_map/ppermute | solution.py:362
  61.8 19.8 %collective-permute-start.12 = (bf16[360,1024]{1,0:T(8,128)(2,1)}, bf16[360,1024]{1,0:T(8,128)(2,1)}, u32[]{:S(2)}, u32[]{:S(2)}) collective-permute-start(bf16[360,1024]{1,0:T(8,128)(2,1)} %get-tuple-element.71.refs_6_), channel_id=1, source_target_pairs={{0,8},{8,0},{16,24},{24,16},{1,9},{9,1},{17,25},{25,17},{2,10},{10... | collective-permute-start | bytes 2211848 | tf_op jit(solution)/shard_map/ppermute | solution.py:362
  63.2 34.1 %collective-permute-start.15 = (bf16[576,1024]{1,0:T(8,128)(2,1)}, bf16[576,1024]{1,0:T(8,128)(2,1)}, u32[]{:S(2)}, u32[]{:S(2)}) collective-permute-start(bf16[576,1024]{1,0:T(8,128)(2,1)} %collective-permute-done.3.refs_0_), channel_id=1, source_target_pairs={{0,1},{1,0},{2,3},{3,2},{4,5},{5,4},{6,7},{7,6},{8,9},{9,8},{10,11... | collective-permute-start | bytes 3538952 | tf_op jit(solution)/shard_map/ppermute | solution.py:365
  70.6 26.2 %collective-permute-start.18 = (bf16[360,1024]{1,0:T(8,128)(2,1)}, bf16[360,1024]{1,0:T(8,128)(2,1)S(1)}, u32[]{:S(2)}, u32[]{:S(2)}) collective-permute-start(bf16[360,1024]{1,0:T(8,128)(2,1)} %get-tuple-element.70.rest_0_.refs_6_), channel_id=1, source_target_pairs={{0,16},{8,24},{16,0},{24,8},{1,17},{9,25},{17,1},{25,9},{2,18},{10... | collective-permute-start | bytes 2211848 | tf_op jit(solution)/shard_map/ppermute | solution.py:362
  71.4 33.8 %collective-permute-start.9 = (bf16[576,1024]{1,0:T(8,128)(2,1)}, bf16[576,1024]{1,0:T(8,128)(2,1)}, u32[]{:S(2)}, u32[]{:S(2)}) collective-permute-start(bf16[576,1024]{1,0:T(8,128)(2,1)} %collective-permute-done.3.refs_0_), channel_id=1, source_target_pairs={{0,2},{1,3},{2,4},{3,5},{4,6},{5,7},{6,0},{7,1},{8,10},{9,11},{10,... | collective-permute-start | bytes 3538952 | tf_op jit(solution)/shard_map/ppermute | solution.py:369
  81.1 39.7 %collective-permute-start.26 = (bf16[360,1024]{1,0:T(8,128)(2,1)}, bf16[360,1024]{1,0:T(8,128)(2,1)}, u32[]{:S(2)}, u32[]{:S(2)}) collective-permute-start(bf16[360,1024]{1,0:T(8,128)(2,1)} %get-tuple-element.70.rest_0_.refs_6_), channel_id=1, source_target_pairs={{0,8},{8,0},{16,24},{24,16},{1,9},{9,1},{17,25},{25,17},{2,10},{10... | collective-permute-start | bytes 2211848 | tf_op jit(solution)/shard_map/ppermute | solution.py:362
  81.6 31.1 %collective-permute-start.14 = (bf16[360,1024]{1,0:T(8,128)(2,1)}, bf16[360,1024]{1,0:T(8,128)(2,1)}, u32[]{:S(2)}, u32[]{:S(2)}) collective-permute-start(bf16[360,1024]{1,0:T(8,128)(2,1)} %collective-permute-done.12.refs_7_), channel_id=1, source_target_pairs={{0,16},{8,24},{16,0},{24,8},{1,17},{9,25},{17,1},{25,9},{2,18},{10... | collective-permute-start | bytes 2211848 | tf_op jit(solution)/shard_map/ppermute | solution.py:362
  96.8 8.0 %copy-start = (bf16[360,1024]{1,0:T(8,128)(2,1)}, bf16[360,1024]{1,0:T(8,128)(2,1)S(1)}, u32[]{:S(2)}) copy-start(bf16[360,1024]{1,0:T(8,128)(2,1)S(1)} %collective-permute-done.18.refs_14_.refs_8_) | copy-start | bytes 2211844
  96.8 24.6 %collective-permute-start.27 = (bf16[360,1024]{1,0:T(8,128)(2,1)S(1)}, bf16[360,1024]{1,0:T(8,128)(2,1)}, u32[]{:S(2)}, u32[]{:S(2)}) collective-permute-start(bf16[360,1024]{1,0:T(8,128)(2,1)S(1)} %collective-permute-done.18.refs_14_.refs_8_), channel_id=1, source_target_pairs={{0,8},{8,0},{16,24},{24,16},{1,9},{9,1},{17,25},{25,17},{2,10},{10... | collective-permute-start | bytes 2211848 | tf_op jit(solution)/shard_map/ppermute | solution.py:362
  104.7 23.7 %collective-permute-start.23 = (bf16[360,1024]{1,0:T(8,128)(2,1)}, bf16[360,1024]{1,0:T(8,128)(2,1)}, u32[]{:S(2)}, u32[]{:S(2)}) collective-permute-start(bf16[360,1024]{1,0:T(8,128)(2,1)} %get-tuple-element.81.refs_6_), channel_id=1, source_target_pairs={{0,16},{8,24},{16,0},{24,8},{1,17},{9,25},{17,1},{25,9},{2,18},{10... | collective-permute-start | bytes 2211848 | tf_op jit(solution)/shard_map/ppermute | solution.py:362
  105.2 48.3 %collective-permute-start.25 = (bf16[576,1024]{1,0:T(8,128)(2,1)}, bf16[576,1024]{1,0:T(8,128)(2,1)}, u32[]{:S(2)}, u32[]{:S(2)}) collective-permute-start(bf16[576,1024]{1,0:T(8,128)(2,1)} %collective-permute-done.9.refs_0_), channel_id=1, source_target_pairs={{0,1},{1,0},{2,3},{3,2},{4,5},{5,4},{6,7},{7,6},{8,9},{9,8},{10,11... | collective-permute-start | bytes 3538952 | tf_op jit(solution)/shard_map/ppermute | solution.py:365
  112.7 40.8 %collective-permute-start.10 = (bf16[576,1024]{1,0:T(8,128)(2,1)}, bf16[576,1024]{1,0:T(8,128)(2,1)}, u32[]{:S(2)}, u32[]{:S(2)}) collective-permute-start(bf16[576,1024]{1,0:T(8,128)(2,1)} %collective-permute-done.9.refs_0_), channel_id=1, source_target_pairs={{0,2},{1,3},{2,4},{3,5},{4,6},{5,7},{6,0},{7,1},{8,10},{9,11},{10,... | collective-permute-start | bytes 3538952 | tf_op jit(solution)/shard_map/ppermute | solution.py:369
  120.8 16.8 %collective-permute-start.22 = (bf16[360,1024]{1,0:T(8,128)(2,1)}, bf16[360,1024]{1,0:T(8,128)(2,1)}, u32[]{:S(2)}, u32[]{:S(2)}) collective-permute-start(bf16[360,1024]{1,0:T(8,128)(2,1)} %get-tuple-element.81.refs_6_), channel_id=1, source_target_pairs={{0,8},{8,0},{16,24},{24,16},{1,9},{9,1},{17,25},{25,17},{2,10},{10... | collective-permute-start | bytes 2211848 | tf_op jit(solution)/shard_map/ppermute | solution.py:362
  121.4 22.8 %collective-permute-start.20 = (bf16[360,1024]{1,0:T(8,128)(2,1)}, bf16[360,1024]{1,0:T(8,128)(2,1)S(1)}, u32[]{:S(2)}, u32[]{:S(2)}) collective-permute-start(bf16[360,1024]{1,0:T(8,128)(2,1)} %get-tuple-element.80.refs_6_), channel_id=1, source_target_pairs={{0,16},{8,24},{16,0},{24,8},{1,17},{9,25},{17,1},{25,9},{2,18},{10... | collective-permute-start | bytes 2211848 | tf_op jit(solution)/shard_map/ppermute | solution.py:362
  122.0 86.9 %all-to-all-start = ((bf16[8,144,1024]{2,1,0:T(8,128)(2,1)}), bf16[8,144,1024]{2,1,0:T(8,128)(2,1)}, u32[]{:S(2)}, u32[]{:S(2)}) async-start(bf16[8,144,1024]{2,1,0:T(8,128)(2,1)} %input_product.3.refs_14_), calls=%async_computation | async-start | bytes 4718592 | tf_op jit(solution)/shard_map/all_to_all | solution.py:446
  128.5 41.0 %collective-permute-start.19 = (bf16[360,1024]{1,0:T(8,128)(2,1)}, bf16[360,1024]{1,0:T(8,128)(2,1)}, u32[]{:S(2)}, u32[]{:S(2)}) collective-permute-start(bf16[360,1024]{1,0:T(8,128)(2,1)} %get-tuple-element.80.refs_6_), channel_id=1, source_target_pairs={{0,8},{8,0},{16,24},{24,16},{1,9},{9,1},{17,25},{25,17},{2,10},{10... | collective-permute-start | bytes 2211848 | tf_op jit(solution)/shard_map/ppermute | solution.py:362
  137.6 23.9 %collective-permute-start.24 = (bf16[360,1024]{1,0:T(8,128)(2,1)}, bf16[360,1024]{1,0:T(8,128)(2,1)}, u32[]{:S(2)}, u32[]{:S(2)}) collective-permute-start(bf16[360,1024]{1,0:T(8,128)(2,1)} %collective-permute-done.22.refs_7_), channel_id=1, source_target_pairs={{0,16},{8,24},{16,0},{24,8},{1,17},{9,25},{17,1},{25,9},{2,18},{10... | collective-permute-start | bytes 2211848 | tf_op jit(solution)/shard_map/ppermute | solution.py:362
  144.2 17.2 %copy-start.1 = (bf16[360,1024]{1,0:T(8,128)(2,1)}, bf16[360,1024]{1,0:T(8,128)(2,1)S(1)}, u32[]{:S(2)}) copy-start(bf16[360,1024]{1,0:T(8,128)(2,1)S(1)} %collective-permute-done.20.refs_14_.refs_8_) | copy-start | bytes 2211844
  144.2 27.3 %collective-permute-start.21 = (bf16[360,1024]{1,0:T(8,128)(2,1)S(1)}, bf16[360,1024]{1,0:T(8,128)(2,1)}, u32[]{:S(2)}, u32[]{:S(2)}) collective-permute-start(bf16[360,1024]{1,0:T(8,128)(2,1)S(1)} %collective-permute-done.20.refs_14_.refs_8_), channel_id=1, source_target_pairs={{0,8},{8,0},{16,24},{24,16},{1,9},{9,1},{17,25},{25,17},{2,10},{10... | collective-permute-start | bytes 2211848 | tf_op jit(solution)/shard_map/ppermute | solution.py:362
  153.5 27.6 %collective-permute-start.11 = (bf16[576,1024]{1,0:T(8,128)(2,1)}, bf16[576,1024]{1,0:T(8,128)(2,1)}, u32[]{:S(2)}, u32[]{:S(2)}) collective-permute-start(bf16[576,1024]{1,0:T(8,128)(2,1)} %collective-permute-done.10.refs_0_), channel_id=1, source_target_pairs={{0,1},{1,0},{2,3},{3,2},{4,5},{5,4},{6,7},{7,6},{8,9},{9,8},{10,11... | collective-permute-start | bytes 3538952 | tf_op jit(solution)/shard_map/ppermute | solution.py:365
  161.4 19.7 %collective-permute-start.28 = (bf16[360,1024]{1,0:T(8,128)(2,1)}, bf16[360,1024]{1,0:T(8,128)(2,1)}, u32[]{:S(2)}, u32[]{:S(2)}) collective-permute-start(bf16[360,1024]{1,0:T(8,128)(2,1)} %get-tuple-element.94.refs_0_), channel_id=1, source_target_pairs={{0,16},{8,24},{16,0},{24,8},{1,17},{9,25},{17,1},{25,9},{2,18},{10... | collective-permute-start | bytes 2211848 | tf_op jit(solution)/shard_map/ppermute | solution.py:362
  161.5 27.7 %collective-permute-start.35 = (bf16[360,1024]{1,0:T(8,128)(2,1)}, bf16[360,1024]{1,0:T(8,128)(2,1)}, u32[]{:S(2)}, u32[]{:S(2)}) collective-permute-start(bf16[360,1024]{1,0:T(8,128)(2,1)} %get-tuple-element.94.refs_0_), channel_id=1, source_target_pairs={{0,8},{8,0},{16,24},{24,16},{1,9},{9,1},{17,25},{25,17},{2,10},{10... | collective-permute-start | bytes 2211848 | tf_op jit(solution)/shard_map/ppermute | solution.py:362
  169.5 27.4 %collective-permute-start.32 = (bf16[360,1024]{1,0:T(8,128)(2,1)}, bf16[360,1024]{1,0:T(8,128)(2,1)}, u32[]{:S(2)}, u32[]{:S(2)}) collective-permute-start(bf16[360,1024]{1,0:T(8,128)(2,1)} %get-tuple-element.99.refs_0_), channel_id=1, source_target_pairs={{0,16},{8,24},{16,0},{24,8},{1,17},{9,25},{17,1},{25,9},{2,18},{10... | collective-permute-start | bytes 2211848 | tf_op jit(solution)/shard_map/ppermute | solution.py:362
  181.1 8.3 %copy-start.5 = (bf16[360,1024]{1,0:T(8,128)(2,1)S(1)}, bf16[360,1024]{1,0:T(8,128)(2,1)}, u32[]{:S(2)}) copy-start(bf16[360,1024]{1,0:T(8,128)(2,1)} %get-tuple-element.99.refs_0_) | copy-start | bytes 2211844
  189.1 19.8 %collective-permute-start.29 = (bf16[360,1024]{1,0:T(8,128)(2,1)}, bf16[360,1024]{1,0:T(8,128)(2,1)}, u32[]{:S(2)}, u32[]{:S(2)}) collective-permute-start(bf16[360,1024]{1,0:T(8,128)(2,1)} %get-tuple-element.98.refs_4_), channel_id=1, source_target_pairs={{0,8},{8,0},{16,24},{24,16},{1,9},{9,1},{17,25},{25,17},{2,10},{10... | collective-permute-start | bytes 2211848 | tf_op jit(solution)/shard_map/ppermute | solution.py:362
  189.2 23.5 %collective-permute-start.36 = (bf16[360,1024]{1,0:T(8,128)(2,1)}, bf16[360,1024]{1,0:T(8,128)(2,1)}, u32[]{:S(2)}, u32[]{:S(2)}) collective-permute-start(bf16[360,1024]{1,0:T(8,128)(2,1)} %collective-permute-done.35.refs_1_), channel_id=1, source_target_pairs={{0,16},{8,24},{16,0},{24,8},{1,17},{9,25},{17,1},{25,9},{2,18},{10... | collective-permute-start | bytes 2211848 | tf_op jit(solution)/shard_map/ppermute | solution.py:362
  189.4 35.4 %collective-permute-start.31 = (bf16[360,1024]{1,0:T(8,128)(2,1)S(1)}, bf16[360,1024]{1,0:T(8,128)(2,1)}, u32[]{:S(2)}, u32[]{:S(2)}) collective-permute-start(bf16[360,1024]{1,0:T(8,128)(2,1)S(1)} %copy-done.5), channel_id=1, source_target_pairs={{0,8},{8,0},{16,24},{24,16},{1,9},{9,1},{17,25},{25,17},{2,10},{10... | collective-permute-start | bytes 2211848 | tf_op jit(solution)/shard_map/ppermute | solution.py:362
  196.9 42.0 %collective-permute-start.33 = (bf16[360,1024]{1,0:T(8,128)(2,1)}, bf16[360,1024]{1,0:T(8,128)(2,1)}, u32[]{:S(2)}, u32[]{:S(2)}) collective-permute-start(bf16[360,1024]{1,0:T(8,128)(2,1)} %collective-permute-done.32.refs_2_), channel_id=1, source_target_pairs={{0,8},{8,0},{16,24},{24,16},{1,9},{9,1},{17,25},{25,17},{2,10},{10... | collective-permute-start | bytes 2211848 | tf_op jit(solution)/shard_map/ppermute | solution.py:362
  196.9 42.0 %collective-permute-start.34 = (bf16[360,1024]{1,0:T(8,128)(2,1)}, bf16[360,1024]{1,0:T(8,128)(2,1)}, u32[]{:S(2)}, u32[]{:S(2)}) collective-permute-start(bf16[360,1024]{1,0:T(8,128)(2,1)} %get-tuple-element.98.refs_4_), channel_id=1, source_target_pairs={{0,16},{8,24},{16,0},{24,8},{1,17},{9,25},{17,1},{25,9},{2,18},{10... | collective-permute-start | bytes 2211848 | tf_op jit(solution)/shard_map/ppermute | solution.py:362
  208.9 35.0 %collective-permute-start.30 = (bf16[360,1024]{1,0:T(8,128)(2,1)}, bf16[360,1024]{1,0:T(8,128)(2,1)}, u32[]{:S(2)}, u32[]{:S(2)}) collective-permute-start(bf16[360,1024]{1,0:T(8,128)(2,1)} %collective-permute-done.29.refs_5_), channel_id=1, source_target_pairs={{0,16},{8,24},{16,0},{24,8},{1,17},{9,25},{17,1},{25,9},{2,18},{10... | collective-permute-start | bytes 2211848 | tf_op jit(solution)/shard_map/ppermute | solution.py:362

commit v4 on v3

--- a/solution.py
+++ b/solution.py
@@ -145,7 +145,7 @@
             for message in acts:
                 term = lax.dot_general(
                     message[:, slice_width : slice_width + units],
-                    message[:, offset : offset + tile],
+                    message[:, pl.ds(pl.multiple_of(offset + step * tile, tile), tile)],
                     (((0,), (0,)), ((), ())),
                     preferred_element_type=jnp.float32,
                 )
@@ -181,12 +181,16 @@
     second_out[...] = outs[2]
     piece[...] = outs[3].astype(piece.dtype)
     if unpack:
-        all_acts, all_grads = rest[-2:]
-        tokens = acts[0].shape[0]
-        for i, message in enumerate(acts):
-            rows = slice(i * tokens, (i + 1) * tokens)
-            all_acts[rows, :] = message[:, :slice_width]
-            all_grads[:, rows] = message[:, slice_width : slice_width + units].T
+
+        @pl.when(step == 0)
+        def _():
+            all_acts, all_grads = rest[-2:]
+            tokens = acts[0].shape[0]
+            for i, message in enumerate(acts):
+                rows = slice(i * tokens, (i + 1) * tokens)
+                all_acts[rows, :] = message[:, :slice_width]
+                all_grads[:, rows] = message[:, slice_width : slice_width + units].T
+
     if n_pieces:
 
         @pl.when(step == n_steps - 1)
@@ -203,7 +207,8 @@
     rows, model_width = states[0].shape
     n_tensor, step, side, offset = where
     slice_width = model_width // n_tensor
-    tile = 2 * LEAD if width % (2 * LEAD) == 0 and offset % (2 * LEAD) == 0 else LEAD
+    wide = units is None and width % (2 * LEAD) == 0 and offset % (2 * LEAD) == 0
+    tile = 2 * LEAD if wide else LEAD
     n_steps = width // tile
 
     def state_at(j, ids):

time: 247 us -> 248 us (level)
  no operation moved by 1% of the time
where the time goes in v4:
time: 248 us; the launch traced here: 247 us
  waiting for transfers between devices  118 us (48%)
  Pallas kernels  93.4 us (38%)
  starting transfers between devices  29.8 us (12%)
  other arithmetic  3.44 us (1%)
    ppermute x30, waiting for transfers between devices, swap(): return lax.ppermute(array, 'dp', [(i, i ^ mask) for i in range(n_dp)])  110 us
    pallas_call x9, Pallas kernels, optimizer_step(): pl.pallas_call(functools.partial(step_kernel, inverse, units, slice_width...  64.7 us
    ppermute x30, starting transfers between devices, swap(): return lax.ppermute(array, 'dp', [(i, i ^ mask) for i in range(n_dp)])  22 us
    pallas_call x2, Pallas kernels, input_product(): pl.pallas_call(product_kernel, out_shape=jax.ShapeDtypeStruct((slices, to...  14 us
    pallas_call x3, Pallas kernels, place_pieces(): pl.pallas_call(functools.partial(place_kernel, slice_width, [group[:2] fo...  11.2 us
    ppermute x3, waiting for transfers between devices, shift_pair(): return lax.ppermute(array, 'tensor', moves)  8.71 us
    all_to_all x1, starting transfers between devices, square_body(): terms = lax.all_to_all(terms, 'tensor', 0, 0)  5.68 us
  transfers between devices with their start and end apart: 38, of which 16 were waited for; matrix products, arithmetic and copies ran while one was open for 1% of the time, Pallas kernels for 33%

profile of v4, /device:TPU:22, one launch (start us, length us, event | category | flops | bytes accessed | tf_op | source)
XLA Modules:
  0.0 246.9 jit_solution(2540459659766367707)
XLA Ops:
  0.6 0.6 pad_add_fusion.ids
  1.2 3.4 %pack_messages.1 = (bf16[144,1408]{1,0:T(8,128)(2,1)}, bf16[144,1408]{1,0:T(8,128)(2,1)}, bf16[144,1408]{1,0:T(8,128)(2,1)}, bf16[144,1408]{1,0:T(8,128)(2,1)}) custom-call(s32[2]{0:T(128)} %pad_add_fusion.ids, bf16[144,8192]{1,0:T(8,128)(2,1)} %bitcast.8, bf16[144,1440]{1,0:T(8,128)(2,1)} %bitcast.9), custom_call_target="tpu_custom_call" | custom-call | bytes 1658880 | tf_op jit(solution)/shard_map/pack_messages/pallas_call | solution.py:79
  4.6 0.5 collective-permute-start
  5.1 0.5 collective-permute-start.1
  5.7 2.4 collective-permute-start.2
  8.1 9.8 %input_product.2.refs_8_.rest_1_ = bf16[8,144,1024]{2,1,0:T(8,128)(2,1)} custom-call(bf16[144,1440]{1,0:T(8,128)(2,1)} %bitcast.10, bf16[1440,8192]{1,0:T(8,128)(2,1)} %weight.3, bf16[144,1408]{1,0:T(8,128)(2,1)} %get-tuple-element.53.rest_0_.refs_0_), custom_call_target="tpu_custom_call" | custom-call | flops 36864000000 | bytes 17694720 | tf_op jit(solution)/shard_map/input_product/pallas_call | solution.py:334
  17.9 7.0 %collective-permute-done.1.refs_2_ = bf16[144,1408]{1,0:T(8,128)(2,1)S(1)} collective-permute-done((bf16[144,1408]{1,0:T(8,128)(2,1)}, bf16[144,1408]{1,0:T(8,128)(2,1)S(1)}, u32[]{:S(2)}, u32[]{:S(2)}) %collective-permute-start.1) | collective-permute-done | bytes 405536 | tf_op jit(solution)/shard_map/ppermute | solution.py:367
  24.9 0.8 copy-done.3
  25.7 6.3 %optimizer_step.9 = (bf16[360,512]{1,0:T(8,128)(2,1)}, f32[360,8192]{1,0:T(8,128)}, f32[360,8192]{1,0:T(8,128)}, f32[360,8192]{1,0:T(8,128)}, bf16[576,1024]{1,0:T(8,128)(2,1)}, /*index=5*/bf16[360,576]{1,0:T(8,128)(2,1)}) custom-call(s32[2]{0:T(128)} %pad_add_fusion.ids, bf16[144,1408]{1,0:T(8,128)(2,1)} %get-tuple-element.53.rest_0_.refs_0_, ...), custom_call_target="tpu_custom_call" | custom-call | flops 4096000000 | bytes 5529600 | tf_op jit(solution)/shard_map/optimizer_step/pallas_call | solution.py:257
  31.9 0.1 collective-permute-start.7
  32.0 1.6 collective-permute-start.3
  33.7 0.6 collective-permute-start.5
  34.2 1.4 collective-permute-start.4
  35.7 5.3 %optimizer_step.10 = (bf16[360,512]{1,0:T(8,128)(2,1)}, f32[360,8192]{1,0:T(8,128)}, f32[360,8192]{1,0:T(8,128)}, f32[360,8192]{1,0:T(8,128)}) custom-call(s32[2]{0:T(128)} %pad_add_fusion.ids, bf16[144,1408]{1,0:T(8,128)(2,1)} %get-tuple-element.53.rest_0_.refs_0_, ...), custom_call_target="tpu_custom_call", output_to_operand_aliasing={{1}: (9, {}), {2}: (10, {}), {3}: (11, {})} | custom-call | flops 4096000000 | bytes 5529600 | tf_op jit(solution)/shard_map/optimizer_step/pallas_call | solution.py:257
  40.9 1.6 collective-permute-start.8
  42.5 2.8 %collective-permute-done.5.refs_9_.refs_8_ = bf16[360,512]{1,0:T(8,128)(2,1)S(1)} collective-permute-done((bf16[360,512]{1,0:T(8,128)(2,1)}, bf16[360,512]{1,0:T(8,128)(2,1)S(1)}, u32[]{:S(2)}, u32[]{:S(2)}) %collective-permute-start.5) | collective-permute-done | bytes 368672 | tf_op jit(solution)/shard_map/ppermute | solution.py:367
  45.3 1.5 collective-permute-start.16
  46.8 0.5 collective-permute-start.6
  47.3 6.0 %collective-permute-done.8.refs_13_.refs_8_ = bf16[360,512]{1,0:T(8,128)(2,1)} collective-permute-done((bf16[360,512]{1,0:T(8,128)(2,1)}, bf16[360,512]{1,0:T(8,128)(2,1)}, u32[]{:S(2)}, u32[]{:S(2)}) %collective-permute-start.8) | collective-permute-done | bytes 368672 | tf_op jit(solution)/shard_map/ppermute | solution.py:367
  53.3 1.5 collective-permute-start.17
  54.8 6.6 %optimizer_step.11 = (bf16[360,1024]{1,0:T(8,128)(2,1)}, f32[360,8192]{1,0:T(8,128)}, f32[360,8192]{1,0:T(8,128)}, f32[360,8192]{1,0:T(8,128)}) custom-call(s32[2]{0:T(128)} %pad_add_fusion.ids, bf16[576,1024]{1,0:T(8,128)(2,1)} %collective-permute-done.7.refs_0_, ...), custom_call_target="tpu_custom_call", output_to_operand_aliasing={{1}: (7, {}), {2}: (8, {}), {3}: (9, {})} | custom-call | flops 8192000000 | bytes 11059200 | tf_op jit(solution)/shard_map/optimizer_step/pallas_call | solution.py:257
  61.4 0.6 collective-permute-start.13
  62.0 1.1 collective-permute-start.12
  63.1 7.4 %optimizer_step.12 = (bf16[360,1024]{1,0:T(8,128)(2,1)}, f32[360,8192]{1,0:T(8,128)}, f32[360,8192]{1,0:T(8,128)}, f32[360,8192]{1,0:T(8,128)}, bf16[4,360,8192]{2,1,0:T(8,128)(2,1)}) custom-call(s32[2]{0:T(128)} %pad_add_fusion.ids, bf16[576,1024]{1,0:T(8,128)(2,1)} %collective-permute-done.3.refs_0_, ...), custom_call_target="tpu_custom_call", output_to_operand_aliasing={{1}: (11, {}), {2}: (12, {}), {3}: (13, {})} | custom-call | flops 8192000000 | bytes 14008320 | tf_op jit(solution)/shard_map/optimizer_step/pallas_call | solution.py:257
  70.5 1.0 collective-permute-start.18
  71.5 0.2 collective-permute-start.9
  71.8 4.2 %input_product.3.refs_14_ = bf16[8,144,1024]{2,1,0:T(8,128)(2,1)} custom-call(bf16[144,1440]{1,0:T(8,128)(2,1)} %bitcast.11, bf16[1440,8192]{1,0:T(8,128)(2,1)} %weight.3, bf16[360,1024]{1,0:T(8,128)(2,1)} %get-tuple-element.70.rest_0_.refs_6_, bf16[8,144,1024]{2,1,0:T(8,128)(2,1)} %input_product.2.refs_8_.rest_1_), custom_call_target="tpu_custom_call", output_to_operand_aliasing={{}: (3, {})} | custom-call | flops 12288000000 | bytes 5898240 | tf_op jit(solution)/shard_map/input_product/pallas_call | solution.py:334
  76.0 5.2 %collective-permute-done.13.refs_15_.refs_8_ = bf16[360,1024]{1,0:T(8,128)(2,1)} collective-permute-done((bf16[360,1024]{1,0:T(8,128)(2,1)}, bf16[360,1024]{1,0:T(8,128)(2,1)}, u32[]{:S(2)}, u32[]{:S(2)}) %collective-permute-start.13) | collective-permute-done | bytes 737312 | tf_op jit(solution)/shard_map/ppermute | solution.py:367
  81.2 0.5 collective-permute-start.26
  81.8 0.3 collective-permute-start.14
  82.0 14.9 %collective-permute-done.18.refs_14_.refs_8_ = bf16[360,1024]{1,0:T(8,128)(2,1)S(1)} collective-permute-done((bf16[360,1024]{1,0:T(8,128)(2,1)}, bf16[360,1024]{1,0:T(8,128)(2,1)S(1)}, u32[]{:S(2)}, u32[]{:S(2)}) %collective-permute-start.18) | collective-permute-done | bytes 737312 | tf_op jit(solution)/shard_map/ppermute | solution.py:367
  96.9 0.5 collective-permute-start.27
  97.5 7.4 %optimizer_step.13 = (bf16[360,1024]{1,0:T(8,128)(2,1)}, f32[360,8192]{1,0:T(8,128)}, f32[360,8192]{1,0:T(8,128)}, f32[360,8192]{1,0:T(8,128)}, bf16[4,360,8192]{2,1,0:T(8,128)(2,1)}) custom-call(s32[2]{0:T(128)} %pad_add_fusion.ids, ...), custom_call_target="tpu_custom_call", output_to_operand_aliasing={{1}: (11, {}), {2}: (12, {}), {3}: (13, {}), {4}: (14, {})} | custom-call | flops 8192000000 | bytes 14008320 | tf_op jit(solution)/shard_map/optimizer_step/pallas_call | solution.py:257
  104.9 0.4 collective-permute-start.23
  105.2 7.6 %collective-permute-done.14.refs_9_ = bf16[360,1024]{1,0:T(8,128)(2,1)} collective-permute-done((bf16[360,1024]{1,0:T(8,128)(2,1)}, bf16[360,1024]{1,0:T(8,128)(2,1)}, u32[]{:S(2)}, u32[]{:S(2)}) %collective-permute-start.14) | collective-permute-done | bytes 737312 | tf_op jit(solution)/shard_map/ppermute | solution.py:367
  112.8 0.2 collective-permute-start.10
  113.0 7.9 %optimizer_step.14 = (bf16[360,1024]{1,0:T(8,128)(2,1)}, f32[360,8192]{1,0:T(8,128)}, f32[360,8192]{1,0:T(8,128)}, f32[360,8192]{1,0:T(8,128)}, bf16[4,360,8192]{2,1,0:T(8,128)(2,1)}) custom-call(s32[2]{0:T(128)} %pad_add_fusion.ids, ...), custom_call_target="tpu_custom_call", output_to_operand_aliasing={{1}: (11, {}), {2}: (12, {}), {3}: (13, {}), {4}: (14, {})} | custom-call | flops 8192000000 | bytes 16957440 | tf_op jit(solution)/shard_map/optimizer_step/pallas_call | solution.py:257
  121.0 0.6 collective-permute-start.22
  121.6 0.6 collective-permute-start.20
  122.1 5.7 %all-to-all-start = ((bf16[8,144,1024]{2,1,0:T(8,128)(2,1)}), bf16[8,144,1024]{2,1,0:T(8,128)(2,1)}, u32[]{:S(2)}, u32[]{:S(2)}) async-start(bf16[8,144,1024]{2,1,0:T(8,128)(2,1)} %input_product.3.refs_14_), calls=%async_computation | async-start | bytes 4718592 | tf_op jit(solution)/shard_map/all_to_all | solution.py:451
  127.8 0.8 collective-permute-done.23.refs_14_.refs_8_
  128.6 0.9 collective-permute-start.19
  129.5 8.2 %collective-permute-done.22.refs_7_ = bf16[360,1024]{1,0:T(8,128)(2,1)} collective-permute-done((bf16[360,1024]{1,0:T(8,128)(2,1)}, bf16[360,1024]{1,0:T(8,128)(2,1)}, u32[]{:S(2)}, u32[]{:S(2)}) %collective-permute-start.22) | collective-permute-done | bytes 737312 | tf_op jit(solution)/shard_map/ppermute | solution.py:367
  137.7 6.6 %collective-permute-done.20.refs_14_.refs_8_ = bf16[360,1024]{1,0:T(8,128)(2,1)S(1)} collective-permute-done((bf16[360,1024]{1,0:T(8,128)(2,1)}, bf16[360,1024]{1,0:T(8,128)(2,1)S(1)}, u32[]{:S(2)}, u32[]{:S(2)}) %collective-permute-start.20) | collective-permute-done | bytes 737312 | tf_op jit(solution)/shard_map/ppermute | solution.py:367
  144.3 0.5 collective-permute-start.21
  144.9 8.7 %collective-permute-done.10.refs_0_ = bf16[576,1024]{1,0:T(8,128)(2,1)} collective-permute-done((bf16[576,1024]{1,0:T(8,128)(2,1)}, bf16[576,1024]{1,0:T(8,128)(2,1)}, u32[]{:S(2)}, u32[]{:S(2)}) %collective-permute-start.10) | collective-permute-done | bytes 1179680 | tf_op jit(solution)/shard_map/ppermute | solution.py:374
  153.6 7.9 %optimizer_step.15 = (bf16[360,1024]{1,0:T(8,128)(2,1)}, f32[360,8192]{1,0:T(8,128)}, f32[360,8192]{1,0:T(8,128)}, f32[360,8192]{1,0:T(8,128)}, bf16[4,360,8192]{2,1,0:T(8,128)(2,1)}) custom-call(s32[2]{0:T(128)} %pad_add_fusion.ids, ...), custom_call_target="tpu_custom_call", output_to_operand_aliasing={{1}: (11, {}), {2}: (12, {}), {3}: (13, {}), {4}: (14, {})} | custom-call | flops 8192000000 | bytes 16957440 | tf_op jit(solution)/shard_map/optimizer_step/pallas_call | solution.py:257
  161.6 0.1 collective-permute-start.35
  161.7 7.9 %optimizer_step.16 = (bf16[360,1024]{1,0:T(8,128)(2,1)}, f32[360,8192]{1,0:T(8,128)}, f32[360,8192]{1,0:T(8,128)}, f32[360,8192]{1,0:T(8,128)}, bf16[4,360,8192]{2,1,0:T(8,128)(2,1)}) custom-call(s32[2]{0:T(128)} %pad_add_fusion.ids, ...), custom_call_target="tpu_custom_call", output_to_operand_aliasing={{1}: (11, {}), {2}: (12, {}), {3}: (13, {}), {4}: (14, {})} | custom-call | flops 8192000000 | bytes 16957440 | tf_op jit(solution)/shard_map/optimizer_step/pallas_call | solution.py:257
  169.6 2.0 collective-permute-start.32
  171.6 9.6 %collective-permute-done.28.refs_14_.refs_2_ = bf16[360,1024]{1,0:T(8,128)(2,1)} collective-permute-done((bf16[360,1024]{1,0:T(8,128)(2,1)}, bf16[360,1024]{1,0:T(8,128)(2,1)}, u32[]{:S(2)}, u32[]{:S(2)}) %collective-permute-start.28) | collective-permute-done | bytes 737312 | tf_op jit(solution)/shard_map/ppermute | solution.py:367
  181.2 8.0 %optimizer_step.17 = (bf16[360,1024]{1,0:T(8,128)(2,1)}, f32[360,8192]{1,0:T(8,128)}, f32[360,8192]{1,0:T(8,128)}, f32[360,8192]{1,0:T(8,128)}, bf16[4,360,8192]{2,1,0:T(8,128)(2,1)}) custom-call(s32[2]{0:T(128)} %pad_add_fusion.ids, ...), custom_call_target="tpu_custom_call", output_to_operand_aliasing={{1}: (11, {}), {2}: (12, {}), {3}: (13, {}), {4}: (14, {})} | custom-call | flops 8192000000 | bytes 16957440 | tf_op jit(solution)/shard_map/optimizer_step/pallas_call | solution.py:257
  189.3 0.1 collective-permute-start.36
  189.4 1.9 collective-permute-start.31
  191.4 5.6 %collective-permute-done.32.refs_2_ = bf16[360,1024]{1,0:T(8,128)(2,1)} collective-permute-done((bf16[360,1024]{1,0:T(8,128)(2,1)}, bf16[360,1024]{1,0:T(8,128)(2,1)}, u32[]{:S(2)}, u32[]{:S(2)}) %collective-permute-start.32) | collective-permute-done | bytes 737312 | tf_op jit(solution)/shard_map/ppermute | solution.py:367
  197.0 0.1 collective-permute-start.34
  197.0 12.0 %collective-permute-done.29.refs_5_ = bf16[360,1024]{1,0:T(8,128)(2,1)} collective-permute-done((bf16[360,1024]{1,0:T(8,128)(2,1)}, bf16[360,1024]{1,0:T(8,128)(2,1)}, u32[]{:S(2)}, u32[]{:S(2)}) %collective-permute-start.29) | collective-permute-done | bytes 737312 | tf_op jit(solution)/shard_map/ppermute | solution.py:367
  209.0 2.9 %reduce_sum.12.refs_5_.refs_8_.refs_2_ = bf16[144,1024]{1,0:T(8,128)(2,1)} reduce(bf16[8,144,1024]{2,1,0:T(8,128)(2,1)} %all-to-all-done, bf16[]{:T(256)} %constant.10.clone.1), dimensions={0}, to_apply=%region_0.0 | reduce | flops 1032192 | bytes 2654210 | tf_op jit(solution)/shard_map/reduce_sum | solution.py:452
  211.9 0.8 collective-permute-done.36.refs_3_
  212.7 3.4 %place_pieces.3.refs_7_ = bf16[4,360,8192]{2,1,0:T(8,128)(2,1)} custom-call(s32[2]{0:T(128)} %pad_add_fusion.ids, bf16[360,1024]{1,0:T(8,128)(2,1)} %get-tuple-element.94.refs_0_, bf16[360,1024]{1,0:T(8,128)(2,1)} %collective-permute-done.35.refs_1_, bf16[360,1024]{1,0:T(8,128)(2,1)} %collective-permute-done.28.refs_14_.refs_2_, ...), custom_call_target="tpu_custom_call", output_to_operand_aliasing={{}: (5, {})} | custom-call | flops 1253376000 | bytes 5898240 | tf_op jit(solution)/shard_map/place_pieces/pallas_call | solution.py:305
  216.2 8.6 %collective-permute-done.31.refs_1_ = bf16[360,1024]{1,0:T(8,128)(2,1)} collective-permute-done((bf16[360,1024]{1,0:T(8,128)(2,1)S(1)}, bf16[360,1024]{1,0:T(8,128)(2,1)}, u32[]{:S(2)}, u32[]{:S(2)}) %collective-permute-start.31) | collective-permute-done | bytes 737312 | tf_op jit(solution)/shard_map/ppermute | solution.py:367
  224.8 14.1 %collective-permute-done.33.refs_3_ = bf16[360,1024]{1,0:T(8,128)(2,1)} collective-permute-done((bf16[360,1024]{1,0:T(8,128)(2,1)}, bf16[360,1024]{1,0:T(8,128)(2,1)}, u32[]{:S(2)}, u32[]{:S(2)}) %collective-permute-start.33) | collective-permute-done | bytes 737312 | tf_op jit(solution)/shard_map/ppermute | solution.py:367
  238.9 5.1 %place_pieces.4.refs_1_ = bf16[4,360,8192]{2,1,0:T(8,128)(2,1)} custom-call(s32[2]{0:T(128)} %pad_add_fusion.ids, bf16[360,1024]{1,0:T(8,128)(2,1)} %get-tuple-element.99.refs_0_, bf16[360,1024]{1,0:T(8,128)(2,1)} %collective-permute-done.31.refs_1_, bf16[360,1024]{1,0:T(8,128)(2,1)} %collective-permute-done.32.refs_2_, ...), custom_call_target="tpu_custom_call", output_to_operand_aliasing={{}: (8, {})} | custom-call | flops 2193408000 | bytes 10321920 | tf_op jit(solution)/shard_map/place_pieces/pallas_call | solution.py:305
  244.0 2.7 %place_pieces.5 = bf16[4,360,8192]{2,1,0:T(8,128)(2,1)} custom-call(s32[2]{0:T(128)} %pad_add_fusion.ids, bf16[360,1024]{1,0:T(8,128)(2,1)} %collective-permute-done.30.refs_0_, bf16[4,360,8192]{2,1,0:T(8,128)(2,1)} %place_pieces.4.refs_1_, bf16[144,1024]{1,0:T(8,128)(2,1)} %reduce_sum.12.refs_5_.refs_8_.refs_2_), custom_call_target="tpu_custom_call", output_to_operand_aliasing={{}: (2, {})} | custom-call | flops 313344000 | bytes 1474560 | tf_op jit(solution)/shard_map/place_pieces/pallas_call | solution.py:305
  (43 shorter events, 0.3 us)
Async XLA Ops:
  4.6 13.3 %collective-permute-start = (bf16[144,1408]{1,0:T(8,128)(2,1)}, bf16[144,1408]{1,0:T(8,128)(2,1)S(1)}, u32[]{:S(2)}, u32[]{:S(2)}) collective-permute-start(bf16[144,1408]{1,0:T(8,128)(2,1)} %get-tuple-element.54), channel_id=1, source_target_pairs={{0,8},{8,0},{16,24},{24,16},{1,9},{9,1},{17,25},{25,17},{2,10},{10... | collective-permute-start | bytes 1216520 | tf_op jit(solution)/shard_map/ppermute | solution.py:367
  5.1 19.7 %collective-permute-start.1 = (bf16[144,1408]{1,0:T(8,128)(2,1)}, bf16[144,1408]{1,0:T(8,128)(2,1)S(1)}, u32[]{:S(2)}, u32[]{:S(2)}) collective-permute-start(bf16[144,1408]{1,0:T(8,128)(2,1)} %get-tuple-element.55), channel_id=1, source_target_pairs={{0,16},{8,24},{16,0},{24,8},{1,17},{9,25},{17,1},{25,9},{2,18},{10... | collective-permute-start | bytes 1216520 | tf_op jit(solution)/shard_map/ppermute | solution.py:367
  5.7 19.2 %collective-permute-start.2 = (bf16[144,1408]{1,0:T(8,128)(2,1)}, bf16[144,1408]{1,0:T(8,128)(2,1)}, u32[]{:S(2)}, u32[]{:S(2)}) collective-permute-start(bf16[144,1408]{1,0:T(8,128)(2,1)} %get-tuple-element.56), channel_id=1, source_target_pairs={{0,24},{8,16},{16,8},{24,0},{1,25},{9,17},{17,9},{25,1},{2,26},{10... | collective-permute-start | bytes 1216520 | tf_op jit(solution)/shard_map/ppermute | solution.py:367
  17.9 7.0 %copy-start.2 = (bf16[144,1408]{1,0:T(8,128)(2,1)}, bf16[144,1408]{1,0:T(8,128)(2,1)S(1)}, u32[]{:S(2)}) copy-start(bf16[144,1408]{1,0:T(8,128)(2,1)S(1)} %collective-permute-done.refs_1_) | copy-start | bytes 1216516
  24.9 0.8 copy-start.3
  31.9 22.9 %collective-permute-start.7 = (bf16[576,1024]{1,0:T(8,128)(2,1)}, bf16[576,1024]{1,0:T(8,128)(2,1)}, u32[]{:S(2)}, u32[]{:S(2)}) collective-permute-start(bf16[576,1024]{1,0:T(8,128)(2,1)} %get-tuple-element.57), channel_id=1, source_target_pairs={{0,1},{1,0},{2,3},{3,2},{4,5},{5,4},{6,7},{7,6},{8,9},{9,8},{10,11... | collective-permute-start | bytes 3538952 | tf_op jit(solution)/shard_map/ppermute | solution.py:370
  32.0 31.0 %collective-permute-start.3 = (bf16[576,1024]{1,0:T(8,128)(2,1)}, bf16[576,1024]{1,0:T(8,128)(2,1)}, u32[]{:S(2)}, u32[]{:S(2)}) collective-permute-start(bf16[576,1024]{1,0:T(8,128)(2,1)} %get-tuple-element.57), channel_id=1, source_target_pairs={{0,2},{1,3},{2,4},{3,5},{4,6},{5,7},{6,0},{7,1},{8,10},{9,11},{10,... | collective-permute-start | bytes 3538952 | tf_op jit(solution)/shard_map/ppermute | solution.py:374
  33.7 11.6 %collective-permute-start.5 = (bf16[360,512]{1,0:T(8,128)(2,1)}, bf16[360,512]{1,0:T(8,128)(2,1)S(1)}, u32[]{:S(2)}, u32[]{:S(2)}) collective-permute-start(bf16[360,512]{1,0:T(8,128)(2,1)} %get-tuple-element.59.refs_6_), channel_id=1, source_target_pairs={{0,16},{8,24},{16,0},{24,8},{1,17},{9,25},{17,1},{25,9},{2,18},{10... | collective-permute-start | bytes 1105928 | tf_op jit(solution)/shard_map/ppermute | solution.py:367
  34.2 12.6 %collective-permute-start.4 = (bf16[360,512]{1,0:T(8,128)(2,1)}, bf16[360,512]{1,0:T(8,128)(2,1)S(1)}, u32[]{:S(2)}, u32[]{:S(2)}) collective-permute-start(bf16[360,512]{1,0:T(8,128)(2,1)} %get-tuple-element.59.refs_6_), channel_id=1, source_target_pairs={{0,8},{8,0},{16,24},{24,16},{1,9},{9,1},{17,25},{25,17},{2,10},{10... | collective-permute-start | bytes 1105928 | tf_op jit(solution)/shard_map/ppermute | solution.py:367
  40.9 12.4 %collective-permute-start.8 = (bf16[360,512]{1,0:T(8,128)(2,1)}, bf16[360,512]{1,0:T(8,128)(2,1)}, u32[]{:S(2)}, u32[]{:S(2)}) collective-permute-start(bf16[360,512]{1,0:T(8,128)(2,1)} %get-tuple-element.69.refs_6_), channel_id=1, source_target_pairs={{0,16},{8,24},{16,0},{24,8},{1,17},{9,25},{17,1},{25,9},{2,18},{10... | collective-permute-start | bytes 1105928 | tf_op jit(solution)/shard_map/ppermute | solution.py:367
  45.3 9.5 %copy-start.4 = (bf16[360,512]{1,0:T(8,128)(2,1)}, bf16[360,512]{1,0:T(8,128)(2,1)S(1)}, u32[]{:S(2)}) copy-start(bf16[360,512]{1,0:T(8,128)(2,1)S(1)} %collective-permute-done.5.refs_9_.refs_8_) | copy-start | bytes 1105924
  45.3 25.2 %collective-permute-start.16 = (bf16[360,512]{1,0:T(8,128)(2,1)}, bf16[360,512]{1,0:T(8,128)(2,1)}, u32[]{:S(2)}, u32[]{:S(2)}) collective-permute-start(bf16[360,512]{1,0:T(8,128)(2,1)} %get-tuple-element.69.refs_6_), channel_id=1, source_target_pairs={{0,8},{8,0},{16,24},{24,16},{1,9},{9,1},{17,25},{25,17},{2,10},{10... | collective-permute-start | bytes 1105928 | tf_op jit(solution)/shard_map/ppermute | solution.py:367
  46.8 14.6 %copy-start.6 = (bf16[360,512]{1,0:T(8,128)(2,1)}, bf16[360,512]{1,0:T(8,128)(2,1)S(1)}, u32[]{:S(2)}) copy-start(bf16[360,512]{1,0:T(8,128)(2,1)S(1)} %collective-permute-done.4.refs_7_) | copy-start | bytes 1105924
  46.8 15.2 %collective-permute-start.6 = (bf16[360,512]{1,0:T(8,128)(2,1)S(1)}, bf16[360,512]{1,0:T(8,128)(2,1)}, u32[]{:S(2)}, u32[]{:S(2)}) collective-permute-start(bf16[360,512]{1,0:T(8,128)(2,1)S(1)} %collective-permute-done.4.refs_7_), channel_id=1, source_target_pairs={{0,16},{8,24},{16,0},{24,8},{1,17},{9,25},{17,1},{25,9},{2,18},{10... | collective-permute-start | bytes 1105928 | tf_op jit(solution)/shard_map/ppermute | solution.py:367
  53.3 18.2 %collective-permute-start.17 = (bf16[360,512]{1,0:T(8,128)(2,1)}, bf16[360,512]{1,0:T(8,128)(2,1)}, u32[]{:S(2)}, u32[]{:S(2)}) collective-permute-start(bf16[360,512]{1,0:T(8,128)(2,1)} %collective-permute-done.8.refs_13_.refs_8_), channel_id=1, source_target_pairs={{0,8},{8,0},{16,24},{24,16},{1,9},{9,1},{17,25},{25,17},{2,10},{10... | collective-permute-start | bytes 1105928 | tf_op jit(solution)/shard_map/ppermute | solution.py:367
  61.4 19.8 %collective-permute-start.13 = (bf16[360,1024]{1,0:T(8,128)(2,1)}, bf16[360,1024]{1,0:T(8,128)(2,1)}, u32[]{:S(2)}, u32[]{:S(2)}) collective-permute-start(bf16[360,1024]{1,0:T(8,128)(2,1)} %get-tuple-element.71.refs_6_), channel_id=1, source_target_pairs={{0,16},{8,24},{16,0},{24,8},{1,17},{9,25},{17,1},{25,9},{2,18},{10... | collective-permute-start | bytes 2211848 | tf_op jit(solution)/shard_map/ppermute | solution.py:367
  62.0 19.8 %collective-permute-start.12 = (bf16[360,1024]{1,0:T(8,128)(2,1)}, bf16[360,1024]{1,0:T(8,128)(2,1)}, u32[]{:S(2)}, u32[]{:S(2)}) collective-permute-start(bf16[360,1024]{1,0:T(8,128)(2,1)} %get-tuple-element.71.refs_6_), channel_id=1, source_target_pairs={{0,8},{8,0},{16,24},{24,16},{1,9},{9,1},{17,25},{25,17},{2,10},{10... | collective-permute-start | bytes 2211848 | tf_op jit(solution)/shard_map/ppermute | solution.py:367
  63.1 34.4 %collective-permute-start.15 = (bf16[576,1024]{1,0:T(8,128)(2,1)}, bf16[576,1024]{1,0:T(8,128)(2,1)}, u32[]{:S(2)}, u32[]{:S(2)}) collective-permute-start(bf16[576,1024]{1,0:T(8,128)(2,1)} %collective-permute-done.3.refs_0_), channel_id=1, source_target_pairs={{0,1},{1,0},{2,3},{3,2},{4,5},{5,4},{6,7},{7,6},{8,9},{9,8},{10,11... | collective-permute-start | bytes 3538952 | tf_op jit(solution)/shard_map/ppermute | solution.py:370
  70.5 26.4 %collective-permute-start.18 = (bf16[360,1024]{1,0:T(8,128)(2,1)}, bf16[360,1024]{1,0:T(8,128)(2,1)S(1)}, u32[]{:S(2)}, u32[]{:S(2)}) collective-permute-start(bf16[360,1024]{1,0:T(8,128)(2,1)} %get-tuple-element.70.rest_0_.refs_6_), channel_id=1, source_target_pairs={{0,16},{8,24},{16,0},{24,8},{1,17},{9,25},{17,1},{25,9},{2,18},{10... | collective-permute-start | bytes 2211848 | tf_op jit(solution)/shard_map/ppermute | solution.py:367
  71.5 33.7 %collective-permute-start.9 = (bf16[576,1024]{1,0:T(8,128)(2,1)}, bf16[576,1024]{1,0:T(8,128)(2,1)}, u32[]{:S(2)}, u32[]{:S(2)}) collective-permute-start(bf16[576,1024]{1,0:T(8,128)(2,1)} %collective-permute-done.3.refs_0_), channel_id=1, source_target_pairs={{0,2},{1,3},{2,4},{3,5},{4,6},{5,7},{6,0},{7,1},{8,10},{9,11},{10,... | collective-permute-start | bytes 3538952 | tf_op jit(solution)/shard_map/ppermute | solution.py:374
  81.2 39.7 %collective-permute-start.26 = (bf16[360,1024]{1,0:T(8,128)(2,1)}, bf16[360,1024]{1,0:T(8,128)(2,1)}, u32[]{:S(2)}, u32[]{:S(2)}) collective-permute-start(bf16[360,1024]{1,0:T(8,128)(2,1)} %get-tuple-element.70.rest_0_.refs_6_), channel_id=1, source_target_pairs={{0,8},{8,0},{16,24},{24,16},{1,9},{9,1},{17,25},{25,17},{2,10},{10... | collective-permute-start | bytes 2211848 | tf_op jit(solution)/shard_map/ppermute | solution.py:367
  81.8 31.1 %collective-permute-start.14 = (bf16[360,1024]{1,0:T(8,128)(2,1)}, bf16[360,1024]{1,0:T(8,128)(2,1)}, u32[]{:S(2)}, u32[]{:S(2)}) collective-permute-start(bf16[360,1024]{1,0:T(8,128)(2,1)} %collective-permute-done.12.refs_7_), channel_id=1, source_target_pairs={{0,16},{8,24},{16,0},{24,8},{1,17},{9,25},{17,1},{25,9},{2,18},{10... | collective-permute-start | bytes 2211848 | tf_op jit(solution)/shard_map/ppermute | solution.py:367
  96.9 8.0 %copy-start = (bf16[360,1024]{1,0:T(8,128)(2,1)}, bf16[360,1024]{1,0:T(8,128)(2,1)S(1)}, u32[]{:S(2)}) copy-start(bf16[360,1024]{1,0:T(8,128)(2,1)S(1)} %collective-permute-done.18.refs_14_.refs_8_) | copy-start | bytes 2211844
  96.9 24.6 %collective-permute-start.27 = (bf16[360,1024]{1,0:T(8,128)(2,1)S(1)}, bf16[360,1024]{1,0:T(8,128)(2,1)}, u32[]{:S(2)}, u32[]{:S(2)}) collective-permute-start(bf16[360,1024]{1,0:T(8,128)(2,1)S(1)} %collective-permute-done.18.refs_14_.refs_8_), channel_id=1, source_target_pairs={{0,8},{8,0},{16,24},{24,16},{1,9},{9,1},{17,25},{25,17},{2,10},{10... | collective-permute-start | bytes 2211848 | tf_op jit(solution)/shard_map/ppermute | solution.py:367
  104.9 23.7 %collective-permute-start.23 = (bf16[360,1024]{1,0:T(8,128)(2,1)}, bf16[360,1024]{1,0:T(8,128)(2,1)}, u32[]{:S(2)}, u32[]{:S(2)}) collective-permute-start(bf16[360,1024]{1,0:T(8,128)(2,1)} %get-tuple-element.81.refs_6_), channel_id=1, source_target_pairs={{0,16},{8,24},{16,0},{24,8},{1,17},{9,25},{17,1},{25,9},{2,18},{10... | collective-permute-start | bytes 2211848 | tf_op jit(solution)/shard_map/ppermute | solution.py:367
  105.2 48.3 %collective-permute-start.25 = (bf16[576,1024]{1,0:T(8,128)(2,1)}, bf16[576,1024]{1,0:T(8,128)(2,1)}, u32[]{:S(2)}, u32[]{:S(2)}) collective-permute-start(bf16[576,1024]{1,0:T(8,128)(2,1)} %collective-permute-done.9.refs_0_), channel_id=1, source_target_pairs={{0,1},{1,0},{2,3},{3,2},{4,5},{5,4},{6,7},{7,6},{8,9},{9,8},{10,11... | collective-permute-start | bytes 3538952 | tf_op jit(solution)/shard_map/ppermute | solution.py:370
  112.8 40.7 %collective-permute-start.10 = (bf16[576,1024]{1,0:T(8,128)(2,1)}, bf16[576,1024]{1,0:T(8,128)(2,1)}, u32[]{:S(2)}, u32[]{:S(2)}) collective-permute-start(bf16[576,1024]{1,0:T(8,128)(2,1)} %collective-permute-done.9.refs_0_), channel_id=1, source_target_pairs={{0,2},{1,3},{2,4},{3,5},{4,6},{5,7},{6,0},{7,1},{8,10},{9,11},{10,... | collective-permute-start | bytes 3538952 | tf_op jit(solution)/shard_map/ppermute | solution.py:374
  121.0 16.8 %collective-permute-start.22 = (bf16[360,1024]{1,0:T(8,128)(2,1)}, bf16[360,1024]{1,0:T(8,128)(2,1)}, u32[]{:S(2)}, u32[]{:S(2)}) collective-permute-start(bf16[360,1024]{1,0:T(8,128)(2,1)} %get-tuple-element.81.refs_6_), channel_id=1, source_target_pairs={{0,8},{8,0},{16,24},{24,16},{1,9},{9,1},{17,25},{25,17},{2,10},{10... | collective-permute-start | bytes 2211848 | tf_op jit(solution)/shard_map/ppermute | solution.py:367
  121.6 22.8 %collective-permute-start.20 = (bf16[360,1024]{1,0:T(8,128)(2,1)}, bf16[360,1024]{1,0:T(8,128)(2,1)S(1)}, u32[]{:S(2)}, u32[]{:S(2)}) collective-permute-start(bf16[360,1024]{1,0:T(8,128)(2,1)} %get-tuple-element.80.refs_6_), channel_id=1, source_target_pairs={{0,16},{8,24},{16,0},{24,8},{1,17},{9,25},{17,1},{25,9},{2,18},{10... | collective-permute-start | bytes 2211848 | tf_op jit(solution)/shard_map/ppermute | solution.py:367
  122.1 86.9 %all-to-all-start = ((bf16[8,144,1024]{2,1,0:T(8,128)(2,1)}), bf16[8,144,1024]{2,1,0:T(8,128)(2,1)}, u32[]{:S(2)}, u32[]{:S(2)}) async-start(bf16[8,144,1024]{2,1,0:T(8,128)(2,1)} %input_product.3.refs_14_), calls=%async_computation | async-start | bytes 4718592 | tf_op jit(solution)/shard_map/all_to_all | solution.py:451
  128.6 41.0 %collective-permute-start.19 = (bf16[360,1024]{1,0:T(8,128)(2,1)}, bf16[360,1024]{1,0:T(8,128)(2,1)}, u32[]{:S(2)}, u32[]{:S(2)}) collective-permute-start(bf16[360,1024]{1,0:T(8,128)(2,1)} %get-tuple-element.80.refs_6_), channel_id=1, source_target_pairs={{0,8},{8,0},{16,24},{24,16},{1,9},{9,1},{17,25},{25,17},{2,10},{10... | collective-permute-start | bytes 2211848 | tf_op jit(solution)/shard_map/ppermute | solution.py:367
  137.7 23.9 %collective-permute-start.24 = (bf16[360,1024]{1,0:T(8,128)(2,1)}, bf16[360,1024]{1,0:T(8,128)(2,1)}, u32[]{:S(2)}, u32[]{:S(2)}) collective-permute-start(bf16[360,1024]{1,0:T(8,128)(2,1)} %collective-permute-done.22.refs_7_), channel_id=1, source_target_pairs={{0,16},{8,24},{16,0},{24,8},{1,17},{9,25},{17,1},{25,9},{2,18},{10... | collective-permute-start | bytes 2211848 | tf_op jit(solution)/shard_map/ppermute | solution.py:367
  144.3 17.2 %copy-start.1 = (bf16[360,1024]{1,0:T(8,128)(2,1)}, bf16[360,1024]{1,0:T(8,128)(2,1)S(1)}, u32[]{:S(2)}) copy-start(bf16[360,1024]{1,0:T(8,128)(2,1)S(1)} %collective-permute-done.20.refs_14_.refs_8_) | copy-start | bytes 2211844
  144.3 27.3 %collective-permute-start.21 = (bf16[360,1024]{1,0:T(8,128)(2,1)S(1)}, bf16[360,1024]{1,0:T(8,128)(2,1)}, u32[]{:S(2)}, u32[]{:S(2)}) collective-permute-start(bf16[360,1024]{1,0:T(8,128)(2,1)S(1)} %collective-permute-done.20.refs_14_.refs_8_), channel_id=1, source_target_pairs={{0,8},{8,0},{16,24},{24,16},{1,9},{9,1},{17,25},{25,17},{2,10},{10... | collective-permute-start | bytes 2211848 | tf_op jit(solution)/shard_map/ppermute | solution.py:367
  153.6 27.6 %collective-permute-start.11 = (bf16[576,1024]{1,0:T(8,128)(2,1)}, bf16[576,1024]{1,0:T(8,128)(2,1)}, u32[]{:S(2)}, u32[]{:S(2)}) collective-permute-start(bf16[576,1024]{1,0:T(8,128)(2,1)} %collective-permute-done.10.refs_0_), channel_id=1, source_target_pairs={{0,1},{1,0},{2,3},{3,2},{4,5},{5,4},{6,7},{7,6},{8,9},{9,8},{10,11... | collective-permute-start | bytes 3538952 | tf_op jit(solution)/shard_map/ppermute | solution.py:370
  161.5 19.7 %collective-permute-start.28 = (bf16[360,1024]{1,0:T(8,128)(2,1)}, bf16[360,1024]{1,0:T(8,128)(2,1)}, u32[]{:S(2)}, u32[]{:S(2)}) collective-permute-start(bf16[360,1024]{1,0:T(8,128)(2,1)} %get-tuple-element.94.refs_0_), channel_id=1, source_target_pairs={{0,16},{8,24},{16,0},{24,8},{1,17},{9,25},{17,1},{25,9},{2,18},{10... | collective-permute-start | bytes 2211848 | tf_op jit(solution)/shard_map/ppermute | solution.py:367
  161.6 27.7 %collective-permute-start.35 = (bf16[360,1024]{1,0:T(8,128)(2,1)}, bf16[360,1024]{1,0:T(8,128)(2,1)}, u32[]{:S(2)}, u32[]{:S(2)}) collective-permute-start(bf16[360,1024]{1,0:T(8,128)(2,1)} %get-tuple-element.94.refs_0_), channel_id=1, source_target_pairs={{0,8},{8,0},{16,24},{24,16},{1,9},{9,1},{17,25},{25,17},{2,10},{10... | collective-permute-start | bytes 2211848 | tf_op jit(solution)/shard_map/ppermute | solution.py:367
  169.6 27.4 %collective-permute-start.32 = (bf16[360,1024]{1,0:T(8,128)(2,1)}, bf16[360,1024]{1,0:T(8,128)(2,1)}, u32[]{:S(2)}, u32[]{:S(2)}) collective-permute-start(bf16[360,1024]{1,0:T(8,128)(2,1)} %get-tuple-element.99.refs_0_), channel_id=1, source_target_pairs={{0,16},{8,24},{16,0},{24,8},{1,17},{9,25},{17,1},{25,9},{2,18},{10... | collective-permute-start | bytes 2211848 | tf_op jit(solution)/shard_map/ppermute | solution.py:367
  181.2 8.3 %copy-start.5 = (bf16[360,1024]{1,0:T(8,128)(2,1)S(1)}, bf16[360,1024]{1,0:T(8,128)(2,1)}, u32[]{:S(2)}) copy-start(bf16[360,1024]{1,0:T(8,128)(2,1)} %get-tuple-element.99.refs_0_) | copy-start | bytes 2211844
  189.2 19.8 %collective-permute-start.29 = (bf16[360,1024]{1,0:T(8,128)(2,1)}, bf16[360,1024]{1,0:T(8,128)(2,1)}, u32[]{:S(2)}, u32[]{:S(2)}) collective-permute-start(bf16[360,1024]{1,0:T(8,128)(2,1)} %get-tuple-element.98.refs_4_), channel_id=1, source_target_pairs={{0,8},{8,0},{16,24},{24,16},{1,9},{9,1},{17,25},{25,17},{2,10},{10... | collective-permute-start | bytes 2211848 | tf_op jit(solution)/shard_map/ppermute | solution.py:367
  189.3 23.5 %collective-permute-start.36 = (bf16[360,1024]{1,0:T(8,128)(2,1)}, bf16[360,1024]{1,0:T(8,128)(2,1)}, u32[]{:S(2)}, u32[]{:S(2)}) collective-permute-start(bf16[360,1024]{1,0:T(8,128)(2,1)} %collective-permute-done.35.refs_1_), channel_id=1, source_target_pairs={{0,16},{8,24},{16,0},{24,8},{1,17},{9,25},{17,1},{25,9},{2,18},{10... | collective-permute-start | bytes 2211848 | tf_op jit(solution)/shard_map/ppermute | solution.py:367
  189.4 35.4 %collective-permute-start.31 = (bf16[360,1024]{1,0:T(8,128)(2,1)S(1)}, bf16[360,1024]{1,0:T(8,128)(2,1)}, u32[]{:S(2)}, u32[]{:S(2)}) collective-permute-start(bf16[360,1024]{1,0:T(8,128)(2,1)S(1)} %copy-done.5), channel_id=1, source_target_pairs={{0,8},{8,0},{16,24},{24,16},{1,9},{9,1},{17,25},{25,17},{2,10},{10... | collective-permute-start | bytes 2211848 | tf_op jit(solution)/shard_map/ppermute | solution.py:367
  196.9 42.0 %collective-permute-start.33 = (bf16[360,1024]{1,0:T(8,128)(2,1)}, bf16[360,1024]{1,0:T(8,128)(2,1)}, u32[]{:S(2)}, u32[]{:S(2)}) collective-permute-start(bf16[360,1024]{1,0:T(8,128)(2,1)} %collective-permute-done.32.refs_2_), channel_id=1, source_target_pairs={{0,8},{8,0},{16,24},{24,16},{1,9},{9,1},{17,25},{25,17},{2,10},{10... | collective-permute-start | bytes 2211848 | tf_op jit(solution)/shard_map/ppermute | solution.py:367
  197.0 42.0 %collective-permute-start.34 = (bf16[360,1024]{1,0:T(8,128)(2,1)}, bf16[360,1024]{1,0:T(8,128)(2,1)}, u32[]{:S(2)}, u32[]{:S(2)}) collective-permute-start(bf16[360,1024]{1,0:T(8,128)(2,1)} %get-tuple-element.98.refs_4_), channel_id=1, source_target_pairs={{0,16},{8,24},{16,0},{24,8},{1,17},{9,25},{17,1},{25,9},{2,18},{10... | collective-permute-start | bytes 2211848 | tf_op jit(solution)/shard_map/ppermute | solution.py:367
  209.0 35.0 %collective-permute-start.30 = (bf16[360,1024]{1,0:T(8,128)(2,1)}, bf16[360,1024]{1,0:T(8,128)(2,1)}, u32[]{:S(2)}, u32[]{:S(2)}) collective-permute-start(bf16[360,1024]{1,0:T(8,128)(2,1)} %collective-permute-done.29.refs_5_), channel_id=1, source_target_pairs={{0,16},{8,24},{16,0},{24,8},{1,17},{9,25},{17,1},{25,9},{2,18},{10... | collective-permute-start | bytes 2211848 | tf_op jit(solution)/shard_map/ppermute | solution.py:367
